TPU v7x, 128 devices: a whole 4x4x4 slice. The times are simulated.
128 devices in a mesh: cp: 32 (over z, y_hi, x), tp: 4 (over y_lo, core).
Axes of the slice: x: 4, y: 4 (y_hi: 2, y_lo: 2; y = y_hi * 2 + y_lo), z: 4, core: 2. Of those that a mesh axis runs over, the one named last changes fastest.
Arguments:
- queries: bfloat16 [256, 128, 128], P('cp', 'tp'), may hold values from -32 to 32
- keys: bfloat16 [65536, 8, 128], P('cp', 'tp'), may hold values from -24 to 24
- values: bfloat16 [65536, 8, 128], P('cp', 'tp'), may hold values from -12 to 12
- lengths: int32 [32], P('cp'), may hold values from 1024 to 2048
- start: int32 [1], replicated, may hold values from 32512 to 65280
- out_weight: bfloat16 [16384, 16384], P('tp', 'cp'), may hold values from -0.046875 to 0.046875
Outputs:
- projected: bfloat16 [256, 16384], P('tp', 'cp')
All inputs are finite; a program needn't handle non-finite values.
Results may differ from a plain program's by a relative error of at most 0.0065.
Values may be sent and summed in bfloat16 or wider, within the bound.
No kernel may reach another device: no remote copies, remote signals or barrier semaphores. Data moves between devices by JAX's collectives and lax.ppermute only.
A program may use at most 64 MiB of HBM per device.

v0:
```python
import functools
import itertools
import math

import jax
import jax.numpy as jnp
from jax import lax
from jax.experimental import pallas as pl
from jax.experimental.pallas import tpu as pltpu
from jax.sharding import PartitionSpec as P

NEG = -1e30
BIG = 2.0**100
RING = 4
MIB = 2**20


def coords(cp, tp):
    z, yh, x = cp // 8, (cp // 4) % 2, cp % 4
    yl, core = tp // 2, tp % 2
    return z, yh, x, yl, core


def moved(x, a=0, b=0, yh=0, yl=0, core=0):
    pairs = []
    for cp, tp in itertools.product(range(32), range(4)):
        zi, yhi, xi, yli, ci = coords(cp, tp)
        dz, dx = (a, b) if ci == 0 else (b, a)
        zo, xo = (zi + dz) % RING, (xi + dx) % RING
        yho, ylo, co = yhi ^ yh, yli ^ yl, ci ^ core
        pairs.append((cp * 4 + tp, ((zo * 2 + yho) * 4 + xo) * 4 + ylo * 2 + co))
    return lax.ppermute(x, ("cp", "tp"), pairs)


def after(x, *earlier):
    return lax.optimization_barrier((x, *earlier))[0]


def source(me, da, db, dy):
    z, yh, x, _, core = me
    dz = jnp.where(core == 0, da, db)
    dx = jnp.where(core == 0, db, da)
    return (z - dz) & (RING - 1), yh ^ dy, (x - dx) & (RING - 1)


def spread(row, eye):
    return jnp.sum(jnp.where(eye, row, 0.0), axis=1, keepdims=True)


def gathered_row(column, eye):
    return jnp.sum(jnp.where(eye, column, 0.0), axis=0, keepdims=True)


def diagonal():
    shape = (128, 128)
    return lax.broadcasted_iota(jnp.int32, shape, 0) == lax.broadcasted_iota(jnp.int32, shape, 1)


def stat_rows(m, l):
    high = l.astype(jnp.bfloat16).astype(jnp.float32)
    return jnp.concatenate([m, high, l - high, jnp.zeros((13, 128), jnp.float32)], axis=0).astype(jnp.bfloat16)


def attend_kernel(me_ref, len_ref, start_ref, q_ref, k_ref, v_ref, o_ref, vx, kx, *, db, kvs, nb, span, tile, scale):
    step = pl.program_id(0)
    rows = nb * 128

    @pl.when(step == 0)
    def _():
        me = tuple(me_ref[i] for i in range(5))
        shard = (me[0] * 2 + me[1]) * 4 + me[2]
        lane = lax.broadcasted_iota(jnp.int32, (1, 128), 1)
        z, yh, x = source(me, lane >> 4, db, (lane >> 3) & 1)
        seen = start_ref[0] + z * 64 + yh * 32 + x * 8 + (lane & 7) + 1 - shard * span
        seen = jnp.minimum(seen, len_ref[0])
        slot = lax.broadcasted_iota(jnp.int32, (span, 128), 0)
        mask = jnp.where((slot >= seen) & (lane < 64), NEG, 0.0).astype(jnp.bfloat16)
        for i, kv in enumerate(kvs):
            kx[i, :, :128] = k_ref[kv]
            kx[i, :, 128:] = mask
            vx[i, :, :128] = v_ref[kv]
            vx[i, :, 128:] = jnp.ones((span, 128), jnp.bfloat16)

    eye = diagonal()
    row = lax.broadcasted_iota(jnp.int32, (rows, 128), 0)
    lane = lax.broadcasted_iota(jnp.int32, (rows, 128), 1)
    hot = jnp.where(lane == (step * nb + (row >> 7)) * 8 + (row & 7), 1.0, 0.0).astype(jnp.bfloat16)

    def scores(i, t):
        q = jnp.concatenate([q_ref[:, kvs[i]].reshape(rows, 128), hot], axis=1)
        return lax.dot_general(
            q, kx[i, pl.ds(t, tile), :], (((1,), (1,)), ((), ())), preferred_element_type=jnp.float32
        )

    def point(m):
        return jnp.maximum(m * scale, 0.01 * NEG).astype(jnp.bfloat16).astype(jnp.float32)

    def put(i, m, acc):
        for b in range(nb):
            r = slice(b * 128, (b + 1) * 128)
            o_ref[b, i, :128, :] = acc[r, :128].astype(jnp.bfloat16)
            o_ref[b, i, 128:, :] = stat_rows(gathered_row(m[r], eye), gathered_row(acc[r, 128:], eye))

    ok = []
    for i in range(len(kvs)):
        first = scores(i, 0)
        m = point(jnp.max(first, axis=1, keepdims=True))
        p = []
        for t in range(0, span, tile):
            s = first if t == 0 else scores(i, t)
            p.append(jnp.exp2(s * scale - m).astype(jnp.bfloat16))
        acc = jnp.dot(jnp.concatenate(p, axis=1), vx[i], preferred_element_type=jnp.float32)
        ok.append(jnp.min(jnp.where(acc[:, 128:] < BIG, 1.0, 0.0)))
        put(i, m, acc)

    @pl.when(functools.reduce(jnp.minimum, ok) < 0.5)
    def _():
        for i in range(len(kvs)):

            def top(n, m):
                s = scores(i, pl.multiple_of(n * tile, tile))
                return jnp.maximum(m, jnp.max(s, axis=1, keepdims=True))

            m = point(lax.fori_loop(0, span // tile, top, jnp.full((rows, 1), NEG, jnp.float32)))

            def add(n, acc):
                t = pl.multiple_of(n * tile, tile)
                p = jnp.exp2(scores(i, t) * scale - m).astype(jnp.bfloat16)
                return acc + jnp.dot(p, vx[i, pl.ds(t, tile), :], preferred_element_type=jnp.float32)

            put(i, m, lax.fori_loop(0, span // tile, add, jnp.zeros((rows, 256), jnp.float32)))


def attend(me, lengths, start, q, k, v, db, kvs):
    blocks = q.shape[0]
    span = v.shape[1]
    nb, tile = 8 // len(kvs), 256
    smem, vmem = pl.BlockSpec(memory_space=pltpu.SMEM), pl.BlockSpec(memory_space=pltpu.VMEM)
    return pl.pallas_call(
        functools.partial(
            attend_kernel, db=db, kvs=kvs, nb=nb, span=span, tile=tile, scale=math.log2(math.e) / math.sqrt(128)
        ),
        grid=(blocks // nb,),
        in_specs=[smem, smem, smem, pl.BlockSpec((nb, *q.shape[1:]), lambda i: (i, 0, 0, 0)), vmem, vmem],
        out_specs=pl.BlockSpec((nb, len(kvs), 144, 128), lambda i: (i, 0, 0, 0)),
        out_shape=jax.ShapeDtypeStruct((blocks, len(kvs), 144, 128), jnp.bfloat16),
        scratch_shapes=[pltpu.VMEM((len(kvs), span, 256), jnp.bfloat16)] * 2,
        compiler_params=pltpu.CompilerParams(vmem_limit_bytes=28 * MIB, dimension_semantics=("arbitrary",)),
        cost_estimate=pl.CostEstimate(
            flops=8 * blocks * len(kvs) * 128 * span * 128,
            bytes_accessed=4 * MIB,
            transcendentals=blocks * len(kvs) * 128 * span,
        ),
        name="attend_plane",
    )(me, lengths, start, q, k, v)


def merged(parts, eye):
    stats = [p[128:, :].astype(jnp.float32) for p in parts]
    m = functools.reduce(jnp.maximum, [s[0:1] for s in stats])
    total = jnp.zeros((1, 128), jnp.float32)
    out = jnp.zeros((128, 128), jnp.float32)
    for p, s in zip(parts, stats):
        factor = jnp.exp2(s[0:1] - m)
        total = total + factor * (s[1:2] + s[2:3])
        out = out + spread(factor, eye) * p[:128, :].astype(jnp.float32)
    return out, m, total


def combine_kernel(*refs):
    parts, o_ref = refs[:-1], refs[-1]
    eye = diagonal()
    for b, kv in itertools.product(range(o_ref.shape[0]), range(o_ref.shape[1])):
        out, m, total = merged([p[b, kv] for p in parts], eye)
        o_ref[b, kv, :128, :] = out.astype(jnp.bfloat16)
        o_ref[b, kv, 128:, :] = stat_rows(m, total)


def combine(parts):
    return pl.pallas_call(
        combine_kernel,
        out_shape=jax.ShapeDtypeStruct(parts[0].shape, jnp.bfloat16),
        compiler_params=pltpu.CompilerParams(vmem_limit_bytes=16 * MIB),
        name="combine",
    )(*parts)


def finish_kernel(mine, theirs, o_ref):
    eye = diagonal()
    for kv in range(mine.shape[1]):
        attn = []
        for dy in range(2):
            out, _, total = merged([mine[dy, kv], theirs[1 - dy, kv]], eye)
            attn.append((out * spread(1.0 / total, eye)).astype(jnp.bfloat16))
        for h in range(16):
            c = (kv * 16 + h) * 128
            o_ref[:, c : c + 128] = jnp.concatenate([a[h * 8 : (h + 1) * 8, :] for a in attn], axis=0)


def finish(mine, theirs):
    return pl.pallas_call(
        finish_kernel,
        out_shape=jax.ShapeDtypeStruct((16, mine.shape[1] * 2048), jnp.bfloat16),
        name="finish",
    )(mine, theirs)


def project_kernel(me_ref, x0, x1, x2, x3, w_ref, o_ref, acc):
    step = pl.program_id(0)
    x = jnp.concatenate([r[...] for r in (x0, x1, x2, x3)], axis=0)
    y = jnp.dot(x, w_ref[...], preferred_element_type=jnp.float32)

    @pl.when(step == 0)
    def _():
        acc[...] = y

    @pl.when(step > 0)
    def _():
        acc[...] += y

    @pl.when(step == pl.num_programs(0) - 1)
    def _():
        me = tuple(me_ref[i] for i in range(5))
        yl, core = me[3], me[4]
        for db, da, dy in itertools.product(range(RING), range(RING), range(2)):
            z, yh, xx = source(me, da, db, dy)
            row = (((z & 1) ^ core) * 2 + ((z >> 1) ^ yl)) * 64 + yh * 32 + xx * 8
            at = (db * RING + da) * 16 + dy * 8
            o_ref[pl.ds(pl.multiple_of(row, 8), 8), :] = acc[at : at + 8, :]


def project(me, planes, w):
    rows = sum(p.shape[0] for p in planes)
    steps = 4
    depth = w.shape[0] // steps
    return pl.pallas_call(
        project_kernel,
        grid=(steps,),
        in_specs=[pl.BlockSpec(memory_space=pltpu.SMEM)]
        + [pl.BlockSpec((p.shape[0], depth), lambda i: (0, i)) for p in planes]
        + [pl.BlockSpec((depth, w.shape[1]), lambda i: (i, 0))],
        out_specs=pl.BlockSpec((rows, w.shape[1]), lambda i: (0, 0)),
        out_shape=jax.ShapeDtypeStruct((rows, w.shape[1]), jnp.float32),
        scratch_shapes=[pltpu.VMEM((rows, w.shape[1]), jnp.float32)],
        compiler_params=pltpu.CompilerParams(vmem_limit_bytes=56 * MIB, dimension_semantics=("arbitrary",)),
        name="project",
    )(me, *planes, w)


def on_device(queries, keys, values, lengths, start, out_weight):
    nkv = keys.shape[1]
    me = jnp.stack(coords(lax.axis_index("cp"), lax.axis_index("tp"))).astype(jnp.int32)
    k = keys.transpose(1, 0, 2)
    v = values.transpose(1, 0, 2)
    q = queries.reshape(8, nkv, 16, 128).transpose(1, 2, 0, 3).reshape(1, nkv, 128, 128)
    q = jnp.concatenate([q, moved(q, yh=1)], axis=0)
    q = jnp.concatenate([q] + [moved(q, a=d) for d in (1, 2, 3)], axis=0)
    planes = {0: q}
    for d in (1, 3, 2):
        planes[d] = moved(q, b=d)

    kvs = tuple(range(nkv))
    parts = []
    for d in (0, 1, 3, 2):
        x = after(planes[d], parts[-1]) if parts else planes[d]
        parts.append(attend(me, lengths, start, x, k, v, d, kvs))
    c = combine([parts[0]] + [moved(p, b=-d) for p, d in zip(parts[1:], (1, 3, 2))])
    c = combine([c[:2]] + [moved(c[2 * d : 2 * d + 2], a=-d) for d in (1, 3, 2)])
    attn = finish(c, moved(c, yh=1))
    attn = jnp.concatenate([attn] + [moved(attn, a=d) for d in (1, 2, 3)], axis=0)
    rows = [attn] + [moved(attn, b=d) for d in (1, 2, 3)]
    y = project(me, rows, out_weight)
    y = y[:128] + moved(y[128:], core=1)
    y = y[:64] + moved(y[64:], yl=1)
    return y.astype(jnp.bfloat16)


def solution(mesh):
    in_specs = (
        P("cp", "tp", None),
        P("cp", "tp", None),
        P("cp", "tp", None),
        P("cp"),
        P(),
        P("tp", "cp"),
    )
    return jax.shard_map(on_device, mesh=mesh, in_specs=in_specs, out_specs=P("tp", "cp"), check_vma=False)
```

profile of v0, /device:TPU:0, one launch (start us, length us, event | category | flops | bytes accessed | tf_op | source)
XLA Modules:
  0.0 143.6 jit_solution(14238013123039050045)
XLA Ops:
  0.9 3.4 %collective-permute-start = (bf16[1,2,128,128]{3,2,1,0:T(8,128)(2,1)S(1)}, bf16[1,2,128,128]{3,2,1,0:T(8,128)(2,1)S(1)}, u32[]{:S(2)}, u32[]{:S(2)}) collective-permute-start(bf16[1,2,128,128]{3,2,1,0:T(8,128)(2,1)S(1)} %bitcast.19), channel_id=1, source_target_pairs={{0,16},{1,17},{2,18},{3,19},{4,20},{5,21},{6,22},{7,23},{8,24},{9,... | collective-permute-start | bytes 196616 | tf_op jit(solution)/shard_map/ppermute | solution.py:32
  4.2 2.5 %collective-permute-done = bf16[1,2,128,128]{3,2,1,0:T(8,128)(2,1)S(1)} collective-permute-done((bf16[1,2,128,128]{3,2,1,0:T(8,128)(2,1)S(1)}, bf16[1,2,128,128]{3,2,1,0:T(8,128)(2,1)S(1)}, u32[]{:S(2)}, u32[]{:S(2)}) %collective-permute-start) | collective-permute-done | bytes 65568 | tf_op jit(solution)/shard_map/ppermute | solution.py:32
  6.7 2.1 %collective-permute-start.1 = (bf16[2,2,128,128]{3,2,1,0:T(8,128)(2,1)S(1)}, bf16[2,2,128,128]{3,2,1,0:T(8,128)(2,1)S(1)}, u32[]{:S(2)}, u32[]{:S(2)}) collective-permute-start(bf16[2,2,128,128]{3,2,1,0:T(8,128)(2,1)S(1)} %pad_maximum_fusion.1), channel_id=1, source_target_pairs={{0,32},{1,5},{2,34},{3,7},{4,36},{5,9},{6,38},{7,11},{8,40},{9,13}... | collective-permute-start | bytes 393224 | tf_op jit(solution)/shard_map/ppermute | solution.py:32
  9.7 2.2 %collective-permute-start.3 = (bf16[2,2,128,128]{3,2,1,0:T(8,128)(2,1)S(1)}, bf16[2,2,128,128]{3,2,1,0:T(8,128)(2,1)S(1)}, u32[]{:S(2)}, u32[]{:S(2)}) collective-permute-start(bf16[2,2,128,128]{3,2,1,0:T(8,128)(2,1)S(1)} %pad_maximum_fusion.1), channel_id=1, source_target_pairs={{0,96},{1,13},{2,98},{3,15},{4,100},{5,1},{6,102},{7,3},{8,104},{9... | collective-permute-start | bytes 393224 | tf_op jit(solution)/shard_map/ppermute | solution.py:32
  11.9 1.9 %collective-permute-start.2 = (bf16[2,2,128,128]{3,2,1,0:T(8,128)(2,1)S(1)}, bf16[2,2,128,128]{3,2,1,0:T(8,128)(2,1)S(1)}, u32[]{:S(2)}, u32[]{:S(2)}) collective-permute-start(bf16[2,2,128,128]{3,2,1,0:T(8,128)(2,1)S(1)} %pad_maximum_fusion.1), channel_id=1, source_target_pairs={{0,64},{1,9},{2,66},{3,11},{4,68},{5,13},{6,70},{7,15},{8,72},{9,1... | collective-permute-start | bytes 393224 | tf_op jit(solution)/shard_map/ppermute | solution.py:32
  13.9 4.5 %collective-permute-done.2 = bf16[2,2,128,128]{3,2,1,0:T(8,128)(2,1)S(1)} collective-permute-done((bf16[2,2,128,128]{3,2,1,0:T(8,128)(2,1)S(1)}, bf16[2,2,128,128]{3,2,1,0:T(8,128)(2,1)S(1)}, u32[]{:S(2)}, u32[]{:S(2)}) %collective-permute-start.2) | collective-permute-done | bytes 131104 | tf_op jit(solution)/shard_map/ppermute | solution.py:32
  18.4 1.6 %collective-permute-start.4 = (bf16[8,2,128,128]{3,2,1,0:T(8,128)(2,1)S(1)}, bf16[8,2,128,128]{3,2,1,0:T(8,128)(2,1)S(1)}, u32[]{:S(2)}, u32[]{:S(2)}) collective-permute-start(bf16[8,2,128,128]{3,2,1,0:T(8,128)(2,1)S(1)} %constant_dynamic-update-slice_fusion.q_ref), channel_id=1, source_target_pairs={{0,4},{1,33},{2,6},{3,35},{4,8},{5,37},{6,10},{7,39},{8,12},{9,41}... | collective-permute-start | bytes 1572872 | tf_op jit(solution)/shard_map/ppermute | solution.py:32
  20.0 1.8 %copy_bitcast_fusion = (bf16[2,2048,128]{2,1,0:T(8,128)(2,1)S(1)}, bf16[2,2048,128]{2,1,0:T(8,128)(2,1)S(1)}) fusion(bf16[2048,2,128]{2,1,0:T(2,128)(2,1)} %param.8, bf16[2048,2,128]{2,1,0:T(2,128)(2,1)} %param.7), kind=kLoop, calls=%fused_computation | loop fusion | bytes 4194304 | tf_op jit(solution)/shard_map/transpose | solution.py:254
  23.2 2.8 %collective-permute-start.8 = (bf16[8,2,128,128]{3,2,1,0:T(8,128)(2,1)S(1)}, bf16[8,2,128,128]{3,2,1,0:T(8,128)(2,1)S(1)}, u32[]{:S(2)}, u32[]{:S(2)}) collective-permute-start(bf16[8,2,128,128]{3,2,1,0:T(8,128)(2,1)S(1)} %constant_dynamic-update-slice_fusion.q_ref), channel_id=1, source_target_pairs={{0,8},{1,65},{2,10},{3,67},{4,12},{5,69},{6,14},{7,71},{8,0},{9,73... | collective-permute-start | bytes 1572872 | tf_op jit(solution)/shard_map/ppermute | solution.py:32
  27.4 6.7 %attend_plane.4.refs_0_ = bf16[8,2,144,128]{3,2,1,0:T(8,128)(2,1)S(1)} custom-call(s32[5]{0:T(128)S(1)} %stack.23.me_ref, s32[1]{0:T(128)S(6)} %copy.20.len_ref, s32[1]{0:T(128)S(6)} %copy.21.start_ref, bf16[8,2,128,128]{3,2,1,0:T(8,128)(2,1)S(1)} %constant_dynamic-update-slice_fusion.q_ref, bf16[2,2048,128]{2,1,0:T(8,128)(2,1)S(1)} %get-tuple-element.16.k_ref, ...), custom_call_target="tpu_custom_call" | custom-call | flops 4294967296 | bytes 4194304 | tf_op jit(solution)/shard_map/attend_plane/pallas_call | solution.py:139
  34.2 6.8 %attend_plane.5 = bf16[8,2,144,128]{3,2,1,0:T(8,128)(2,1)S(1)} custom-call(s32[5]{0:T(128)S(1)} %stack.23.me_ref, s32[1]{0:T(128)S(6)} %copy.20.len_ref, s32[1]{0:T(128)S(6)} %copy.21.start_ref, bf16[8,2,128,128]{3,2,1,0:T(8,128)(2,1)S(1)} %collective-permute-done.4.q_ref, bf16[2,2048,128]{2,1,0:T(8,128)(2,1)S(1)} %get-tuple-element.16.k_ref, ...), custom_call_target="tpu_custom_call" | custom-call | flops 4294967296 | bytes 4194304 | tf_op jit(solution)/shard_map/attend_plane/pallas_call | solution.py:139
  40.9 7.0 %attend_plane.6 = bf16[8,2,144,128]{3,2,1,0:T(8,128)(2,1)S(1)} custom-call(s32[5]{0:T(128)S(1)} %stack.23.me_ref, s32[1]{0:T(128)S(6)} %copy.20.len_ref, s32[1]{0:T(128)S(6)} %copy.21.start_ref, bf16[8,2,128,128]{3,2,1,0:T(8,128)(2,1)S(1)} %collective-permute-done.6.q_ref, bf16[2,2048,128]{2,1,0:T(8,128)(2,1)S(1)} %get-tuple-element.16.k_ref, ...), custom_call_target="tpu_custom_call" | custom-call | flops 4294967296 | bytes 4194304 | tf_op jit(solution)/shard_map/attend_plane/pallas_call | solution.py:139
  47.9 6.8 %attend_plane.7 = bf16[8,2,144,128]{3,2,1,0:T(8,128)(2,1)S(1)} custom-call(s32[5]{0:T(128)S(1)} %stack.23.me_ref, s32[1]{0:T(128)S(6)} %copy.20.len_ref, s32[1]{0:T(128)S(6)} %copy.21.start_ref, bf16[8,2,128,128]{3,2,1,0:T(8,128)(2,1)S(1)} %collective-permute-done.8.q_ref, bf16[2,2048,128]{2,1,0:T(8,128)(2,1)S(1)} %get-tuple-element.16.k_ref, ...), custom_call_target="tpu_custom_call" | custom-call | flops 4294967296 | bytes 4194304 | tf_op jit(solution)/shard_map/attend_plane/pallas_call | solution.py:139
  55.8 2.8 %collective-permute-start.5 = (bf16[8,2,144,128]{3,2,1,0:T(8,128)(2,1)S(1)}, bf16[8,2,144,128]{3,2,1,0:T(8,128)(2,1)S(1)}, u32[]{:S(2)}, u32[]{:S(2)}) collective-permute-start(bf16[8,2,144,128]{3,2,1,0:T(8,128)(2,1)S(1)} %attend_plane.5), channel_id=1, source_target_pairs={{0,12},{1,97},{2,14},{3,99},{4,0},{5,101},{6,2},{7,103},{8,4},{9,1... | collective-permute-start | bytes 1769480 | tf_op jit(solution)/shard_map/ppermute | solution.py:32
  58.5 7.7 %collective-permute-done.9.refs_3_ = bf16[8,2,144,128]{3,2,1,0:T(8,128)(2,1)S(1)} collective-permute-done((bf16[8,2,144,128]{3,2,1,0:T(8,128)(2,1)S(1)}, bf16[8,2,144,128]{3,2,1,0:T(8,128)(2,1)S(1)}, u32[]{:S(2)}, u32[]{:S(2)}) %collective-permute-start.9) | collective-permute-done | bytes 589856 | tf_op jit(solution)/shard_map/ppermute | solution.py:32
  66.3 6.2 %collective-permute-done.7.refs_2_ = bf16[8,2,144,128]{3,2,1,0:T(8,128)(2,1)S(1)} collective-permute-done((bf16[8,2,144,128]{3,2,1,0:T(8,128)(2,1)S(1)}, bf16[8,2,144,128]{3,2,1,0:T(8,128)(2,1)S(1)}, u32[]{:S(2)}, u32[]{:S(2)}) %collective-permute-start.7) | collective-permute-done | bytes 589856 | tf_op jit(solution)/shard_map/ppermute | solution.py:32
  73.8 2.8 %collective-permute-start.12 = (bf16[2,2,144,128]{3,2,1,0:T(8,128)(2,1)S(1)}, bf16[2,2,144,128]{3,2,1,0:T(8,128)(2,1)S(1)}, u32[]{:S(2)}, u32[]{:S(2)}) collective-permute-start(bf16[2,2,144,128]{3,2,1,0:T(8,128)(2,1)S(1)} %get-tuple-element.11), channel_id=1, source_target_pairs={{0,64},{1,9},{2,66},{3,11},{4,68},{5,13},{6,70},{7,15},{8,72},{9,1... | collective-permute-start | bytes 442376 | tf_op jit(solution)/shard_map/ppermute | solution.py:32
  77.3 2.6 %collective-permute-start.10 = (bf16[2,2,144,128]{3,2,1,0:T(8,128)(2,1)S(1)}, bf16[2,2,144,128]{3,2,1,0:T(8,128)(2,1)S(1)}, u32[]{:S(2)}, u32[]{:S(2)}) collective-permute-start(bf16[2,2,144,128]{3,2,1,0:T(8,128)(2,1)S(1)} %get-tuple-element.13), channel_id=1, source_target_pairs={{0,96},{1,13},{2,98},{3,15},{4,100},{5,1},{6,102},{7,3},{8,104},{9... | collective-permute-start | bytes 442376 | tf_op jit(solution)/shard_map/ppermute | solution.py:32
  80.5 2.5 %collective-permute-done.11.refs_2_ = bf16[2,2,144,128]{3,2,1,0:T(8,128)(2,1)S(1)} collective-permute-done((bf16[2,2,144,128]{3,2,1,0:T(8,128)(2,1)S(1)}, bf16[2,2,144,128]{3,2,1,0:T(8,128)(2,1)S(1)}, u32[]{:S(2)}, u32[]{:S(2)}) %collective-permute-start.11) | collective-permute-done | bytes 147488 | tf_op jit(solution)/shard_map/ppermute | solution.py:32
  83.4 3.3 %collective-permute-start.13 = (bf16[2,2,144,128]{3,2,1,0:T(8,128)(2,1)S(1)}, bf16[2,2,144,128]{3,2,1,0:T(8,128)(2,1)S(1)}, u32[]{:S(2)}, u32[]{:S(2)}) collective-permute-start(bf16[2,2,144,128]{3,2,1,0:T(8,128)(2,1)S(1)} %combine.3.mine), channel_id=1, source_target_pairs={{0,16},{1,17},{2,18},{3,19},{4,20},{5,21},{6,22},{7,23},{8,24},{9,... | collective-permute-start | bytes 442376 | tf_op jit(solution)/shard_map/ppermute | solution.py:32
  86.7 3.4 %collective-permute-done.13.theirs = bf16[2,2,144,128]{3,2,1,0:T(8,128)(2,1)S(1)} collective-permute-done((bf16[2,2,144,128]{3,2,1,0:T(8,128)(2,1)S(1)}, bf16[2,2,144,128]{3,2,1,0:T(8,128)(2,1)S(1)}, u32[]{:S(2)}, u32[]{:S(2)}) %collective-permute-start.13) | collective-permute-done | bytes 147488 | tf_op jit(solution)/shard_map/ppermute | solution.py:32
  90.8 1.9 %finish.1 = bf16[16,4096]{1,0:T(8,128)(2,1)} custom-call(bf16[2,2,144,128]{3,2,1,0:T(8,128)(2,1)} %copy-done, bf16[2,2,144,128]{3,2,1,0:T(8,128)(2,1)} %copy-done.6), custom_call_target="tpu_custom_call" | custom-call | tf_op jit(solution)/shard_map/finish/pallas_call | solution.py:201
  92.7 3.2 %collective-permute-start.16 = (bf16[16,4096]{1,0:T(8,128)(2,1)}, bf16[16,4096]{1,0:T(8,128)(2,1)S(1)}, u32[]{:S(2)}, u32[]{:S(2)}) collective-permute-start(bf16[16,4096]{1,0:T(8,128)(2,1)} %finish.1), channel_id=1, source_target_pairs={{0,96},{1,13},{2,98},{3,15},{4,100},{5,1},{6,102},{7,3},{8,104},{9... | collective-permute-start | bytes 393224 | tf_op jit(solution)/shard_map/ppermute | solution.py:32
  96.8 4.7 %collective-permute-done.16 = bf16[16,4096]{1,0:T(8,128)(2,1)S(1)} collective-permute-done((bf16[16,4096]{1,0:T(8,128)(2,1)}, bf16[16,4096]{1,0:T(8,128)(2,1)S(1)}, u32[]{:S(2)}, u32[]{:S(2)}) %collective-permute-start.16) | collective-permute-done | bytes 131104 | tf_op jit(solution)/shard_map/ppermute | solution.py:32
  101.5 2.7 %collective-permute-done.15 = bf16[16,4096]{1,0:T(8,128)(2,1)S(1)} collective-permute-done((bf16[16,4096]{1,0:T(8,128)(2,1)}, bf16[16,4096]{1,0:T(8,128)(2,1)S(1)}, u32[]{:S(2)}, u32[]{:S(2)}) %collective-permute-start.15) | collective-permute-done | bytes 131104 | tf_op jit(solution)/shard_map/ppermute | solution.py:32
  104.2 5.1 %collective-permute-done.14 = bf16[16,4096]{1,0:T(8,128)(2,1)S(1)} collective-permute-done((bf16[16,4096]{1,0:T(8,128)(2,1)}, bf16[16,4096]{1,0:T(8,128)(2,1)S(1)}, u32[]{:S(2)}, u32[]{:S(2)}) %collective-permute-start.14) | collective-permute-done | bytes 131104 | tf_op jit(solution)/shard_map/ppermute | solution.py:32
  112.5 7.1 %collective-permute-done.19.x3 = bf16[64,4096]{1,0:T(8,128)(2,1)S(1)} collective-permute-done((bf16[64,4096]{1,0:T(8,128)(2,1)S(1)}, bf16[64,4096]{1,0:T(8,128)(2,1)S(1)}, u32[]{:S(2)}, u32[]{:S(2)}) %collective-permute-start.19) | collective-permute-done | bytes 524320 | tf_op jit(solution)/shard_map/ppermute | solution.py:32
  119.6 2.1 %collective-permute-done.18.x2 = bf16[64,4096]{1,0:T(8,128)(2,1)S(1)} collective-permute-done((bf16[64,4096]{1,0:T(8,128)(2,1)S(1)}, bf16[64,4096]{1,0:T(8,128)(2,1)S(1)}, u32[]{:S(2)}, u32[]{:S(2)}) %collective-permute-start.18) | collective-permute-done | bytes 524320 | tf_op jit(solution)/shard_map/ppermute | solution.py:32
  121.7 5.5 %collective-permute-done.17.x1 = bf16[64,4096]{1,0:T(8,128)(2,1)S(1)} collective-permute-done((bf16[64,4096]{1,0:T(8,128)(2,1)S(1)}, bf16[64,4096]{1,0:T(8,128)(2,1)S(1)}, u32[]{:S(2)}, u32[]{:S(2)}) %collective-permute-start.17) | collective-permute-done | bytes 524320 | tf_op jit(solution)/shard_map/ppermute | solution.py:32
  128.0 5.5 %project.1 = f32[256,512]{1,0:T(8,128)} custom-call(s32[5]{0:T(128)} %copy-done.1, bf16[64,4096]{1,0:T(8,128)(2,1)} %copy-done.2, bf16[64,4096]{1,0:T(8,128)(2,1)} %copy-done.5, bf16[64,4096]{1,0:T(8,128)(2,1)} %copy-done.4, bf16[64,4096]{1,0:T(8,128)(2,1)} %copy-done.3, bf16[4096,512]{1,0:T(8,128)(2,1)} %w_ref.1), custom_call_target="tpu_custom_call" | custom-call | tf_op jit(solution)/shard_map/project/pallas_call | solution.py:236
  137.1 2.0 %collective-permute-start.21 = (f32[64,512]{1,0:T(8,128)S(1)}, f32[64,512]{1,0:T(8,128)S(1)}, u32[]{:S(2)}, u32[]{:S(2)}) collective-permute-start(f32[64,512]{1,0:T(8,128)S(1)} %slice.39), channel_id=1, source_target_pairs={{0,2},{1,3},{2,0},{3,1},{4,6},{5,7},{6,4},{7,5},{8,10},{9,11},{10,... | collective-permute-start | bytes 393224 | tf_op jit(solution)/shard_map/ppermute | solution.py:32
  139.1 3.8 %collective-permute-done.21 = f32[64,512]{1,0:T(8,128)S(1)} collective-permute-done((f32[64,512]{1,0:T(8,128)S(1)}, f32[64,512]{1,0:T(8,128)S(1)}, u32[]{:S(2)}, u32[]{:S(2)}) %collective-permute-start.21) | collective-permute-done | bytes 131104 | tf_op jit(solution)/shard_map/ppermute | solution.py:32
  (49 shorter events, 17.1 us)
Async XLA Ops:
  0.9 5.8 %collective-permute-start = (bf16[1,2,128,128]{3,2,1,0:T(8,128)(2,1)S(1)}, bf16[1,2,128,128]{3,2,1,0:T(8,128)(2,1)S(1)}, u32[]{:S(2)}, u32[]{:S(2)}) collective-permute-start(bf16[1,2,128,128]{3,2,1,0:T(8,128)(2,1)S(1)} %bitcast.19), channel_id=1, source_target_pairs={{0,16},{1,17},{2,18},{3,19},{4,20},{5,21},{6,22},{7,23},{8,24},{9,... | collective-permute-start | bytes 196616 | tf_op jit(solution)/shard_map/ppermute | solution.py:32
  6.7 7.1 %collective-permute-start.1 = (bf16[2,2,128,128]{3,2,1,0:T(8,128)(2,1)S(1)}, bf16[2,2,128,128]{3,2,1,0:T(8,128)(2,1)S(1)}, u32[]{:S(2)}, u32[]{:S(2)}) collective-permute-start(bf16[2,2,128,128]{3,2,1,0:T(8,128)(2,1)S(1)} %pad_maximum_fusion.1), channel_id=1, source_target_pairs={{0,32},{1,5},{2,34},{3,7},{4,36},{5,9},{6,38},{7,11},{8,40},{9,13}... | collective-permute-start | bytes 393224 | tf_op jit(solution)/shard_map/ppermute | solution.py:32
  9.7 8.7 %collective-permute-start.3 = (bf16[2,2,128,128]{3,2,1,0:T(8,128)(2,1)S(1)}, bf16[2,2,128,128]{3,2,1,0:T(8,128)(2,1)S(1)}, u32[]{:S(2)}, u32[]{:S(2)}) collective-permute-start(bf16[2,2,128,128]{3,2,1,0:T(8,128)(2,1)S(1)} %pad_maximum_fusion.1), channel_id=1, source_target_pairs={{0,96},{1,13},{2,98},{3,15},{4,100},{5,1},{6,102},{7,3},{8,104},{9... | collective-permute-start | bytes 393224 | tf_op jit(solution)/shard_map/ppermute | solution.py:32
  11.9 6.5 %collective-permute-start.2 = (bf16[2,2,128,128]{3,2,1,0:T(8,128)(2,1)S(1)}, bf16[2,2,128,128]{3,2,1,0:T(8,128)(2,1)S(1)}, u32[]{:S(2)}, u32[]{:S(2)}) collective-permute-start(bf16[2,2,128,128]{3,2,1,0:T(8,128)(2,1)S(1)} %pad_maximum_fusion.1), channel_id=1, source_target_pairs={{0,64},{1,9},{2,66},{3,11},{4,68},{5,13},{6,70},{7,15},{8,72},{9,1... | collective-permute-start | bytes 393224 | tf_op jit(solution)/shard_map/ppermute | solution.py:32
  18.4 15.7 %collective-permute-start.4 = (bf16[8,2,128,128]{3,2,1,0:T(8,128)(2,1)S(1)}, bf16[8,2,128,128]{3,2,1,0:T(8,128)(2,1)S(1)}, u32[]{:S(2)}, u32[]{:S(2)}) collective-permute-start(bf16[8,2,128,128]{3,2,1,0:T(8,128)(2,1)S(1)} %constant_dynamic-update-slice_fusion.q_ref), channel_id=1, source_target_pairs={{0,4},{1,33},{2,6},{3,35},{4,8},{5,37},{6,10},{7,39},{8,12},{9,41}... | collective-permute-start | bytes 1572872 | tf_op jit(solution)/shard_map/ppermute | solution.py:32
  23.2 24.7 %copy-start.1 = (s32[5]{0:T(128)}, s32[5]{0:T(128)S(1)}, u32[]{:S(2)}) copy-start(s32[5]{0:T(128)S(1)} %stack.23.me_ref) | copy-start | bytes 64
  23.2 24.7 %collective-permute-start.8 = (bf16[8,2,128,128]{3,2,1,0:T(8,128)(2,1)S(1)}, bf16[8,2,128,128]{3,2,1,0:T(8,128)(2,1)S(1)}, u32[]{:S(2)}, u32[]{:S(2)}) collective-permute-start(bf16[8,2,128,128]{3,2,1,0:T(8,128)(2,1)S(1)} %constant_dynamic-update-slice_fusion.q_ref), channel_id=1, source_target_pairs={{0,8},{1,65},{2,10},{3,67},{4,12},{5,69},{6,14},{7,71},{8,0},{9,73... | collective-permute-start | bytes 1572872 | tf_op jit(solution)/shard_map/ppermute | solution.py:32
  26.0 14.9 %collective-permute-start.6 = (bf16[8,2,128,128]{3,2,1,0:T(8,128)(2,1)S(1)}, bf16[8,2,128,128]{3,2,1,0:T(8,128)(2,1)S(1)}, u32[]{:S(2)}, u32[]{:S(2)}) collective-permute-start(bf16[8,2,128,128]{3,2,1,0:T(8,128)(2,1)S(1)} %constant_dynamic-update-slice_fusion.q_ref), channel_id=1, source_target_pairs={{0,12},{1,97},{2,14},{3,99},{4,0},{5,101},{6,2},{7,103},{8,4},{9,1... | collective-permute-start | bytes 1572872 | tf_op jit(solution)/shard_map/ppermute | solution.py:32
  54.7 11.6 %collective-permute-start.9 = (bf16[8,2,144,128]{3,2,1,0:T(8,128)(2,1)S(1)}, bf16[8,2,144,128]{3,2,1,0:T(8,128)(2,1)S(1)}, u32[]{:S(2)}, u32[]{:S(2)}) collective-permute-start(bf16[8,2,144,128]{3,2,1,0:T(8,128)(2,1)S(1)} %attend_plane.7), channel_id=1, source_target_pairs={{0,8},{1,65},{2,10},{3,67},{4,12},{5,69},{6,14},{7,71},{8,0},{9,73... | collective-permute-start | bytes 1769480 | tf_op jit(solution)/shard_map/ppermute | solution.py:32
  55.3 17.2 %collective-permute-start.7 = (bf16[8,2,144,128]{3,2,1,0:T(8,128)(2,1)S(1)}, bf16[8,2,144,128]{3,2,1,0:T(8,128)(2,1)S(1)}, u32[]{:S(2)}, u32[]{:S(2)}) collective-permute-start(bf16[8,2,144,128]{3,2,1,0:T(8,128)(2,1)S(1)} %attend_plane.6), channel_id=1, source_target_pairs={{0,4},{1,33},{2,6},{3,35},{4,8},{5,37},{6,10},{7,39},{8,12},{9,41}... | collective-permute-start | bytes 1769480 | tf_op jit(solution)/shard_map/ppermute | solution.py:32
  55.8 16.7 %collective-permute-start.5 = (bf16[8,2,144,128]{3,2,1,0:T(8,128)(2,1)S(1)}, bf16[8,2,144,128]{3,2,1,0:T(8,128)(2,1)S(1)}, u32[]{:S(2)}, u32[]{:S(2)}) collective-permute-start(bf16[8,2,144,128]{3,2,1,0:T(8,128)(2,1)S(1)} %attend_plane.5), channel_id=1, source_target_pairs={{0,12},{1,97},{2,14},{3,99},{4,0},{5,101},{6,2},{7,103},{8,4},{9,1... | collective-permute-start | bytes 1769480 | tf_op jit(solution)/shard_map/ppermute | solution.py:32
  73.8 6.7 %collective-permute-start.12 = (bf16[2,2,144,128]{3,2,1,0:T(8,128)(2,1)S(1)}, bf16[2,2,144,128]{3,2,1,0:T(8,128)(2,1)S(1)}, u32[]{:S(2)}, u32[]{:S(2)}) collective-permute-start(bf16[2,2,144,128]{3,2,1,0:T(8,128)(2,1)S(1)} %get-tuple-element.11), channel_id=1, source_target_pairs={{0,64},{1,9},{2,66},{3,11},{4,68},{5,13},{6,70},{7,15},{8,72},{9,1... | collective-permute-start | bytes 442376 | tf_op jit(solution)/shard_map/ppermute | solution.py:32
  76.7 6.4 %collective-permute-start.11 = (bf16[2,2,144,128]{3,2,1,0:T(8,128)(2,1)S(1)}, bf16[2,2,144,128]{3,2,1,0:T(8,128)(2,1)S(1)}, u32[]{:S(2)}, u32[]{:S(2)}) collective-permute-start(bf16[2,2,144,128]{3,2,1,0:T(8,128)(2,1)S(1)} %get-tuple-element.12), channel_id=1, source_target_pairs={{0,32},{1,5},{2,34},{3,7},{4,36},{5,9},{6,38},{7,11},{8,40},{9,13}... | collective-permute-start | bytes 442376 | tf_op jit(solution)/shard_map/ppermute | solution.py:32
  77.3 5.7 %collective-permute-start.10 = (bf16[2,2,144,128]{3,2,1,0:T(8,128)(2,1)S(1)}, bf16[2,2,144,128]{3,2,1,0:T(8,128)(2,1)S(1)}, u32[]{:S(2)}, u32[]{:S(2)}) collective-permute-start(bf16[2,2,144,128]{3,2,1,0:T(8,128)(2,1)S(1)} %get-tuple-element.13), channel_id=1, source_target_pairs={{0,96},{1,13},{2,98},{3,15},{4,100},{5,1},{6,102},{7,3},{8,104},{9... | collective-permute-start | bytes 442376 | tf_op jit(solution)/shard_map/ppermute | solution.py:32
  83.4 6.7 %copy-start = (bf16[2,2,144,128]{3,2,1,0:T(8,128)(2,1)}, bf16[2,2,144,128]{3,2,1,0:T(8,128)(2,1)S(1)}, u32[]{:S(2)}) copy-start(bf16[2,2,144,128]{3,2,1,0:T(8,128)(2,1)S(1)} %combine.3.mine) | copy-start | bytes 442372
  83.4 6.7 %collective-permute-start.13 = (bf16[2,2,144,128]{3,2,1,0:T(8,128)(2,1)S(1)}, bf16[2,2,144,128]{3,2,1,0:T(8,128)(2,1)S(1)}, u32[]{:S(2)}, u32[]{:S(2)}) collective-permute-start(bf16[2,2,144,128]{3,2,1,0:T(8,128)(2,1)S(1)} %combine.3.mine), channel_id=1, source_target_pairs={{0,16},{1,17},{2,18},{3,19},{4,20},{5,21},{6,22},{7,23},{8,24},{9,... | collective-permute-start | bytes 442376 | tf_op jit(solution)/shard_map/ppermute | solution.py:32
  90.1 0.7 copy-start.6
  92.7 8.7 %collective-permute-start.16 = (bf16[16,4096]{1,0:T(8,128)(2,1)}, bf16[16,4096]{1,0:T(8,128)(2,1)S(1)}, u32[]{:S(2)}, u32[]{:S(2)}) collective-permute-start(bf16[16,4096]{1,0:T(8,128)(2,1)} %finish.1), channel_id=1, source_target_pairs={{0,96},{1,13},{2,98},{3,15},{4,100},{5,1},{6,102},{7,3},{8,104},{9... | collective-permute-start | bytes 393224 | tf_op jit(solution)/shard_map/ppermute | solution.py:32
  96.0 8.2 %collective-permute-start.15 = (bf16[16,4096]{1,0:T(8,128)(2,1)}, bf16[16,4096]{1,0:T(8,128)(2,1)S(1)}, u32[]{:S(2)}, u32[]{:S(2)}) collective-permute-start(bf16[16,4096]{1,0:T(8,128)(2,1)} %finish.1), channel_id=1, source_target_pairs={{0,64},{1,9},{2,66},{3,11},{4,68},{5,13},{6,70},{7,15},{8,72},{9,1... | collective-permute-start | bytes 393224 | tf_op jit(solution)/shard_map/ppermute | solution.py:32
  96.0 13.4 %collective-permute-start.14 = (bf16[16,4096]{1,0:T(8,128)(2,1)}, bf16[16,4096]{1,0:T(8,128)(2,1)S(1)}, u32[]{:S(2)}, u32[]{:S(2)}) collective-permute-start(bf16[16,4096]{1,0:T(8,128)(2,1)} %finish.1), channel_id=1, source_target_pairs={{0,32},{1,5},{2,34},{3,7},{4,36},{5,9},{6,38},{7,11},{8,40},{9,13}... | collective-permute-start | bytes 393224 | tf_op jit(solution)/shard_map/ppermute | solution.py:32
  110.3 16.9 %copy-start.2 = (bf16[64,4096]{1,0:T(8,128)(2,1)}, bf16[64,4096]{1,0:T(8,128)(2,1)S(1)}, u32[]{:S(2)}) copy-start(bf16[64,4096]{1,0:T(8,128)(2,1)S(1)} %pad_maximum_fusion.x0) | copy-start | bytes 1572868
  110.3 9.2 %collective-permute-start.19 = (bf16[64,4096]{1,0:T(8,128)(2,1)S(1)}, bf16[64,4096]{1,0:T(8,128)(2,1)S(1)}, u32[]{:S(2)}, u32[]{:S(2)}) collective-permute-start(bf16[64,4096]{1,0:T(8,128)(2,1)S(1)} %pad_maximum_fusion.x0), channel_id=1, source_target_pairs={{0,12},{1,97},{2,14},{3,99},{4,0},{5,101},{6,2},{7,103},{8,4},{9,1... | collective-permute-start | bytes 1572872 | tf_op jit(solution)/shard_map/ppermute | solution.py:32
  110.9 10.8 %collective-permute-start.18 = (bf16[64,4096]{1,0:T(8,128)(2,1)S(1)}, bf16[64,4096]{1,0:T(8,128)(2,1)S(1)}, u32[]{:S(2)}, u32[]{:S(2)}) collective-permute-start(bf16[64,4096]{1,0:T(8,128)(2,1)S(1)} %pad_maximum_fusion.x0), channel_id=1, source_target_pairs={{0,8},{1,65},{2,10},{3,67},{4,12},{5,69},{6,14},{7,71},{8,0},{9,73... | collective-permute-start | bytes 1572872 | tf_op jit(solution)/shard_map/ppermute | solution.py:32
  111.8 15.4 %collective-permute-start.17 = (bf16[64,4096]{1,0:T(8,128)(2,1)S(1)}, bf16[64,4096]{1,0:T(8,128)(2,1)S(1)}, u32[]{:S(2)}, u32[]{:S(2)}) collective-permute-start(bf16[64,4096]{1,0:T(8,128)(2,1)S(1)} %pad_maximum_fusion.x0), channel_id=1, source_target_pairs={{0,4},{1,33},{2,6},{3,35},{4,8},{5,37},{6,10},{7,39},{8,12},{9,41}... | collective-permute-start | bytes 1572872 | tf_op jit(solution)/shard_map/ppermute | solution.py:32
  119.6 7.7 %copy-start.3 = (bf16[64,4096]{1,0:T(8,128)(2,1)}, bf16[64,4096]{1,0:T(8,128)(2,1)S(1)}, u32[]{:S(2)}) copy-start(bf16[64,4096]{1,0:T(8,128)(2,1)S(1)} %collective-permute-done.19.x3) | copy-start | bytes 1572868
  121.7 5.5 %copy-start.4 = (bf16[64,4096]{1,0:T(8,128)(2,1)}, bf16[64,4096]{1,0:T(8,128)(2,1)S(1)}, u32[]{:S(2)}) copy-start(bf16[64,4096]{1,0:T(8,128)(2,1)S(1)} %collective-permute-done.18.x2) | copy-start | bytes 1572868
  127.2 0.8 copy-start.5
  134.5 1.6 %collective-permute-start.20 = (f32[128,512]{1,0:T(8,128)S(1)}, f32[128,512]{1,0:T(8,128)S(1)}, u32[]{:S(2)}, u32[]{:S(2)}) collective-permute-start(f32[128,512]{1,0:T(8,128)S(1)} %slice.37), channel_id=1, source_target_pairs={{0,1},{1,0},{2,3},{3,2},{4,5},{5,4},{6,7},{7,6},{8,9},{9,8},{10,11... | collective-permute-start | bytes 786440 | tf_op jit(solution)/shard_map/ppermute | solution.py:32
  137.1 5.8 %collective-permute-start.21 = (f32[64,512]{1,0:T(8,128)S(1)}, f32[64,512]{1,0:T(8,128)S(1)}, u32[]{:S(2)}, u32[]{:S(2)}) collective-permute-start(f32[64,512]{1,0:T(8,128)S(1)} %slice.39), channel_id=1, source_target_pairs={{0,2},{1,3},{2,0},{3,1},{4,6},{5,7},{6,4},{7,5},{8,10},{9,11},{10,... | collective-permute-start | bytes 393224 | tf_op jit(solution)/shard_map/ppermute | solution.py:32
where the time goes:
time: 144 us
  waiting for transfers between devices  60.2 us (42%)
  starting transfers between devices  36.8 us (26%)
  Pallas kernels  36.3 us (25%)
  local copies, waits for them, and re-layouts  6.19 us (4%)
  other arithmetic  2.59 us (2%)
  between operations  1.55 us (1%)
    ppermute x22, waiting for transfers between devices, moved(): return lax.ppermute(x, ('cp', 'tp'), pairs)  60.2 us
    ppermute x22, starting transfers between devices, moved(): return lax.ppermute(x, ('cp', 'tp'), pairs)  36.8 us
    pallas_call x4, Pallas kernels, attend(): pl.pallas_call(functools.partial(attend_kernel, db=db, kvs=kvs, nb=nb, sp...  27.2 us
    pallas_call x1, Pallas kernels, project(): pl.pallas_call(project_kernel, grid=(steps,), in_specs=[pl.BlockSpec(memo...  5.49 us
  transfers between devices with their start and end apart: 22, of which 16 were waited for; matrix products, arithmetic and copies ran while one was open for 2% of the time, Pallas kernels for 14%

commit v1 on v0

--- a/solution.py
+++ b/solution.py
@@ -32,8 +32,8 @@
     return lax.ppermute(x, ("cp", "tp"), pairs)
 
 
-def after(x, *earlier):
-    return lax.optimization_barrier((x, *earlier))[0]
+def together(*arrays):
+    return lax.optimization_barrier(arrays)
 
 
 def source(me, da, db, dy):
@@ -61,7 +61,7 @@
     return jnp.concatenate([m, high, l - high, jnp.zeros((13, 128), jnp.float32)], axis=0).astype(jnp.bfloat16)
 
 
-def attend_kernel(me_ref, len_ref, start_ref, q_ref, k_ref, v_ref, o_ref, vx, kx, *, db, kvs, nb, span, tile, scale):
+def attend_kernel(me_ref, len_ref, start_ref, q_ref, k_ref, v_ref, o_ref, vx, kx, *, db, kvs, first, nb, span, tile, scale):
     step = pl.program_id(0)
     rows = nb * 128
 
@@ -84,7 +84,7 @@
     eye = diagonal()
     row = lax.broadcasted_iota(jnp.int32, (rows, 128), 0)
     lane = lax.broadcasted_iota(jnp.int32, (rows, 128), 1)
-    hot = jnp.where(lane == (step * nb + (row >> 7)) * 8 + (row & 7), 1.0, 0.0).astype(jnp.bfloat16)
+    hot = jnp.where(lane == (first + step * nb + (row >> 7)) * 8 + (row & 7), 1.0, 0.0).astype(jnp.bfloat16)
 
     def scores(i, t):
         q = jnp.concatenate([q_ref[:, kvs[i]].reshape(rows, 128), hot], axis=1)
@@ -103,11 +103,11 @@
 
     ok = []
     for i in range(len(kvs)):
-        first = scores(i, 0)
-        m = point(jnp.max(first, axis=1, keepdims=True))
+        s0 = scores(i, 0)
+        m = point(jnp.max(s0, axis=1, keepdims=True))
         p = []
         for t in range(0, span, tile):
-            s = first if t == 0 else scores(i, t)
+            s = s0 if t == 0 else scores(i, t)
             p.append(jnp.exp2(s * scale - m).astype(jnp.bfloat16))
         acc = jnp.dot(jnp.concatenate(p, axis=1), vx[i], preferred_element_type=jnp.float32)
         ok.append(jnp.min(jnp.where(acc[:, 128:] < BIG, 1.0, 0.0)))
@@ -131,17 +131,17 @@
             put(i, m, lax.fori_loop(0, span // tile, add, jnp.zeros((rows, 256), jnp.float32)))
 
 
-def attend(me, lengths, start, q, k, v, db, kvs):
-    blocks = q.shape[0]
+def attend(me, lengths, start, q, *, k, v, kvs, db, first=0, blocks=8):
     span = v.shape[1]
     nb, tile = 8 // len(kvs), 256
+    skip = first // nb
     smem, vmem = pl.BlockSpec(memory_space=pltpu.SMEM), pl.BlockSpec(memory_space=pltpu.VMEM)
     return pl.pallas_call(
         functools.partial(
-            attend_kernel, db=db, kvs=kvs, nb=nb, span=span, tile=tile, scale=math.log2(math.e) / math.sqrt(128)
+            attend_kernel, db=db, kvs=kvs, first=first, nb=nb, span=span, tile=tile, scale=math.log2(math.e) / math.sqrt(128)
         ),
         grid=(blocks // nb,),
-        in_specs=[smem, smem, smem, pl.BlockSpec((nb, *q.shape[1:]), lambda i: (i, 0, 0, 0)), vmem, vmem],
+        in_specs=[smem, smem, smem, pl.BlockSpec((nb, *q.shape[1:]), lambda i: (skip + i, 0, 0, 0)), vmem, vmem],
         out_specs=pl.BlockSpec((nb, len(kvs), 144, 128), lambda i: (i, 0, 0, 0)),
         out_shape=jax.ShapeDtypeStruct((blocks, len(kvs), 144, 128), jnp.bfloat16),
         scratch_shapes=[pltpu.VMEM((len(kvs), span, 256), jnp.bfloat16)] * 2,
@@ -167,22 +167,26 @@
     return out, m, total
 
 
-def combine_kernel(*refs):
-    parts, o_ref = refs[:-1], refs[-1]
+def combine_kernel(*refs, own):
+    o_ref = refs[-1]
     eye = diagonal()
     for b, kv in itertools.product(range(o_ref.shape[0]), range(o_ref.shape[1])):
-        out, m, total = merged([p[b, kv] for p in parts], eye)
+        share = o_ref.shape[0] // own
+        out, m, total = merged([refs[b // share][b % share, kv]] + [r[b, kv] for r in refs[own:-1]], eye)
         o_ref[b, kv, :128, :] = out.astype(jnp.bfloat16)
         o_ref[b, kv, 128:, :] = stat_rows(m, total)
 
 
-def combine(parts):
-    return pl.pallas_call(
-        combine_kernel,
-        out_shape=jax.ShapeDtypeStruct(parts[0].shape, jnp.bfloat16),
-        compiler_params=pltpu.CompilerParams(vmem_limit_bytes=16 * MIB),
+def combine(own, others):
+    vmem = pl.BlockSpec(memory_space=pltpu.VMEM)
+    return pl.pallas_call(
+        functools.partial(combine_kernel, own=len(own)),
+        in_specs=[vmem] * (len(own) + len(others)),
+        out_specs=vmem,
+        out_shape=jax.ShapeDtypeStruct(others[0].shape, jnp.bfloat16),
+        compiler_params=pltpu.CompilerParams(vmem_limit_bytes=8 * MIB),
         name="combine",
-    )(*parts)
+    )(*own, *others)
 
 
 def finish_kernel(mine, theirs, o_ref):
@@ -198,53 +202,76 @@
 
 
 def finish(mine, theirs):
+    vmem = pl.BlockSpec(memory_space=pltpu.VMEM)
     return pl.pallas_call(
         finish_kernel,
+        in_specs=[vmem, vmem],
+        out_specs=vmem,
+        compiler_params=pltpu.CompilerParams(vmem_limit_bytes=4 * MIB),
         out_shape=jax.ShapeDtypeStruct((16, mine.shape[1] * 2048), jnp.bfloat16),
         name="finish",
     )(mine, theirs)
 
 
-def project_kernel(me_ref, x0, x1, x2, x3, w_ref, o_ref, acc):
-    step = pl.program_id(0)
-    x = jnp.concatenate([r[...] for r in (x0, x1, x2, x3)], axis=0)
-    y = jnp.dot(x, w_ref[...], preferred_element_type=jnp.float32)
-
-    @pl.when(step == 0)
-    def _():
-        acc[...] = y
-
-    @pl.when(step > 0)
-    def _():
-        acc[...] += y
-
-    @pl.when(step == pl.num_programs(0) - 1)
-    def _():
-        me = tuple(me_ref[i] for i in range(5))
-        yl, core = me[3], me[4]
-        for db, da, dy in itertools.product(range(RING), range(RING), range(2)):
+def assemble_kernel(x0, x1, x2, x3, _, o_ref):
+    for i, x in enumerate((x0, x1, x2, x3)):
+        o_ref[i * x.shape[0] : (i + 1) * x.shape[0], :] = x[...]
+
+
+def assemble(*pieces):
+    vmem = pl.BlockSpec(memory_space=pltpu.VMEM)
+    rows, width = pieces[0].shape
+    return pl.pallas_call(
+        assemble_kernel,
+        in_specs=[vmem] * 4 + [pl.BlockSpec(memory_space=pl.ANY)],
+        out_specs=vmem,
+        out_shape=jax.ShapeDtypeStruct((RING * rows, width), pieces[0].dtype),
+        compiler_params=pltpu.CompilerParams(vmem_limit_bytes=4 * MIB),
+        name="assemble",
+    )(*pieces)
+
+
+def project_kernel(x_ref, w_ref, o_ref):
+    o_ref[...] = jnp.dot(x_ref[...], w_ref[...], preferred_element_type=jnp.float32)
+
+
+def project(x, w):
+    vmem = pl.BlockSpec(memory_space=pltpu.VMEM)
+    return pl.pallas_call(
+        project_kernel,
+        in_specs=[vmem, vmem],
+        out_specs=vmem,
+        out_shape=jax.ShapeDtypeStruct((x.shape[0], w.shape[1]), jnp.float32),
+        compiler_params=pltpu.CompilerParams(vmem_limit_bytes=8 * MIB),
+        cost_estimate=pl.CostEstimate(
+            flops=8 * x.shape[0] * w.shape[0] * w.shape[1], bytes_accessed=4 * MIB, transcendentals=0
+        ),
+        name="project",
+    )(x, w)
+
+
+def place_kernel(me_ref, y0, y1, y3, x_ref, w_ref, o_ref):
+    me = tuple(me_ref[i] for i in range(5))
+    yl, core = me[3], me[4]
+    y2 = jnp.dot(x_ref[...], w_ref[...], preferred_element_type=jnp.float32)
+    for db, y in ((0, y0), (1, y1), (2, y2), (3, y3)):
+        for da, dy in itertools.product(range(RING), range(2)):
             z, yh, xx = source(me, da, db, dy)
             row = (((z & 1) ^ core) * 2 + ((z >> 1) ^ yl)) * 64 + yh * 32 + xx * 8
-            at = (db * RING + da) * 16 + dy * 8
-            o_ref[pl.ds(pl.multiple_of(row, 8), 8), :] = acc[at : at + 8, :]
-
-
-def project(me, planes, w):
-    rows = sum(p.shape[0] for p in planes)
-    steps = 4
-    depth = w.shape[0] // steps
-    return pl.pallas_call(
-        project_kernel,
-        grid=(steps,),
-        in_specs=[pl.BlockSpec(memory_space=pltpu.SMEM)]
-        + [pl.BlockSpec((p.shape[0], depth), lambda i: (0, i)) for p in planes]
-        + [pl.BlockSpec((depth, w.shape[1]), lambda i: (i, 0))],
-        out_specs=pl.BlockSpec((rows, w.shape[1]), lambda i: (0, 0)),
-        out_shape=jax.ShapeDtypeStruct((rows, w.shape[1]), jnp.float32),
-        scratch_shapes=[pltpu.VMEM((rows, w.shape[1]), jnp.float32)],
-        compiler_params=pltpu.CompilerParams(vmem_limit_bytes=56 * MIB, dimension_semantics=("arbitrary",)),
-        name="project",
-    )(me, *planes, w)
+            at = da * 16 + dy * 8
+            o_ref[pl.ds(pl.multiple_of(row, 8), 8), :] = y[at : at + 8, :]
+
+
+def place(me, y0, y1, y3, x, w):
+    vmem = pl.BlockSpec(memory_space=pltpu.VMEM)
+    return pl.pallas_call(
+        place_kernel,
+        in_specs=[pl.BlockSpec(memory_space=pltpu.SMEM)] + [vmem] * 5,
+        out_specs=vmem,
+        out_shape=jax.ShapeDtypeStruct((RING * x.shape[0], w.shape[1]), jnp.float32),
+        compiler_params=pltpu.CompilerParams(vmem_limit_bytes=8 * MIB),
+        name="place",
+    )(me, y0, y1, y3, x, w)
 
 
 def on_device(queries, keys, values, lengths, start, out_weight):
@@ -254,22 +281,31 @@
     v = values.transpose(1, 0, 2)
     q = queries.reshape(8, nkv, 16, 128).transpose(1, 2, 0, 3).reshape(1, nkv, 128, 128)
     q = jnp.concatenate([q, moved(q, yh=1)], axis=0)
+    q, k, v, me = together(q, k, v, me)
     q = jnp.concatenate([q] + [moved(q, a=d) for d in (1, 2, 3)], axis=0)
-    planes = {0: q}
-    for d in (1, 3, 2):
-        planes[d] = moved(q, b=d)
+    q1, q3, q2 = (moved(q, b=d) for d in (1, 3, 2))
 
     kvs = tuple(range(nkv))
-    parts = []
-    for d in (0, 1, 3, 2):
-        x = after(planes[d], parts[-1]) if parts else planes[d]
-        parts.append(attend(me, lengths, start, x, k, v, d, kvs))
-    c = combine([parts[0]] + [moved(p, b=-d) for p, d in zip(parts[1:], (1, 3, 2))])
-    c = combine([c[:2]] + [moved(c[2 * d : 2 * d + 2], a=-d) for d in (1, 3, 2)])
+    part = functools.partial(attend, me, lengths, start, k=k, v=v, kvs=kvs)
+    own0 = part(q, db=0, first=0, blocks=4)
+    q1, own0 = together(q1, own0)
+    p1 = part(q1, db=1)
+    r1 = moved(p1, b=-1)
+    q3, p1 = together(q3, p1)
+    p3 = part(q3, db=3)
+    r3 = moved(p3, b=-3)
+    q2, p3, r1 = together(q2, p3, r1)
+    p2 = part(q2, db=2)
+    r2 = moved(p2, b=-2)
+    q, p2, r3 = together(q, p2, r3)
+    own1 = part(q, db=0, first=4, blocks=4)
+    c = combine([own0, own1], [r1, r3, r2])
+    c = combine([c[:2]], [moved(c[2 * d : 2 * d + 2], a=-d) for d in (1, 3, 2)])
     attn = finish(c, moved(c, yh=1))
-    attn = jnp.concatenate([attn] + [moved(attn, a=d) for d in (1, 2, 3)], axis=0)
-    rows = [attn] + [moved(attn, b=d) for d in (1, 2, 3)]
-    y = project(me, rows, out_weight)
+    pieces = [moved(attn, a=d) for d in (1, 2, 3)]
+    attn = assemble(attn, *pieces, moved(pieces[1], core=1))
+    x1, x3, x2 = (moved(attn, b=d) for d in (1, 3, 2))
+    y = place(me, project(attn, out_weight), project(x1, out_weight), project(x3, out_weight), x2, out_weight)
     y = y[:128] + moved(y[128:], core=1)
     y = y[:64] + moved(y[64:], yl=1)
     return y.astype(jnp.bfloat16)

time: 144 us -> 124 us (0.86)
  waiting for transfers between devices: 60.2 us -> 45.3 us
  local copies, waits for them, and re-layouts: 6.19 us -> 2.91 us
  starting transfers between devices: 36.8 us -> 39.9 us
  Pallas kernels: 36.3 us -> 33.6 us
  other arithmetic: 2.59 us -> 0.7 us
    ppermute x22 -> x23, waiting for transfers between devices: 60.2 us -> 45.3 us  [moved(): return lax.ppermute(x, ('cp', 'tp'), pairs)]
    ppermute x22 -> x23, starting transfers between devices: 36.8 us -> 39.9 us  [moved(): return lax.ppermute(x, ('cp', 'tp'), pairs)]
    pallas_call x8 -> x13, Pallas kernels: 36.3 us -> 33.6 us  [the longest x5 27.8 us: attend(): pl.pallas_call(functools.partial(attend_kernel, db=db, kvs=kvs, first=fir...]
    unnamed x18 -> x5, local copies, waits for them, and re-layouts: 2.39 us -> 0.05 us
  transfers between devices with their start and end apart: 22 -> 23, of which waited for: 16 -> 18; matrix products, arithmetic and copies ran while one was open for 2% -> 2% of each run, Pallas kernels for 14% -> 24%
where the time goes in v1:
time: 124 us
  waiting for transfers between devices  45.3 us (37%)
  starting transfers between devices  39.9 us (32%)
  Pallas kernels  33.6 us (27%)
  local copies, waits for them, and re-layouts  2.91 us (2%)
  between operations  1.54 us (1%)
    ppermute x23, waiting for transfers between devices, moved(): return lax.ppermute(x, ('cp', 'tp'), pairs)  45.3 us
    ppermute x23, starting transfers between devices, moved(): return lax.ppermute(x, ('cp', 'tp'), pairs)  39.9 us
    pallas_call x5, Pallas kernels, attend(): pl.pallas_call(functools.partial(attend_kernel, db=db, kvs=kvs, first=fir...  27.8 us
    pallas_call x3, Pallas kernels, project(): pl.pallas_call(project_kernel, in_specs=[vmem, vmem], out_specs=vmem, out...  2.49 us
  transfers between devices with their start and end apart: 23, of which 18 were waited for; matrix products, arithmetic and copies ran while one was open for 2% of the time, Pallas kernels for 24%

profile of v1, /device:TPU:0, one launch (start us, length us, event | category | flops | bytes accessed | tf_op | source)
XLA Modules:
  0.0 123.9 jit_solution(4400891831743743551)
XLA Ops:
  0.9 3.4 %collective-permute-start = (bf16[1,2,128,128]{3,2,1,0:T(8,128)(2,1)S(1)}, bf16[1,2,128,128]{3,2,1,0:T(8,128)(2,1)S(1)}, u32[]{:S(2)}, u32[]{:S(2)}) collective-permute-start(bf16[1,2,128,128]{3,2,1,0:T(8,128)(2,1)S(1)} %bitcast.15), channel_id=1, source_target_pairs={{0,16},{1,17},{2,18},{3,19},{4,20},{5,21},{6,22},{7,23},{8,24},{9,... | collective-permute-start | bytes 196616 | tf_op jit(solution)/shard_map/ppermute | solution.py:32
  4.2 1.8 %copy_bitcast_fusion = (bf16[2,2048,128]{2,1,0:T(8,128)(2,1)S(1)}, bf16[2,2048,128]{2,1,0:T(8,128)(2,1)S(1)}) fusion(bf16[2048,2,128]{2,1,0:T(2,128)(2,1)} %param.8, bf16[2048,2,128]{2,1,0:T(2,128)(2,1)} %param.7), kind=kLoop, calls=%fused_computation | loop fusion | bytes 4194304 | tf_op jit(solution)/shard_map/transpose | solution.py:281
  6.7 2.1 %collective-permute-start.1 = (bf16[2,2,128,128]{3,2,1,0:T(8,128)(2,1)S(1)}, bf16[2,2,128,128]{3,2,1,0:T(8,128)(2,1)S(1)}, u32[]{:S(2)}, u32[]{:S(2)}) collective-permute-start(bf16[2,2,128,128]{3,2,1,0:T(8,128)(2,1)S(1)} %pad_maximum_fusion), channel_id=1, source_target_pairs={{0,32},{1,5},{2,34},{3,7},{4,36},{5,9},{6,38},{7,11},{8,40},{9,13}... | collective-permute-start | bytes 393224 | tf_op jit(solution)/shard_map/ppermute | solution.py:32
  8.8 3.6 %collective-permute-start.2 = (bf16[2,2,128,128]{3,2,1,0:T(8,128)(2,1)S(1)}, bf16[2,2,128,128]{3,2,1,0:T(8,128)(2,1)S(1)}, u32[]{:S(2)}, u32[]{:S(2)}) collective-permute-start(bf16[2,2,128,128]{3,2,1,0:T(8,128)(2,1)S(1)} %pad_maximum_fusion), channel_id=1, source_target_pairs={{0,64},{1,9},{2,66},{3,11},{4,68},{5,13},{6,70},{7,15},{8,72},{9,1... | collective-permute-start | bytes 393224 | tf_op jit(solution)/shard_map/ppermute | solution.py:32
  13.9 2.8 %collective-permute-done.2 = bf16[2,2,128,128]{3,2,1,0:T(8,128)(2,1)S(1)} collective-permute-done((bf16[2,2,128,128]{3,2,1,0:T(8,128)(2,1)S(1)}, bf16[2,2,128,128]{3,2,1,0:T(8,128)(2,1)S(1)}, u32[]{:S(2)}, u32[]{:S(2)}) %collective-permute-start.2) | collective-permute-done | bytes 131104 | tf_op jit(solution)/shard_map/ppermute | solution.py:32
  17.5 1.6 %collective-permute-start.4 = (bf16[8,2,128,128]{3,2,1,0:T(8,128)(2,1)S(1)}, bf16[8,2,128,128]{3,2,1,0:T(8,128)(2,1)S(1)}, u32[]{:S(2)}, u32[]{:S(2)}) collective-permute-start(bf16[8,2,128,128]{3,2,1,0:T(8,128)(2,1)S(1)} %constant_dynamic-update-slice_fusion.q_ref), channel_id=1, source_target_pairs={{0,4},{1,33},{2,6},{3,35},{4,8},{5,37},{6,10},{7,39},{8,12},{9,41}... | collective-permute-start | bytes 1572872 | tf_op jit(solution)/shard_map/ppermute | solution.py:32
  20.3 1.8 %collective-permute-start.6 = (bf16[8,2,128,128]{3,2,1,0:T(8,128)(2,1)S(1)}, bf16[8,2,128,128]{3,2,1,0:T(8,128)(2,1)S(1)}, u32[]{:S(2)}, u32[]{:S(2)}) collective-permute-start(bf16[8,2,128,128]{3,2,1,0:T(8,128)(2,1)S(1)} %constant_dynamic-update-slice_fusion.q_ref), channel_id=1, source_target_pairs={{0,12},{1,97},{2,14},{3,99},{4,0},{5,101},{6,2},{7,103},{8,4},{9,1... | collective-permute-start | bytes 1572872 | tf_op jit(solution)/shard_map/ppermute | solution.py:32
  22.1 3.7 %attend_plane.5.refs_0_ = bf16[4,2,144,128]{3,2,1,0:T(8,128)(2,1)S(1)} custom-call(s32[5]{0:T(128)S(1)} %stack.23.me_ref, s32[1]{0:T(128)S(6)} %copy.17.len_ref, s32[1]{0:T(128)S(6)} %copy.18.start_ref, bf16[8,2,128,128]{3,2,1,0:T(8,128)(2,1)S(1)} %constant_dynamic-update-slice_fusion.q_ref, bf16[2,2048,128]{2,1,0:T(8,128)(2,1)S(1)} %get-tuple-element.18.k_ref, ...), custom_call_target="tpu_custom_call" | custom-call | flops 2147483648 | bytes 4194304 | tf_op jit(solution)/shard_map/attend_plane/pallas_call | solution.py:139
  25.9 2.0 %collective-permute-done.4.q_ref = bf16[8,2,128,128]{3,2,1,0:T(8,128)(2,1)S(1)} collective-permute-done((bf16[8,2,128,128]{3,2,1,0:T(8,128)(2,1)S(1)}, bf16[8,2,128,128]{3,2,1,0:T(8,128)(2,1)S(1)}, u32[]{:S(2)}, u32[]{:S(2)}) %collective-permute-start.4) | collective-permute-done | bytes 524320 | tf_op jit(solution)/shard_map/ppermute | solution.py:32
  27.9 6.8 %attend_plane.6 = bf16[8,2,144,128]{3,2,1,0:T(8,128)(2,1)S(1)} custom-call(s32[5]{0:T(128)S(1)} %stack.23.me_ref, s32[1]{0:T(128)S(6)} %copy.17.len_ref, s32[1]{0:T(128)S(6)} %copy.18.start_ref, bf16[8,2,128,128]{3,2,1,0:T(8,128)(2,1)S(1)} %collective-permute-done.4.q_ref, bf16[2,2048,128]{2,1,0:T(8,128)(2,1)S(1)} %get-tuple-element.18.k_ref, ...), custom_call_target="tpu_custom_call" | custom-call | flops 4294967296 | bytes 4194304 | tf_op jit(solution)/shard_map/attend_plane/pallas_call | solution.py:139
  34.7 1.6 %collective-permute-start.7 = (bf16[8,2,144,128]{3,2,1,0:T(8,128)(2,1)S(1)}, bf16[8,2,144,128]{3,2,1,0:T(8,128)(2,1)S(1)}, u32[]{:S(2)}, u32[]{:S(2)}) collective-permute-start(bf16[8,2,144,128]{3,2,1,0:T(8,128)(2,1)S(1)} %attend_plane.6), channel_id=1, source_target_pairs={{0,12},{1,97},{2,14},{3,99},{4,0},{5,101},{6,2},{7,103},{8,4},{9,1... | collective-permute-start | bytes 1769480 | tf_op jit(solution)/shard_map/ppermute | solution.py:32
  37.1 6.7 %attend_plane.7 = bf16[8,2,144,128]{3,2,1,0:T(8,128)(2,1)S(1)} custom-call(s32[5]{0:T(128)S(1)} %stack.23.me_ref, s32[1]{0:T(128)S(6)} %copy.17.len_ref, s32[1]{0:T(128)S(6)} %copy.18.start_ref, bf16[8,2,128,128]{3,2,1,0:T(8,128)(2,1)S(1)} %collective-permute-done.6.q_ref, bf16[2,2048,128]{2,1,0:T(8,128)(2,1)S(1)} %get-tuple-element.18.k_ref, ...), custom_call_target="tpu_custom_call" | custom-call | flops 4294967296 | bytes 4194304 | tf_op jit(solution)/shard_map/attend_plane/pallas_call | solution.py:139
  44.8 2.2 %collective-permute-done.5.q_ref = bf16[8,2,128,128]{3,2,1,0:T(8,128)(2,1)S(1)} collective-permute-done((bf16[8,2,128,128]{3,2,1,0:T(8,128)(2,1)S(1)}, bf16[8,2,128,128]{3,2,1,0:T(8,128)(2,1)S(1)}, u32[]{:S(2)}, u32[]{:S(2)}) %collective-permute-start.5) | collective-permute-done | bytes 524320 | tf_op jit(solution)/shard_map/ppermute | solution.py:32
  47.0 6.8 %attend_plane.8 = bf16[8,2,144,128]{3,2,1,0:T(8,128)(2,1)S(1)} custom-call(s32[5]{0:T(128)S(1)} %stack.23.me_ref, s32[1]{0:T(128)S(6)} %copy.17.len_ref, s32[1]{0:T(128)S(6)} %copy.18.start_ref, bf16[8,2,128,128]{3,2,1,0:T(8,128)(2,1)S(1)} %collective-permute-done.5.q_ref, bf16[2,2048,128]{2,1,0:T(8,128)(2,1)S(1)} %get-tuple-element.18.k_ref, ...), custom_call_target="tpu_custom_call" | custom-call | flops 4294967296 | bytes 4194304 | tf_op jit(solution)/shard_map/attend_plane/pallas_call | solution.py:139
  55.0 3.7 %attend_plane.9.refs_1_ = bf16[4,2,144,128]{3,2,1,0:T(8,128)(2,1)S(1)} custom-call(s32[5]{0:T(128)S(1)} %stack.23.me_ref, s32[1]{0:T(128)S(6)} %copy.17.len_ref, s32[1]{0:T(128)S(6)} %copy.18.start_ref, bf16[8,2,128,128]{3,2,1,0:T(8,128)(2,1)S(1)} %constant_dynamic-update-slice_fusion.q_ref, bf16[2,2048,128]{2,1,0:T(8,128)(2,1)S(1)} %get-tuple-element.18.k_ref, ...), custom_call_target="tpu_custom_call" | custom-call | flops 2147483648 | bytes 4194304 | tf_op jit(solution)/shard_map/attend_plane/pallas_call | solution.py:139
  58.8 6.7 %collective-permute-done.9.refs_4_ = bf16[8,2,144,128]{3,2,1,0:T(8,128)(2,1)S(1)} collective-permute-done((bf16[8,2,144,128]{3,2,1,0:T(8,128)(2,1)S(1)}, bf16[8,2,144,128]{3,2,1,0:T(8,128)(2,1)S(1)}, u32[]{:S(2)}, u32[]{:S(2)}) %collective-permute-start.9) | collective-permute-done | bytes 589856 | tf_op jit(solution)/shard_map/ppermute | solution.py:32
  66.8 2.3 %collective-permute-start.10 = (bf16[2,2,144,128]{3,2,1,0:T(8,128)(2,1)S(1)}, bf16[2,2,144,128]{3,2,1,0:T(8,128)(2,1)S(1)}, u32[]{:S(2)}, u32[]{:S(2)}) collective-permute-start(bf16[2,2,144,128]{3,2,1,0:T(8,128)(2,1)S(1)} %get-tuple-element.29), channel_id=1, source_target_pairs={{0,96},{1,13},{2,98},{3,15},{4,100},{5,1},{6,102},{7,3},{8,104},{9... | collective-permute-start | bytes 442376 | tf_op jit(solution)/shard_map/ppermute | solution.py:32
  69.1 1.6 %collective-permute-start.12 = (bf16[2,2,144,128]{3,2,1,0:T(8,128)(2,1)S(1)}, bf16[2,2,144,128]{3,2,1,0:T(8,128)(2,1)S(1)}, u32[]{:S(2)}, u32[]{:S(2)}) collective-permute-start(bf16[2,2,144,128]{3,2,1,0:T(8,128)(2,1)S(1)} %get-tuple-element.27), channel_id=1, source_target_pairs={{0,64},{1,9},{2,66},{3,11},{4,68},{5,13},{6,70},{7,15},{8,72},{9,1... | collective-permute-start | bytes 442376 | tf_op jit(solution)/shard_map/ppermute | solution.py:32
  72.0 5.0 %collective-permute-done.11.refs_2_ = bf16[2,2,144,128]{3,2,1,0:T(8,128)(2,1)S(1)} collective-permute-done((bf16[2,2,144,128]{3,2,1,0:T(8,128)(2,1)S(1)}, bf16[2,2,144,128]{3,2,1,0:T(8,128)(2,1)S(1)}, u32[]{:S(2)}, u32[]{:S(2)}) %collective-permute-start.11) | collective-permute-done | bytes 147488 | tf_op jit(solution)/shard_map/ppermute | solution.py:32
  77.4 3.3 %collective-permute-start.13 = (bf16[2,2,144,128]{3,2,1,0:T(8,128)(2,1)S(1)}, bf16[2,2,144,128]{3,2,1,0:T(8,128)(2,1)S(1)}, u32[]{:S(2)}, u32[]{:S(2)}) collective-permute-start(bf16[2,2,144,128]{3,2,1,0:T(8,128)(2,1)S(1)} %combine.3.mine), channel_id=1, source_target_pairs={{0,16},{1,17},{2,18},{3,19},{4,20},{5,21},{6,22},{7,23},{8,24},{9,... | collective-permute-start | bytes 442376 | tf_op jit(solution)/shard_map/ppermute | solution.py:32
  80.7 3.5 %collective-permute-done.13.theirs = bf16[2,2,144,128]{3,2,1,0:T(8,128)(2,1)S(1)} collective-permute-done((bf16[2,2,144,128]{3,2,1,0:T(8,128)(2,1)S(1)}, bf16[2,2,144,128]{3,2,1,0:T(8,128)(2,1)S(1)}, u32[]{:S(2)}, u32[]{:S(2)}) %collective-permute-start.13) | collective-permute-done | bytes 147488 | tf_op jit(solution)/shard_map/ppermute | solution.py:32
  84.9 2.5 %collective-permute-start.14 = (bf16[16,4096]{1,0:T(8,128)(2,1)S(1)}, bf16[16,4096]{1,0:T(8,128)(2,1)S(1)}, u32[]{:S(2)}, u32[]{:S(2)}) collective-permute-start(bf16[16,4096]{1,0:T(8,128)(2,1)S(1)} %finish.1.x0), channel_id=1, source_target_pairs={{0,32},{1,5},{2,34},{3,7},{4,36},{5,9},{6,38},{7,11},{8,40},{9,13}... | collective-permute-start | bytes 393224 | tf_op jit(solution)/shard_map/ppermute | solution.py:32
  88.1 3.0 %collective-permute-done.15.x2 = bf16[16,4096]{1,0:T(8,128)(2,1)S(1)} collective-permute-done((bf16[16,4096]{1,0:T(8,128)(2,1)S(1)}, bf16[16,4096]{1,0:T(8,128)(2,1)S(1)}, u32[]{:S(2)}, u32[]{:S(2)}) %collective-permute-start.15) | collective-permute-done | bytes 131104 | tf_op jit(solution)/shard_map/ppermute | solution.py:32
  92.5 5.9 %collective-permute-start.18 = (bf16[64,4096]{1,0:T(8,128)(2,1)S(1)}, bf16[64,4096]{1,0:T(8,128)(2,1)S(1)}, u32[]{:S(2)}, u32[]{:S(2)}) collective-permute-start(bf16[64,4096]{1,0:T(8,128)(2,1)S(1)} %assemble.1.x_ref), channel_id=1, source_target_pairs={{0,4},{1,33},{2,6},{3,35},{4,8},{5,37},{6,10},{7,39},{8,12},{9,41}... | collective-permute-start | bytes 1572872 | tf_op jit(solution)/shard_map/ppermute | solution.py:32
  98.4 2.0 %collective-permute-start.19 = (bf16[64,4096]{1,0:T(8,128)(2,1)S(1)}, bf16[64,4096]{1,0:T(8,128)(2,1)S(1)}, u32[]{:S(2)}, u32[]{:S(2)}) collective-permute-start(bf16[64,4096]{1,0:T(8,128)(2,1)S(1)} %assemble.1.x_ref), channel_id=1, source_target_pairs={{0,12},{1,97},{2,14},{3,99},{4,0},{5,101},{6,2},{7,103},{8,4},{9,1... | collective-permute-start | bytes 1572872 | tf_op jit(solution)/shard_map/ppermute | solution.py:32
  100.4 1.4 %collective-permute-start.20 = (bf16[64,4096]{1,0:T(8,128)(2,1)S(1)}, bf16[64,4096]{1,0:T(8,128)(2,1)S(1)}, u32[]{:S(2)}, u32[]{:S(2)}) collective-permute-start(bf16[64,4096]{1,0:T(8,128)(2,1)S(1)} %assemble.1.x_ref), channel_id=1, source_target_pairs={{0,8},{1,65},{2,10},{3,67},{4,12},{5,69},{6,14},{7,71},{8,0},{9,73... | collective-permute-start | bytes 1572872 | tf_op jit(solution)/shard_map/ppermute | solution.py:32
  102.7 4.8 %collective-permute-done.18.x_ref = bf16[64,4096]{1,0:T(8,128)(2,1)S(1)} collective-permute-done((bf16[64,4096]{1,0:T(8,128)(2,1)S(1)}, bf16[64,4096]{1,0:T(8,128)(2,1)S(1)}, u32[]{:S(2)}, u32[]{:S(2)}) %collective-permute-start.18) | collective-permute-done | bytes 524320 | tf_op jit(solution)/shard_map/ppermute | solution.py:32
  108.3 4.4 %collective-permute-done.19.x_ref = bf16[64,4096]{1,0:T(8,128)(2,1)S(1)} collective-permute-done((bf16[64,4096]{1,0:T(8,128)(2,1)S(1)}, bf16[64,4096]{1,0:T(8,128)(2,1)S(1)}, u32[]{:S(2)}, u32[]{:S(2)}) %collective-permute-start.19) | collective-permute-done | bytes 524320 | tf_op jit(solution)/shard_map/ppermute | solution.py:32
  114.6 1.4 %place.1 = f32[256,512]{1,0:T(8,128)S(1)} custom-call(s32[5]{0:T(128)S(1)} %stack.23.me_ref, f32[64,512]{1,0:T(8,128)S(1)} %project.3.y0, f32[64,512]{1,0:T(8,128)S(1)} %project.4.y1, f32[64,512]{1,0:T(8,128)S(1)} %project.5.y3, bf16[64,4096]{1,0:T(8,128)(2,1)S(1)} %collective-permute-done.20.x_ref, bf16[4096,512]{1,0:T(8,128)(2,1)S(1)} %copy-done), custom_call_target="tpu_custom_call" | custom-call | tf_op jit(solution)/shard_map/place/pallas_call | solution.py:267
  116.1 1.5 %collective-permute-done.21 = f32[128,512]{1,0:T(8,128)S(1)} collective-permute-done((f32[128,512]{1,0:T(8,128)S(1)}, f32[128,512]{1,0:T(8,128)S(1)}, u32[]{:S(2)}, u32[]{:S(2)}) %collective-permute-start.21) | collective-permute-done | bytes 262176 | tf_op jit(solution)/shard_map/ppermute | solution.py:32
  117.7 1.7 %collective-permute-start.22 = (f32[64,512]{1,0:T(8,128)S(1)}, f32[64,512]{1,0:T(8,128)S(1)}, u32[]{:S(2)}, u32[]{:S(2)}) collective-permute-start(f32[64,512]{1,0:T(8,128)S(1)} %slice.39), channel_id=1, source_target_pairs={{0,2},{1,3},{2,0},{3,1},{4,6},{5,7},{6,4},{7,5},{8,10},{9,11},{10,... | collective-permute-start | bytes 393224 | tf_op jit(solution)/shard_map/ppermute | solution.py:32
  119.4 3.9 %collective-permute-done.22 = f32[64,512]{1,0:T(8,128)S(1)} collective-permute-done((f32[64,512]{1,0:T(8,128)S(1)}, f32[64,512]{1,0:T(8,128)S(1)}, u32[]{:S(2)}, u32[]{:S(2)}) %collective-permute-start.22) | collective-permute-done | bytes 131104 | tf_op jit(solution)/shard_map/ppermute | solution.py:32
  (42 shorter events, 16.8 us)
Async XLA Ops:
  0.9 5.8 %collective-permute-start = (bf16[1,2,128,128]{3,2,1,0:T(8,128)(2,1)S(1)}, bf16[1,2,128,128]{3,2,1,0:T(8,128)(2,1)S(1)}, u32[]{:S(2)}, u32[]{:S(2)}) collective-permute-start(bf16[1,2,128,128]{3,2,1,0:T(8,128)(2,1)S(1)} %bitcast.15), channel_id=1, source_target_pairs={{0,16},{1,17},{2,18},{3,19},{4,20},{5,21},{6,22},{7,23},{8,24},{9,... | collective-permute-start | bytes 196616 | tf_op jit(solution)/shard_map/ppermute | solution.py:32
  6.7 7.1 %collective-permute-start.1 = (bf16[2,2,128,128]{3,2,1,0:T(8,128)(2,1)S(1)}, bf16[2,2,128,128]{3,2,1,0:T(8,128)(2,1)S(1)}, u32[]{:S(2)}, u32[]{:S(2)}) collective-permute-start(bf16[2,2,128,128]{3,2,1,0:T(8,128)(2,1)S(1)} %pad_maximum_fusion), channel_id=1, source_target_pairs={{0,32},{1,5},{2,34},{3,7},{4,36},{5,9},{6,38},{7,11},{8,40},{9,13}... | collective-permute-start | bytes 393224 | tf_op jit(solution)/shard_map/ppermute | solution.py:32
  8.8 7.9 %collective-permute-start.2 = (bf16[2,2,128,128]{3,2,1,0:T(8,128)(2,1)S(1)}, bf16[2,2,128,128]{3,2,1,0:T(8,128)(2,1)S(1)}, u32[]{:S(2)}, u32[]{:S(2)}) collective-permute-start(bf16[2,2,128,128]{3,2,1,0:T(8,128)(2,1)S(1)} %pad_maximum_fusion), channel_id=1, source_target_pairs={{0,64},{1,9},{2,66},{3,11},{4,68},{5,13},{6,70},{7,15},{8,72},{9,1... | collective-permute-start | bytes 393224 | tf_op jit(solution)/shard_map/ppermute | solution.py:32
  12.4 5.0 %collective-permute-start.3 = (bf16[2,2,128,128]{3,2,1,0:T(8,128)(2,1)S(1)}, bf16[2,2,128,128]{3,2,1,0:T(8,128)(2,1)S(1)}, u32[]{:S(2)}, u32[]{:S(2)}) collective-permute-start(bf16[2,2,128,128]{3,2,1,0:T(8,128)(2,1)S(1)} %pad_maximum_fusion), channel_id=1, source_target_pairs={{0,96},{1,13},{2,98},{3,15},{4,100},{5,1},{6,102},{7,3},{8,104},{9... | collective-permute-start | bytes 393224 | tf_op jit(solution)/shard_map/ppermute | solution.py:32
  17.5 10.5 %collective-permute-start.4 = (bf16[8,2,128,128]{3,2,1,0:T(8,128)(2,1)S(1)}, bf16[8,2,128,128]{3,2,1,0:T(8,128)(2,1)S(1)}, u32[]{:S(2)}, u32[]{:S(2)}) collective-permute-start(bf16[8,2,128,128]{3,2,1,0:T(8,128)(2,1)S(1)} %constant_dynamic-update-slice_fusion.q_ref), channel_id=1, source_target_pairs={{0,4},{1,33},{2,6},{3,35},{4,8},{5,37},{6,10},{7,39},{8,12},{9,41}... | collective-permute-start | bytes 1572872 | tf_op jit(solution)/shard_map/ppermute | solution.py:32
  20.3 16.8 %collective-permute-start.6 = (bf16[8,2,128,128]{3,2,1,0:T(8,128)(2,1)S(1)}, bf16[8,2,128,128]{3,2,1,0:T(8,128)(2,1)S(1)}, u32[]{:S(2)}, u32[]{:S(2)}) collective-permute-start(bf16[8,2,128,128]{3,2,1,0:T(8,128)(2,1)S(1)} %constant_dynamic-update-slice_fusion.q_ref), channel_id=1, source_target_pairs={{0,12},{1,97},{2,14},{3,99},{4,0},{5,101},{6,2},{7,103},{8,4},{9,1... | collective-permute-start | bytes 1572872 | tf_op jit(solution)/shard_map/ppermute | solution.py:32
  34.7 12.3 %collective-permute-start.7 = (bf16[8,2,144,128]{3,2,1,0:T(8,128)(2,1)S(1)}, bf16[8,2,144,128]{3,2,1,0:T(8,128)(2,1)S(1)}, u32[]{:S(2)}, u32[]{:S(2)}) collective-permute-start(bf16[8,2,144,128]{3,2,1,0:T(8,128)(2,1)S(1)} %attend_plane.6), channel_id=1, source_target_pairs={{0,12},{1,97},{2,14},{3,99},{4,0},{5,101},{6,2},{7,103},{8,4},{9,1... | collective-permute-start | bytes 1769480 | tf_op jit(solution)/shard_map/ppermute | solution.py:32
  36.3 10.7 %collective-permute-start.5 = (bf16[8,2,128,128]{3,2,1,0:T(8,128)(2,1)S(1)}, bf16[8,2,128,128]{3,2,1,0:T(8,128)(2,1)S(1)}, u32[]{:S(2)}, u32[]{:S(2)}) collective-permute-start(bf16[8,2,128,128]{3,2,1,0:T(8,128)(2,1)S(1)} %constant_dynamic-update-slice_fusion.q_ref), channel_id=1, source_target_pairs={{0,8},{1,65},{2,10},{3,67},{4,12},{5,69},{6,14},{7,71},{8,0},{9,73... | collective-permute-start | bytes 1572872 | tf_op jit(solution)/shard_map/ppermute | solution.py:32
  43.9 11.2 %collective-permute-start.8 = (bf16[8,2,144,128]{3,2,1,0:T(8,128)(2,1)S(1)}, bf16[8,2,144,128]{3,2,1,0:T(8,128)(2,1)S(1)}, u32[]{:S(2)}, u32[]{:S(2)}) collective-permute-start(bf16[8,2,144,128]{3,2,1,0:T(8,128)(2,1)S(1)} %attend_plane.7), channel_id=1, source_target_pairs={{0,4},{1,33},{2,6},{3,35},{4,8},{5,37},{6,10},{7,39},{8,12},{9,41}... | collective-permute-start | bytes 1769480 | tf_op jit(solution)/shard_map/ppermute | solution.py:32
  53.8 11.7 %collective-permute-start.9 = (bf16[8,2,144,128]{3,2,1,0:T(8,128)(2,1)S(1)}, bf16[8,2,144,128]{3,2,1,0:T(8,128)(2,1)S(1)}, u32[]{:S(2)}, u32[]{:S(2)}) collective-permute-start(bf16[8,2,144,128]{3,2,1,0:T(8,128)(2,1)S(1)} %attend_plane.8), channel_id=1, source_target_pairs={{0,8},{1,65},{2,10},{3,67},{4,12},{5,69},{6,14},{7,71},{8,0},{9,73... | collective-permute-start | bytes 1769480 | tf_op jit(solution)/shard_map/ppermute | solution.py:32
  58.8 43.0 %copy-start = (bf16[4096,512]{1,0:T(8,128)(2,1)S(1)}, bf16[4096,512]{1,0:T(8,128)(2,1)}, u32[]{:S(2)}) copy-start(bf16[4096,512]{1,0:T(8,128)(2,1)} %w_ref.7) | copy-start | bytes 12582916
  66.8 5.2 %collective-permute-start.10 = (bf16[2,2,144,128]{3,2,1,0:T(8,128)(2,1)S(1)}, bf16[2,2,144,128]{3,2,1,0:T(8,128)(2,1)S(1)}, u32[]{:S(2)}, u32[]{:S(2)}) collective-permute-start(bf16[2,2,144,128]{3,2,1,0:T(8,128)(2,1)S(1)} %get-tuple-element.29), channel_id=1, source_target_pairs={{0,96},{1,13},{2,98},{3,15},{4,100},{5,1},{6,102},{7,3},{8,104},{9... | collective-permute-start | bytes 442376 | tf_op jit(solution)/shard_map/ppermute | solution.py:32
  69.1 7.9 %collective-permute-start.11 = (bf16[2,2,144,128]{3,2,1,0:T(8,128)(2,1)S(1)}, bf16[2,2,144,128]{3,2,1,0:T(8,128)(2,1)S(1)}, u32[]{:S(2)}, u32[]{:S(2)}) collective-permute-start(bf16[2,2,144,128]{3,2,1,0:T(8,128)(2,1)S(1)} %get-tuple-element.28), channel_id=1, source_target_pairs={{0,32},{1,5},{2,34},{3,7},{4,36},{5,9},{6,38},{7,11},{8,40},{9,13}... | collective-permute-start | bytes 442376 | tf_op jit(solution)/shard_map/ppermute | solution.py:32
  69.1 7.9 %collective-permute-start.12 = (bf16[2,2,144,128]{3,2,1,0:T(8,128)(2,1)S(1)}, bf16[2,2,144,128]{3,2,1,0:T(8,128)(2,1)S(1)}, u32[]{:S(2)}, u32[]{:S(2)}) collective-permute-start(bf16[2,2,144,128]{3,2,1,0:T(8,128)(2,1)S(1)} %get-tuple-element.27), channel_id=1, source_target_pairs={{0,64},{1,9},{2,66},{3,11},{4,68},{5,13},{6,70},{7,15},{8,72},{9,1... | collective-permute-start | bytes 442376 | tf_op jit(solution)/shard_map/ppermute | solution.py:32
  77.4 6.7 %collective-permute-start.13 = (bf16[2,2,144,128]{3,2,1,0:T(8,128)(2,1)S(1)}, bf16[2,2,144,128]{3,2,1,0:T(8,128)(2,1)S(1)}, u32[]{:S(2)}, u32[]{:S(2)}) collective-permute-start(bf16[2,2,144,128]{3,2,1,0:T(8,128)(2,1)S(1)} %combine.3.mine), channel_id=1, source_target_pairs={{0,16},{1,17},{2,18},{3,19},{4,20},{5,21},{6,22},{7,23},{8,24},{9,... | collective-permute-start | bytes 442376 | tf_op jit(solution)/shard_map/ppermute | solution.py:32
  84.5 6.7 %collective-permute-start.15 = (bf16[16,4096]{1,0:T(8,128)(2,1)S(1)}, bf16[16,4096]{1,0:T(8,128)(2,1)S(1)}, u32[]{:S(2)}, u32[]{:S(2)}) collective-permute-start(bf16[16,4096]{1,0:T(8,128)(2,1)S(1)} %finish.1.x0), channel_id=1, source_target_pairs={{0,64},{1,9},{2,66},{3,11},{4,68},{5,13},{6,70},{7,15},{8,72},{9,1... | collective-permute-start | bytes 393224 | tf_op jit(solution)/shard_map/ppermute | solution.py:32
  84.9 7.5 %collective-permute-start.14 = (bf16[16,4096]{1,0:T(8,128)(2,1)S(1)}, bf16[16,4096]{1,0:T(8,128)(2,1)S(1)}, u32[]{:S(2)}, u32[]{:S(2)}) collective-permute-start(bf16[16,4096]{1,0:T(8,128)(2,1)S(1)} %finish.1.x0), channel_id=1, source_target_pairs={{0,32},{1,5},{2,34},{3,7},{4,36},{5,9},{6,38},{7,11},{8,40},{9,13}... | collective-permute-start | bytes 393224 | tf_op jit(solution)/shard_map/ppermute | solution.py:32
  87.3 5.1 %collective-permute-start.16 = (bf16[16,4096]{1,0:T(8,128)(2,1)S(1)}, bf16[16,4096]{1,0:T(8,128)(2,1)S(1)}, u32[]{:S(2)}, u32[]{:S(2)}) collective-permute-start(bf16[16,4096]{1,0:T(8,128)(2,1)S(1)} %finish.1.x0), channel_id=1, source_target_pairs={{0,96},{1,13},{2,98},{3,15},{4,100},{5,1},{6,102},{7,3},{8,104},{9... | collective-permute-start | bytes 393224 | tf_op jit(solution)/shard_map/ppermute | solution.py:32
  91.1 1.3 %collective-permute-start.17 = (bf16[16,4096]{1,0:T(8,128)(2,1)S(1)}, bf16[16,4096]{1,0:T(8,128)(2,1)S(1)}, u32[]{:S(2)}, u32[]{:S(2)}) collective-permute-start(bf16[16,4096]{1,0:T(8,128)(2,1)S(1)} %collective-permute-done.15.x2), channel_id=1, source_target_pairs={{0,1},{1,0},{2,3},{3,2},{4,5},{5,4},{6,7},{7,6},{8,9},{9,8},{10,11... | collective-permute-start | bytes 393224 | tf_op jit(solution)/shard_map/ppermute | solution.py:32
  92.5 15.0 %collective-permute-start.18 = (bf16[64,4096]{1,0:T(8,128)(2,1)S(1)}, bf16[64,4096]{1,0:T(8,128)(2,1)S(1)}, u32[]{:S(2)}, u32[]{:S(2)}) collective-permute-start(bf16[64,4096]{1,0:T(8,128)(2,1)S(1)} %assemble.1.x_ref), channel_id=1, source_target_pairs={{0,4},{1,33},{2,6},{3,35},{4,8},{5,37},{6,10},{7,39},{8,12},{9,41}... | collective-permute-start | bytes 1572872 | tf_op jit(solution)/shard_map/ppermute | solution.py:32
  98.4 14.4 %collective-permute-start.19 = (bf16[64,4096]{1,0:T(8,128)(2,1)S(1)}, bf16[64,4096]{1,0:T(8,128)(2,1)S(1)}, u32[]{:S(2)}, u32[]{:S(2)}) collective-permute-start(bf16[64,4096]{1,0:T(8,128)(2,1)S(1)} %assemble.1.x_ref), channel_id=1, source_target_pairs={{0,12},{1,97},{2,14},{3,99},{4,0},{5,101},{6,2},{7,103},{8,4},{9,1... | collective-permute-start | bytes 1572872 | tf_op jit(solution)/shard_map/ppermute | solution.py:32
  100.4 14.2 %collective-permute-start.20 = (bf16[64,4096]{1,0:T(8,128)(2,1)S(1)}, bf16[64,4096]{1,0:T(8,128)(2,1)S(1)}, u32[]{:S(2)}, u32[]{:S(2)}) collective-permute-start(bf16[64,4096]{1,0:T(8,128)(2,1)S(1)} %assemble.1.x_ref), channel_id=1, source_target_pairs={{0,8},{1,65},{2,10},{3,67},{4,12},{5,69},{6,14},{7,71},{8,0},{9,73... | collective-permute-start | bytes 1572872 | tf_op jit(solution)/shard_map/ppermute | solution.py:32
  116.0 1.6 %collective-permute-start.21 = (f32[128,512]{1,0:T(8,128)S(1)}, f32[128,512]{1,0:T(8,128)S(1)}, u32[]{:S(2)}, u32[]{:S(2)}) collective-permute-start(f32[128,512]{1,0:T(8,128)S(1)} %slice.37), channel_id=1, source_target_pairs={{0,1},{1,0},{2,3},{3,2},{4,5},{5,4},{6,7},{7,6},{8,9},{9,8},{10,11... | collective-permute-start | bytes 786440 | tf_op jit(solution)/shard_map/ppermute | solution.py:32
  117.7 5.6 %collective-permute-start.22 = (f32[64,512]{1,0:T(8,128)S(1)}, f32[64,512]{1,0:T(8,128)S(1)}, u32[]{:S(2)}, u32[]{:S(2)}) collective-permute-start(f32[64,512]{1,0:T(8,128)S(1)} %slice.39), channel_id=1, source_target_pairs={{0,2},{1,3},{2,0},{3,1},{4,6},{5,7},{6,4},{7,5},{8,10},{9,11},{10,... | collective-permute-start | bytes 393224 | tf_op jit(solution)/shard_map/ppermute | solution.py:32

commit v2 on v1

--- a/solution.py
+++ b/solution.py
@@ -61,26 +61,44 @@
     return jnp.concatenate([m, high, l - high, jnp.zeros((13, 128), jnp.float32)], axis=0).astype(jnp.bfloat16)
 
 
-def attend_kernel(me_ref, len_ref, start_ref, q_ref, k_ref, v_ref, o_ref, vx, kx, *, db, kvs, first, nb, span, tile, scale):
-    step = pl.program_id(0)
-    rows = nb * 128
-
-    @pl.when(step == 0)
-    def _():
-        me = tuple(me_ref[i] for i in range(5))
-        shard = (me[0] * 2 + me[1]) * 4 + me[2]
-        lane = lax.broadcasted_iota(jnp.int32, (1, 128), 1)
+def prepare_kernel(me_ref, len_ref, start_ref, k_ref, *refs, planes):
+    nkv, span = k_ref.shape[:2]
+    me = tuple(me_ref[i] for i in range(5))
+    shard = (me[0] * 2 + me[1]) * 4 + me[2]
+    lane = lax.broadcasted_iota(jnp.int32, (1, 128), 1)
+    slot = lax.broadcasted_iota(jnp.int32, (span, 128), 0)
+    for db, kx in zip(planes, refs[-len(planes) :]):
         z, yh, x = source(me, lane >> 4, db, (lane >> 3) & 1)
         seen = start_ref[0] + z * 64 + yh * 32 + x * 8 + (lane & 7) + 1 - shard * span
         seen = jnp.minimum(seen, len_ref[0])
-        slot = lax.broadcasted_iota(jnp.int32, (span, 128), 0)
         mask = jnp.where((slot >= seen) & (lane < 64), NEG, 0.0).astype(jnp.bfloat16)
-        for i, kv in enumerate(kvs):
-            kx[i, :, :128] = k_ref[kv]
-            kx[i, :, 128:] = mask
-            vx[i, :, :128] = v_ref[kv]
-            vx[i, :, 128:] = jnp.ones((span, 128), jnp.bfloat16)
-
+        for kv in range(nkv):
+            kx[kv, :, :128] = k_ref[kv]
+            kx[kv, :, 128:] = mask
+    if len(refs) > len(planes):
+        v_ref, vx = refs[:2]
+        for kv in range(nkv):
+            vx[kv, :, :128] = v_ref[kv]
+            vx[kv, :, 128:] = jnp.ones((span, 128), jnp.bfloat16)
+
+
+def prepare(me, lengths, start, k, planes, *v):
+    smem, vmem = pl.BlockSpec(memory_space=pltpu.SMEM), pl.BlockSpec(memory_space=pltpu.VMEM)
+    count = len(planes) + len(v)
+    return pl.pallas_call(
+        functools.partial(prepare_kernel, planes=planes),
+        in_specs=[smem, smem, smem, vmem] + [vmem] * len(v),
+        out_specs=[vmem] * count,
+        out_shape=[jax.ShapeDtypeStruct((*k.shape[:2], 256), jnp.bfloat16)] * count,
+        compiler_params=pltpu.CompilerParams(vmem_limit_bytes=4 * MIB),
+        name="prepare",
+    )(me, lengths, start, k, *v)
+
+
+def attend_kernel(q_ref, kx, vx, o_ref, *, kvs, first, nb, tile, scale):
+    step = pl.program_id(0)
+    rows = nb * 128
+    span = vx.shape[1]
     eye = diagonal()
     row = lax.broadcasted_iota(jnp.int32, (rows, 128), 0)
     lane = lax.broadcasted_iota(jnp.int32, (rows, 128), 1)
@@ -89,7 +107,7 @@
     def scores(i, t):
         q = jnp.concatenate([q_ref[:, kvs[i]].reshape(rows, 128), hot], axis=1)
         return lax.dot_general(
-            q, kx[i, pl.ds(t, tile), :], (((1,), (1,)), ((), ())), preferred_element_type=jnp.float32
+            q, kx[kvs[i], pl.ds(t, tile), :], (((1,), (1,)), ((), ())), preferred_element_type=jnp.float32
         )
 
     def point(m):
@@ -109,7 +127,7 @@
         for t in range(0, span, tile):
             s = s0 if t == 0 else scores(i, t)
             p.append(jnp.exp2(s * scale - m).astype(jnp.bfloat16))
-        acc = jnp.dot(jnp.concatenate(p, axis=1), vx[i], preferred_element_type=jnp.float32)
+        acc = jnp.dot(jnp.concatenate(p, axis=1), vx[kvs[i]], preferred_element_type=jnp.float32)
         ok.append(jnp.min(jnp.where(acc[:, 128:] < BIG, 1.0, 0.0)))
         put(i, m, acc)
 
@@ -126,33 +144,32 @@
             def add(n, acc):
                 t = pl.multiple_of(n * tile, tile)
                 p = jnp.exp2(scores(i, t) * scale - m).astype(jnp.bfloat16)
-                return acc + jnp.dot(p, vx[i, pl.ds(t, tile), :], preferred_element_type=jnp.float32)
+                return acc + jnp.dot(p, vx[kvs[i], pl.ds(t, tile), :], preferred_element_type=jnp.float32)
 
             put(i, m, lax.fori_loop(0, span // tile, add, jnp.zeros((rows, 256), jnp.float32)))
 
 
-def attend(me, lengths, start, q, *, k, v, kvs, db, first=0, blocks=8):
-    span = v.shape[1]
+def attend(q, kx, vx, kvs, first=0, blocks=8):
+    span = vx.shape[1]
     nb, tile = 8 // len(kvs), 256
     skip = first // nb
-    smem, vmem = pl.BlockSpec(memory_space=pltpu.SMEM), pl.BlockSpec(memory_space=pltpu.VMEM)
+    vmem = pl.BlockSpec(memory_space=pltpu.VMEM)
     return pl.pallas_call(
         functools.partial(
-            attend_kernel, db=db, kvs=kvs, first=first, nb=nb, span=span, tile=tile, scale=math.log2(math.e) / math.sqrt(128)
+            attend_kernel, kvs=kvs, first=first, nb=nb, tile=tile, scale=math.log2(math.e) / math.sqrt(128)
         ),
         grid=(blocks // nb,),
-        in_specs=[smem, smem, smem, pl.BlockSpec((nb, *q.shape[1:]), lambda i: (skip + i, 0, 0, 0)), vmem, vmem],
+        in_specs=[pl.BlockSpec((nb, *q.shape[1:]), lambda i: (skip + i, 0, 0, 0)), vmem, vmem],
         out_specs=pl.BlockSpec((nb, len(kvs), 144, 128), lambda i: (i, 0, 0, 0)),
         out_shape=jax.ShapeDtypeStruct((blocks, len(kvs), 144, 128), jnp.bfloat16),
-        scratch_shapes=[pltpu.VMEM((len(kvs), span, 256), jnp.bfloat16)] * 2,
-        compiler_params=pltpu.CompilerParams(vmem_limit_bytes=28 * MIB, dimension_semantics=("arbitrary",)),
+        compiler_params=pltpu.CompilerParams(vmem_limit_bytes=20 * MIB, dimension_semantics=("arbitrary",)),
         cost_estimate=pl.CostEstimate(
             flops=8 * blocks * len(kvs) * 128 * span * 128,
             bytes_accessed=4 * MIB,
             transcendentals=blocks * len(kvs) * 128 * span,
         ),
         name="attend_plane",
-    )(me, lengths, start, q, k, v)
+    )(q, kx, vx)
 
 
 def merged(parts, eye):
@@ -281,25 +298,27 @@
     v = values.transpose(1, 0, 2)
     q = queries.reshape(8, nkv, 16, 128).transpose(1, 2, 0, 3).reshape(1, nkv, 128, 128)
     q = jnp.concatenate([q, moved(q, yh=1)], axis=0)
-    q, k, v, me = together(q, k, v, me)
+    vx, kx0 = prepare(me, lengths, start, k, (0,), v)
+    q, vx, kx0 = together(q, vx, kx0)
+    kx1, kx2, kx3 = prepare(me, lengths, start, k, (1, 2, 3))
     q = jnp.concatenate([q] + [moved(q, a=d) for d in (1, 2, 3)], axis=0)
-    q1, q3, q2 = (moved(q, b=d) for d in (1, 3, 2))
+    q, kx1, kx2, kx3 = together(q, kx1, kx2, kx3)
+    q1, q2, q3 = (moved(q, b=d) for d in (1, 2, 3))
 
     kvs = tuple(range(nkv))
-    part = functools.partial(attend, me, lengths, start, k=k, v=v, kvs=kvs)
-    own0 = part(q, db=0, first=0, blocks=4)
+    own0 = attend(q, kx0, vx, kvs, 0, 4)
     q1, own0 = together(q1, own0)
-    p1 = part(q1, db=1)
+    p1 = attend(q1, kx1, vx, kvs)
     r1 = moved(p1, b=-1)
-    q3, p1 = together(q3, p1)
-    p3 = part(q3, db=3)
+    q2, q3, p1 = together(q2, q3, p1)
+    p2 = attend(q2, kx2, vx, kvs)
+    r2 = moved(p2, b=-2)
+    q3, p2, r1 = together(q3, p2, r1)
+    p3 = attend(q3, kx3, vx, kvs)
     r3 = moved(p3, b=-3)
-    q2, p3, r1 = together(q2, p3, r1)
-    p2 = part(q2, db=2)
-    r2 = moved(p2, b=-2)
-    q, p2, r3 = together(q, p2, r3)
-    own1 = part(q, db=0, first=4, blocks=4)
-    c = combine([own0, own1], [r1, r3, r2])
+    q, p3, r2 = together(q, p3, r2)
+    own1 = attend(q, kx0, vx, kvs, 4, 4)
+    c = combine([own0, own1], [r1, r2, r3])
     c = combine([c[:2]], [moved(c[2 * d : 2 * d + 2], a=-d) for d in (1, 3, 2)])
     attn = finish(c, moved(c, yh=1))
     pieces = [moved(attn, a=d) for d in (1, 2, 3)]
@@ -307,7 +326,7 @@
     x1, x3, x2 = (moved(attn, b=d) for d in (1, 3, 2))
     y = place(me, project(attn, out_weight), project(x1, out_weight), project(x3, out_weight), x2, out_weight)
     y = y[:128] + moved(y[128:], core=1)
-    y = y[:64] + moved(y[64:], yl=1)
+    y = y[:64] + moved(y[64:].astype(jnp.bfloat16), yl=1).astype(jnp.float32)
     return y.astype(jnp.bfloat16)
 
 

time: 124 us -> 115 us (0.927)
  starting transfers between devices: 39.9 us -> 33.9 us
  Pallas kernels: 33.6 us -> 30.9 us
    ppermute x23, starting transfers between devices: 39.9 us -> 33.9 us  [moved(): return lax.ppermute(x, ('cp', 'tp'), pairs)]
    pallas_call x5 -> x7, Pallas kernels: 27.8 us -> 25.1 us  [the longest x5 22.3 us: attend(): pl.pallas_call(functools.partial(attend_kernel, kvs=kvs, first=first, nb=...]
  transfers between devices with their start and end apart: 23 -> 23, of which waited for: 18 -> 14; matrix products, arithmetic and copies ran while one was open for 2% -> 2% of each run, Pallas kernels for 24% -> 24%
where the time goes in v2:
time: 115 us
  waiting for transfers between devices  44.9 us (39%)
  starting transfers between devices  33.9 us (29%)
  Pallas kernels  30.9 us (27%)
  local copies, waits for them, and re-layouts  2.84 us (2%)
  between operations  1.57 us (1%)
    ppermute x23, waiting for transfers between devices, moved(): return lax.ppermute(x, ('cp', 'tp'), pairs)  44.9 us
    ppermute x23, starting transfers between devices, moved(): return lax.ppermute(x, ('cp', 'tp'), pairs)  33.9 us
    pallas_call x5, Pallas kernels, attend(): pl.pallas_call(functools.partial(attend_kernel, kvs=kvs, first=first, nb=...  22.3 us
    pallas_call x2, Pallas kernels, prepare(): pl.pallas_call(functools.partial(prepare_kernel, planes=planes), in_specs...  2.72 us
    pallas_call x3, Pallas kernels, project(): pl.pallas_call(project_kernel, in_specs=[vmem, vmem], out_specs=vmem, out...  2.5 us
  transfers between devices with their start and end apart: 23, of which 14 were waited for; matrix products, arithmetic and copies ran while one was open for 2% of the time, Pallas kernels for 24%

profile of v2, /device:TPU:0, one launch (start us, length us, event | category | flops | bytes accessed | tf_op | source)
XLA Modules:
  0.0 114.8 jit_solution(1156389489200645181)
XLA Ops:
  0.9 3.4 %collective-permute-start = (bf16[1,2,128,128]{3,2,1,0:T(8,128)(2,1)S(1)}, bf16[1,2,128,128]{3,2,1,0:T(8,128)(2,1)S(1)}, u32[]{:S(2)}, u32[]{:S(2)}) collective-permute-start(bf16[1,2,128,128]{3,2,1,0:T(8,128)(2,1)S(1)} %bitcast.15), channel_id=1, source_target_pairs={{0,16},{1,17},{2,18},{3,19},{4,20},{5,21},{6,22},{7,23},{8,24},{9,... | collective-permute-start | bytes 196616 | tf_op jit(solution)/shard_map/ppermute | solution.py:32
  4.2 1.8 %copy_bitcast_fusion = (bf16[2,2048,128]{2,1,0:T(8,128)(2,1)S(1)}, bf16[2,2048,128]{2,1,0:T(8,128)(2,1)S(1)}) fusion(bf16[2048,2,128]{2,1,0:T(2,128)(2,1)} %param.8, bf16[2048,2,128]{2,1,0:T(2,128)(2,1)} %param.7), kind=kLoop, calls=%fused_computation | loop fusion | bytes 4194304 | tf_op jit(solution)/shard_map/transpose | solution.py:298
  8.7 2.0 %collective-permute-start.1 = (bf16[2,2,128,128]{3,2,1,0:T(8,128)(2,1)S(1)}, bf16[2,2,128,128]{3,2,1,0:T(8,128)(2,1)S(1)}, u32[]{:S(2)}, u32[]{:S(2)}) collective-permute-start(bf16[2,2,128,128]{3,2,1,0:T(8,128)(2,1)S(1)} %pad_maximum_fusion.1), channel_id=1, source_target_pairs={{0,32},{1,5},{2,34},{3,7},{4,36},{5,9},{6,38},{7,11},{8,40},{9,13}... | collective-permute-start | bytes 393224 | tf_op jit(solution)/shard_map/ppermute | solution.py:32
  10.7 3.6 %collective-permute-start.2 = (bf16[2,2,128,128]{3,2,1,0:T(8,128)(2,1)S(1)}, bf16[2,2,128,128]{3,2,1,0:T(8,128)(2,1)S(1)}, u32[]{:S(2)}, u32[]{:S(2)}) collective-permute-start(bf16[2,2,128,128]{3,2,1,0:T(8,128)(2,1)S(1)} %pad_maximum_fusion.1), channel_id=1, source_target_pairs={{0,64},{1,9},{2,66},{3,11},{4,68},{5,13},{6,70},{7,15},{8,72},{9,1... | collective-permute-start | bytes 393224 | tf_op jit(solution)/shard_map/ppermute | solution.py:32
  15.3 1.5 %prepare.3 = (bf16[2,2048,256]{2,1,0:T(8,128)(2,1)S(1)}, bf16[2,2048,256]{2,1,0:T(8,128)(2,1)S(1)}, bf16[2,2048,256]{2,1,0:T(8,128)(2,1)S(1)}) custom-call(s32[5]{0:T(128)S(1)} %stack.23.me_ref, s32[1]{0:T(128)S(6)} %copy.14.len_ref, s32[1]{0:T(128)S(6)} %copy.15.start_ref, bf16[2,2048,128]{2,1,0:T(8,128)(2,1)S(1)} %get-tuple-element.50.k_ref), custom_call_target="tpu_custom_call" | custom-call | tf_op jit(solution)/shard_map/prepare/pallas_call | solution.py:88
  16.8 1.8 %collective-permute-done.2 = bf16[2,2,128,128]{3,2,1,0:T(8,128)(2,1)S(1)} collective-permute-done((bf16[2,2,128,128]{3,2,1,0:T(8,128)(2,1)S(1)}, bf16[2,2,128,128]{3,2,1,0:T(8,128)(2,1)S(1)}, u32[]{:S(2)}, u32[]{:S(2)}) %collective-permute-start.2) | collective-permute-done | bytes 131104 | tf_op jit(solution)/shard_map/ppermute | solution.py:32
  19.3 1.6 %collective-permute-start.4 = (bf16[8,2,128,128]{3,2,1,0:T(8,128)(2,1)S(1)}, bf16[8,2,128,128]{3,2,1,0:T(8,128)(2,1)S(1)}, u32[]{:S(2)}, u32[]{:S(2)}) collective-permute-start(bf16[8,2,128,128]{3,2,1,0:T(8,128)(2,1)S(1)} %pad_maximum_fusion.q_ref), channel_id=1, source_target_pairs={{0,4},{1,33},{2,6},{3,35},{4,8},{5,37},{6,10},{7,39},{8,12},{9,41}... | collective-permute-start | bytes 1572872 | tf_op jit(solution)/shard_map/ppermute | solution.py:32
  20.9 2.7 %collective-permute-start.5 = (bf16[8,2,128,128]{3,2,1,0:T(8,128)(2,1)S(1)}, bf16[8,2,128,128]{3,2,1,0:T(8,128)(2,1)S(1)}, u32[]{:S(2)}, u32[]{:S(2)}) collective-permute-start(bf16[8,2,128,128]{3,2,1,0:T(8,128)(2,1)S(1)} %pad_maximum_fusion.q_ref), channel_id=1, source_target_pairs={{0,8},{1,65},{2,10},{3,67},{4,12},{5,69},{6,14},{7,71},{8,0},{9,73... | collective-permute-start | bytes 1572872 | tf_op jit(solution)/shard_map/ppermute | solution.py:32
  23.6 1.4 %collective-permute-start.6 = (bf16[8,2,128,128]{3,2,1,0:T(8,128)(2,1)S(1)}, bf16[8,2,128,128]{3,2,1,0:T(8,128)(2,1)S(1)}, u32[]{:S(2)}, u32[]{:S(2)}) collective-permute-start(bf16[8,2,128,128]{3,2,1,0:T(8,128)(2,1)S(1)} %pad_maximum_fusion.q_ref), channel_id=1, source_target_pairs={{0,12},{1,97},{2,14},{3,99},{4,0},{5,101},{6,2},{7,103},{8,4},{9,1... | collective-permute-start | bytes 1572872 | tf_op jit(solution)/shard_map/ppermute | solution.py:32
  25.0 2.9 %attend_plane.5.refs_0_ = bf16[4,2,144,128]{3,2,1,0:T(8,128)(2,1)S(1)} custom-call(bf16[8,2,128,128]{3,2,1,0:T(8,128)(2,1)S(1)} %pad_maximum_fusion.q_ref, bf16[2,2048,256]{2,1,0:T(8,128)(2,1)S(1)} %get-tuple-element.32.kx, bf16[2,2048,256]{2,1,0:T(8,128)(2,1)S(1)} %get-tuple-element.33.vx), custom_call_target="tpu_custom_call" | custom-call | flops 2147483648 | bytes 4194304 | tf_op jit(solution)/shard_map/attend_plane/pallas_call | solution.py:157
  28.0 1.8 %collective-permute-done.4.q_ref = bf16[8,2,128,128]{3,2,1,0:T(8,128)(2,1)S(1)} collective-permute-done((bf16[8,2,128,128]{3,2,1,0:T(8,128)(2,1)S(1)}, bf16[8,2,128,128]{3,2,1,0:T(8,128)(2,1)S(1)}, u32[]{:S(2)}, u32[]{:S(2)}) %collective-permute-start.4) | collective-permute-done | bytes 524320 | tf_op jit(solution)/shard_map/ppermute | solution.py:32
  29.8 5.5 %attend_plane.6 = bf16[8,2,144,128]{3,2,1,0:T(8,128)(2,1)S(1)} custom-call(bf16[8,2,128,128]{3,2,1,0:T(8,128)(2,1)S(1)} %collective-permute-done.4.q_ref, bf16[2,2048,256]{2,1,0:T(8,128)(2,1)S(1)} %get-tuple-element.36.kx, bf16[2,2048,256]{2,1,0:T(8,128)(2,1)S(1)} %get-tuple-element.33.vx), custom_call_target="tpu_custom_call" | custom-call | flops 4294967296 | bytes 4194304 | tf_op jit(solution)/shard_map/attend_plane/pallas_call | solution.py:157
  35.3 1.6 %collective-permute-start.7 = (bf16[8,2,144,128]{3,2,1,0:T(8,128)(2,1)S(1)}, bf16[8,2,144,128]{3,2,1,0:T(8,128)(2,1)S(1)}, u32[]{:S(2)}, u32[]{:S(2)}) collective-permute-start(bf16[8,2,144,128]{3,2,1,0:T(8,128)(2,1)S(1)} %attend_plane.6), channel_id=1, source_target_pairs={{0,12},{1,97},{2,14},{3,99},{4,0},{5,101},{6,2},{7,103},{8,4},{9,1... | collective-permute-start | bytes 1769480 | tf_op jit(solution)/shard_map/ppermute | solution.py:32
  36.9 5.5 %attend_plane.7 = bf16[8,2,144,128]{3,2,1,0:T(8,128)(2,1)S(1)} custom-call(bf16[8,2,128,128]{3,2,1,0:T(8,128)(2,1)S(1)} %collective-permute-done.5.q_ref, bf16[2,2048,256]{2,1,0:T(8,128)(2,1)S(1)} %get-tuple-element.39.kx, bf16[2,2048,256]{2,1,0:T(8,128)(2,1)S(1)} %get-tuple-element.33.vx), custom_call_target="tpu_custom_call" | custom-call | flops 4294967296 | bytes 4194304 | tf_op jit(solution)/shard_map/attend_plane/pallas_call | solution.py:157
  42.5 2.7 %collective-permute-start.8 = (bf16[8,2,144,128]{3,2,1,0:T(8,128)(2,1)S(1)}, bf16[8,2,144,128]{3,2,1,0:T(8,128)(2,1)S(1)}, u32[]{:S(2)}, u32[]{:S(2)}) collective-permute-start(bf16[8,2,144,128]{3,2,1,0:T(8,128)(2,1)S(1)} %attend_plane.7), channel_id=1, source_target_pairs={{0,8},{1,65},{2,10},{3,67},{4,12},{5,69},{6,14},{7,71},{8,0},{9,73... | collective-permute-start | bytes 1769480 | tf_op jit(solution)/shard_map/ppermute | solution.py:32
  45.3 5.5 %attend_plane.8 = bf16[8,2,144,128]{3,2,1,0:T(8,128)(2,1)S(1)} custom-call(bf16[8,2,128,128]{3,2,1,0:T(8,128)(2,1)S(1)} %collective-permute-done.6.q_ref, bf16[2,2048,256]{2,1,0:T(8,128)(2,1)S(1)} %get-tuple-element.41.kx, bf16[2,2048,256]{2,1,0:T(8,128)(2,1)S(1)} %get-tuple-element.33.vx), custom_call_target="tpu_custom_call" | custom-call | flops 4294967296 | bytes 4194304 | tf_op jit(solution)/shard_map/attend_plane/pallas_call | solution.py:157
  51.3 2.9 %collective-permute-done.8.refs_3_ = bf16[8,2,144,128]{3,2,1,0:T(8,128)(2,1)S(1)} collective-permute-done((bf16[8,2,144,128]{3,2,1,0:T(8,128)(2,1)S(1)}, bf16[8,2,144,128]{3,2,1,0:T(8,128)(2,1)S(1)}, u32[]{:S(2)}, u32[]{:S(2)}) %collective-permute-start.8) | collective-permute-done | bytes 589856 | tf_op jit(solution)/shard_map/ppermute | solution.py:32
  54.2 2.8 %attend_plane.9.refs_1_ = bf16[4,2,144,128]{3,2,1,0:T(8,128)(2,1)S(1)} custom-call(bf16[8,2,128,128]{3,2,1,0:T(8,128)(2,1)S(1)} %pad_maximum_fusion.q_ref, bf16[2,2048,256]{2,1,0:T(8,128)(2,1)S(1)} %get-tuple-element.32.kx, bf16[2,2048,256]{2,1,0:T(8,128)(2,1)S(1)} %get-tuple-element.33.vx), custom_call_target="tpu_custom_call" | custom-call | flops 2147483648 | bytes 4194304 | tf_op jit(solution)/shard_map/attend_plane/pallas_call | solution.py:157
  57.0 5.0 %collective-permute-done.9.refs_4_ = bf16[8,2,144,128]{3,2,1,0:T(8,128)(2,1)S(1)} collective-permute-done((bf16[8,2,144,128]{3,2,1,0:T(8,128)(2,1)S(1)}, bf16[8,2,144,128]{3,2,1,0:T(8,128)(2,1)S(1)}, u32[]{:S(2)}, u32[]{:S(2)}) %collective-permute-start.9) | collective-permute-done | bytes 589856 | tf_op jit(solution)/shard_map/ppermute | solution.py:32
  63.3 2.3 %collective-permute-start.10 = (bf16[2,2,144,128]{3,2,1,0:T(8,128)(2,1)S(1)}, bf16[2,2,144,128]{3,2,1,0:T(8,128)(2,1)S(1)}, u32[]{:S(2)}, u32[]{:S(2)}) collective-permute-start(bf16[2,2,144,128]{3,2,1,0:T(8,128)(2,1)S(1)} %get-tuple-element.47), channel_id=1, source_target_pairs={{0,96},{1,13},{2,98},{3,15},{4,100},{5,1},{6,102},{7,3},{8,104},{9... | collective-permute-start | bytes 442376 | tf_op jit(solution)/shard_map/ppermute | solution.py:32
  65.6 1.7 %collective-permute-start.12 = (bf16[2,2,144,128]{3,2,1,0:T(8,128)(2,1)S(1)}, bf16[2,2,144,128]{3,2,1,0:T(8,128)(2,1)S(1)}, u32[]{:S(2)}, u32[]{:S(2)}) collective-permute-start(bf16[2,2,144,128]{3,2,1,0:T(8,128)(2,1)S(1)} %get-tuple-element.45), channel_id=1, source_target_pairs={{0,64},{1,9},{2,66},{3,11},{4,68},{5,13},{6,70},{7,15},{8,72},{9,1... | collective-permute-start | bytes 442376 | tf_op jit(solution)/shard_map/ppermute | solution.py:32
  68.5 5.0 %collective-permute-done.11.refs_2_ = bf16[2,2,144,128]{3,2,1,0:T(8,128)(2,1)S(1)} collective-permute-done((bf16[2,2,144,128]{3,2,1,0:T(8,128)(2,1)S(1)}, bf16[2,2,144,128]{3,2,1,0:T(8,128)(2,1)S(1)}, u32[]{:S(2)}, u32[]{:S(2)}) %collective-permute-start.11) | collective-permute-done | bytes 147488 | tf_op jit(solution)/shard_map/ppermute | solution.py:32
  73.9 1.4 %collective-permute-start.13 = (bf16[2,2,144,128]{3,2,1,0:T(8,128)(2,1)S(1)}, bf16[2,2,144,128]{3,2,1,0:T(8,128)(2,1)S(1)}, u32[]{:S(2)}, u32[]{:S(2)}) collective-permute-start(bf16[2,2,144,128]{3,2,1,0:T(8,128)(2,1)S(1)} %combine.3.mine), channel_id=1, source_target_pairs={{0,16},{1,17},{2,18},{3,19},{4,20},{5,21},{6,22},{7,23},{8,24},{9,... | collective-permute-start | bytes 442376 | tf_op jit(solution)/shard_map/ppermute | solution.py:32
  75.3 5.3 %collective-permute-done.13.theirs = bf16[2,2,144,128]{3,2,1,0:T(8,128)(2,1)S(1)} collective-permute-done((bf16[2,2,144,128]{3,2,1,0:T(8,128)(2,1)S(1)}, bf16[2,2,144,128]{3,2,1,0:T(8,128)(2,1)S(1)}, u32[]{:S(2)}, u32[]{:S(2)}) %collective-permute-start.13) | collective-permute-done | bytes 147488 | tf_op jit(solution)/shard_map/ppermute | solution.py:32
  81.7 2.1 %collective-permute-start.14 = (bf16[16,4096]{1,0:T(8,128)(2,1)S(1)}, bf16[16,4096]{1,0:T(8,128)(2,1)S(1)}, u32[]{:S(2)}, u32[]{:S(2)}) collective-permute-start(bf16[16,4096]{1,0:T(8,128)(2,1)S(1)} %finish.1.x0), channel_id=1, source_target_pairs={{0,32},{1,5},{2,34},{3,7},{4,36},{5,9},{6,38},{7,11},{8,40},{9,13}... | collective-permute-start | bytes 393224 | tf_op jit(solution)/shard_map/ppermute | solution.py:32
  84.9 2.7 %collective-permute-done.15.x2 = bf16[16,4096]{1,0:T(8,128)(2,1)S(1)} collective-permute-done((bf16[16,4096]{1,0:T(8,128)(2,1)S(1)}, bf16[16,4096]{1,0:T(8,128)(2,1)S(1)}, u32[]{:S(2)}, u32[]{:S(2)}) %collective-permute-start.15) | collective-permute-done | bytes 131104 | tf_op jit(solution)/shard_map/ppermute | solution.py:32
  87.6 1.3 %collective-permute-done.14.x1 = bf16[16,4096]{1,0:T(8,128)(2,1)S(1)} collective-permute-done((bf16[16,4096]{1,0:T(8,128)(2,1)S(1)}, bf16[16,4096]{1,0:T(8,128)(2,1)S(1)}, u32[]{:S(2)}, u32[]{:S(2)}) %collective-permute-start.14) | collective-permute-done | bytes 131104 | tf_op jit(solution)/shard_map/ppermute | solution.py:32
  89.1 3.2 %collective-permute-start.19 = (bf16[64,4096]{1,0:T(8,128)(2,1)S(1)}, bf16[64,4096]{1,0:T(8,128)(2,1)S(1)}, u32[]{:S(2)}, u32[]{:S(2)}) collective-permute-start(bf16[64,4096]{1,0:T(8,128)(2,1)S(1)} %assemble.1.x_ref), channel_id=1, source_target_pairs={{0,12},{1,97},{2,14},{3,99},{4,0},{5,101},{6,2},{7,103},{8,4},{9,1... | collective-permute-start | bytes 1572872 | tf_op jit(solution)/shard_map/ppermute | solution.py:32
  93.2 11.9 %collective-permute-done.18.x_ref = bf16[64,4096]{1,0:T(8,128)(2,1)S(1)} collective-permute-done((bf16[64,4096]{1,0:T(8,128)(2,1)S(1)}, bf16[64,4096]{1,0:T(8,128)(2,1)S(1)}, u32[]{:S(2)}, u32[]{:S(2)}) %collective-permute-start.18) | collective-permute-done | bytes 524320 | tf_op jit(solution)/shard_map/ppermute | solution.py:32
  106.8 1.4 %place.1 = f32[256,512]{1,0:T(8,128)S(1)} custom-call(s32[5]{0:T(128)S(1)} %stack.23.me_ref, f32[64,512]{1,0:T(8,128)S(1)} %project.3.y0, f32[64,512]{1,0:T(8,128)S(1)} %project.4.y1, f32[64,512]{1,0:T(8,128)S(1)} %project.5.y3, bf16[64,4096]{1,0:T(8,128)(2,1)S(1)} %collective-permute-done.20.x_ref, bf16[4096,512]{1,0:T(8,128)(2,1)S(1)} %copy-done), custom_call_target="tpu_custom_call" | custom-call | tf_op jit(solution)/shard_map/place/pallas_call | solution.py:284
  108.3 1.5 %collective-permute-done.21 = f32[128,512]{1,0:T(8,128)S(1)} collective-permute-done((f32[128,512]{1,0:T(8,128)S(1)}, f32[128,512]{1,0:T(8,128)S(1)}, u32[]{:S(2)}, u32[]{:S(2)}) %collective-permute-start.21) | collective-permute-done | bytes 262176 | tf_op jit(solution)/shard_map/ppermute | solution.py:32
  110.6 3.6 %collective-permute-done.22 = bf16[64,512]{1,0:T(8,128)(2,1)S(1)} collective-permute-done((bf16[64,512]{1,0:T(8,128)(2,1)S(1)}, bf16[64,512]{1,0:T(8,128)(2,1)S(1)}, u32[]{:S(2)}, u32[]{:S(2)}) %collective-permute-start.22) | collective-permute-done | bytes 65568 | tf_op jit(solution)/shard_map/ppermute | solution.py:32
  (41 shorter events, 13.6 us)
Async XLA Ops:
  0.9 7.8 %collective-permute-start = (bf16[1,2,128,128]{3,2,1,0:T(8,128)(2,1)S(1)}, bf16[1,2,128,128]{3,2,1,0:T(8,128)(2,1)S(1)}, u32[]{:S(2)}, u32[]{:S(2)}) collective-permute-start(bf16[1,2,128,128]{3,2,1,0:T(8,128)(2,1)S(1)} %bitcast.15), channel_id=1, source_target_pairs={{0,16},{1,17},{2,18},{3,19},{4,20},{5,21},{6,22},{7,23},{8,24},{9,... | collective-permute-start | bytes 196616 | tf_op jit(solution)/shard_map/ppermute | solution.py:32
  8.7 8.1 %collective-permute-start.1 = (bf16[2,2,128,128]{3,2,1,0:T(8,128)(2,1)S(1)}, bf16[2,2,128,128]{3,2,1,0:T(8,128)(2,1)S(1)}, u32[]{:S(2)}, u32[]{:S(2)}) collective-permute-start(bf16[2,2,128,128]{3,2,1,0:T(8,128)(2,1)S(1)} %pad_maximum_fusion.1), channel_id=1, source_target_pairs={{0,32},{1,5},{2,34},{3,7},{4,36},{5,9},{6,38},{7,11},{8,40},{9,13}... | collective-permute-start | bytes 393224 | tf_op jit(solution)/shard_map/ppermute | solution.py:32
  10.7 7.9 %collective-permute-start.2 = (bf16[2,2,128,128]{3,2,1,0:T(8,128)(2,1)S(1)}, bf16[2,2,128,128]{3,2,1,0:T(8,128)(2,1)S(1)}, u32[]{:S(2)}, u32[]{:S(2)}) collective-permute-start(bf16[2,2,128,128]{3,2,1,0:T(8,128)(2,1)S(1)} %pad_maximum_fusion.1), channel_id=1, source_target_pairs={{0,64},{1,9},{2,66},{3,11},{4,68},{5,13},{6,70},{7,15},{8,72},{9,1... | collective-permute-start | bytes 393224 | tf_op jit(solution)/shard_map/ppermute | solution.py:32
  14.3 5.0 %collective-permute-start.3 = (bf16[2,2,128,128]{3,2,1,0:T(8,128)(2,1)S(1)}, bf16[2,2,128,128]{3,2,1,0:T(8,128)(2,1)S(1)}, u32[]{:S(2)}, u32[]{:S(2)}) collective-permute-start(bf16[2,2,128,128]{3,2,1,0:T(8,128)(2,1)S(1)} %pad_maximum_fusion.1), channel_id=1, source_target_pairs={{0,96},{1,13},{2,98},{3,15},{4,100},{5,1},{6,102},{7,3},{8,104},{9... | collective-permute-start | bytes 393224 | tf_op jit(solution)/shard_map/ppermute | solution.py:32
  19.3 10.5 %collective-permute-start.4 = (bf16[8,2,128,128]{3,2,1,0:T(8,128)(2,1)S(1)}, bf16[8,2,128,128]{3,2,1,0:T(8,128)(2,1)S(1)}, u32[]{:S(2)}, u32[]{:S(2)}) collective-permute-start(bf16[8,2,128,128]{3,2,1,0:T(8,128)(2,1)S(1)} %pad_maximum_fusion.q_ref), channel_id=1, source_target_pairs={{0,4},{1,33},{2,6},{3,35},{4,8},{5,37},{6,10},{7,39},{8,12},{9,41}... | collective-permute-start | bytes 1572872 | tf_op jit(solution)/shard_map/ppermute | solution.py:32
  20.9 16.1 %collective-permute-start.5 = (bf16[8,2,128,128]{3,2,1,0:T(8,128)(2,1)S(1)}, bf16[8,2,128,128]{3,2,1,0:T(8,128)(2,1)S(1)}, u32[]{:S(2)}, u32[]{:S(2)}) collective-permute-start(bf16[8,2,128,128]{3,2,1,0:T(8,128)(2,1)S(1)} %pad_maximum_fusion.q_ref), channel_id=1, source_target_pairs={{0,8},{1,65},{2,10},{3,67},{4,12},{5,69},{6,14},{7,71},{8,0},{9,73... | collective-permute-start | bytes 1572872 | tf_op jit(solution)/shard_map/ppermute | solution.py:32
  23.6 13.3 %collective-permute-start.6 = (bf16[8,2,128,128]{3,2,1,0:T(8,128)(2,1)S(1)}, bf16[8,2,128,128]{3,2,1,0:T(8,128)(2,1)S(1)}, u32[]{:S(2)}, u32[]{:S(2)}) collective-permute-start(bf16[8,2,128,128]{3,2,1,0:T(8,128)(2,1)S(1)} %pad_maximum_fusion.q_ref), channel_id=1, source_target_pairs={{0,12},{1,97},{2,14},{3,99},{4,0},{5,101},{6,2},{7,103},{8,4},{9,1... | collective-permute-start | bytes 1572872 | tf_op jit(solution)/shard_map/ppermute | solution.py:32
  35.3 10.0 %collective-permute-start.7 = (bf16[8,2,144,128]{3,2,1,0:T(8,128)(2,1)S(1)}, bf16[8,2,144,128]{3,2,1,0:T(8,128)(2,1)S(1)}, u32[]{:S(2)}, u32[]{:S(2)}) collective-permute-start(bf16[8,2,144,128]{3,2,1,0:T(8,128)(2,1)S(1)} %attend_plane.6), channel_id=1, source_target_pairs={{0,12},{1,97},{2,14},{3,99},{4,0},{5,101},{6,2},{7,103},{8,4},{9,1... | collective-permute-start | bytes 1769480 | tf_op jit(solution)/shard_map/ppermute | solution.py:32
  42.5 11.7 %collective-permute-start.8 = (bf16[8,2,144,128]{3,2,1,0:T(8,128)(2,1)S(1)}, bf16[8,2,144,128]{3,2,1,0:T(8,128)(2,1)S(1)}, u32[]{:S(2)}, u32[]{:S(2)}) collective-permute-start(bf16[8,2,144,128]{3,2,1,0:T(8,128)(2,1)S(1)} %attend_plane.7), channel_id=1, source_target_pairs={{0,8},{1,65},{2,10},{3,67},{4,12},{5,69},{6,14},{7,71},{8,0},{9,73... | collective-permute-start | bytes 1769480 | tf_op jit(solution)/shard_map/ppermute | solution.py:32
  50.8 11.2 %collective-permute-start.9 = (bf16[8,2,144,128]{3,2,1,0:T(8,128)(2,1)S(1)}, bf16[8,2,144,128]{3,2,1,0:T(8,128)(2,1)S(1)}, u32[]{:S(2)}, u32[]{:S(2)}) collective-permute-start(bf16[8,2,144,128]{3,2,1,0:T(8,128)(2,1)S(1)} %attend_plane.8), channel_id=1, source_target_pairs={{0,4},{1,33},{2,6},{3,35},{4,8},{5,37},{6,10},{7,39},{8,12},{9,41}... | collective-permute-start | bytes 1769480 | tf_op jit(solution)/shard_map/ppermute | solution.py:32
  62.0 30.3 %copy-start = (bf16[4096,512]{1,0:T(8,128)(2,1)S(1)}, bf16[4096,512]{1,0:T(8,128)(2,1)}, u32[]{:S(2)}) copy-start(bf16[4096,512]{1,0:T(8,128)(2,1)} %w_ref.7) | copy-start | bytes 12582916
  63.3 5.2 %collective-permute-start.10 = (bf16[2,2,144,128]{3,2,1,0:T(8,128)(2,1)S(1)}, bf16[2,2,144,128]{3,2,1,0:T(8,128)(2,1)S(1)}, u32[]{:S(2)}, u32[]{:S(2)}) collective-permute-start(bf16[2,2,144,128]{3,2,1,0:T(8,128)(2,1)S(1)} %get-tuple-element.47), channel_id=1, source_target_pairs={{0,96},{1,13},{2,98},{3,15},{4,100},{5,1},{6,102},{7,3},{8,104},{9... | collective-permute-start | bytes 442376 | tf_op jit(solution)/shard_map/ppermute | solution.py:32
  65.6 7.9 %collective-permute-start.11 = (bf16[2,2,144,128]{3,2,1,0:T(8,128)(2,1)S(1)}, bf16[2,2,144,128]{3,2,1,0:T(8,128)(2,1)S(1)}, u32[]{:S(2)}, u32[]{:S(2)}) collective-permute-start(bf16[2,2,144,128]{3,2,1,0:T(8,128)(2,1)S(1)} %get-tuple-element.46), channel_id=1, source_target_pairs={{0,32},{1,5},{2,34},{3,7},{4,36},{5,9},{6,38},{7,11},{8,40},{9,13}... | collective-permute-start | bytes 442376 | tf_op jit(solution)/shard_map/ppermute | solution.py:32
  65.6 7.9 %collective-permute-start.12 = (bf16[2,2,144,128]{3,2,1,0:T(8,128)(2,1)S(1)}, bf16[2,2,144,128]{3,2,1,0:T(8,128)(2,1)S(1)}, u32[]{:S(2)}, u32[]{:S(2)}) collective-permute-start(bf16[2,2,144,128]{3,2,1,0:T(8,128)(2,1)S(1)} %get-tuple-element.45), channel_id=1, source_target_pairs={{0,64},{1,9},{2,66},{3,11},{4,68},{5,13},{6,70},{7,15},{8,72},{9,1... | collective-permute-start | bytes 442376 | tf_op jit(solution)/shard_map/ppermute | solution.py:32
  73.9 6.7 %collective-permute-start.13 = (bf16[2,2,144,128]{3,2,1,0:T(8,128)(2,1)S(1)}, bf16[2,2,144,128]{3,2,1,0:T(8,128)(2,1)S(1)}, u32[]{:S(2)}, u32[]{:S(2)}) collective-permute-start(bf16[2,2,144,128]{3,2,1,0:T(8,128)(2,1)S(1)} %combine.3.mine), channel_id=1, source_target_pairs={{0,16},{1,17},{2,18},{3,19},{4,20},{5,21},{6,22},{7,23},{8,24},{9,... | collective-permute-start | bytes 442376 | tf_op jit(solution)/shard_map/ppermute | solution.py:32
  81.0 6.7 %collective-permute-start.15 = (bf16[16,4096]{1,0:T(8,128)(2,1)S(1)}, bf16[16,4096]{1,0:T(8,128)(2,1)S(1)}, u32[]{:S(2)}, u32[]{:S(2)}) collective-permute-start(bf16[16,4096]{1,0:T(8,128)(2,1)S(1)} %finish.1.x0), channel_id=1, source_target_pairs={{0,64},{1,9},{2,66},{3,11},{4,68},{5,13},{6,70},{7,15},{8,72},{9,1... | collective-permute-start | bytes 393224 | tf_op jit(solution)/shard_map/ppermute | solution.py:32
  81.7 7.2 %collective-permute-start.14 = (bf16[16,4096]{1,0:T(8,128)(2,1)S(1)}, bf16[16,4096]{1,0:T(8,128)(2,1)S(1)}, u32[]{:S(2)}, u32[]{:S(2)}) collective-permute-start(bf16[16,4096]{1,0:T(8,128)(2,1)S(1)} %finish.1.x0), channel_id=1, source_target_pairs={{0,32},{1,5},{2,34},{3,7},{4,36},{5,9},{6,38},{7,11},{8,40},{9,13}... | collective-permute-start | bytes 393224 | tf_op jit(solution)/shard_map/ppermute | solution.py:32
  83.8 5.1 %collective-permute-start.16 = (bf16[16,4096]{1,0:T(8,128)(2,1)S(1)}, bf16[16,4096]{1,0:T(8,128)(2,1)S(1)}, u32[]{:S(2)}, u32[]{:S(2)}) collective-permute-start(bf16[16,4096]{1,0:T(8,128)(2,1)S(1)} %finish.1.x0), channel_id=1, source_target_pairs={{0,96},{1,13},{2,98},{3,15},{4,100},{5,1},{6,102},{7,3},{8,104},{9... | collective-permute-start | bytes 393224 | tf_op jit(solution)/shard_map/ppermute | solution.py:32
  87.6 1.3 %collective-permute-start.17 = (bf16[16,4096]{1,0:T(8,128)(2,1)S(1)}, bf16[16,4096]{1,0:T(8,128)(2,1)S(1)}, u32[]{:S(2)}, u32[]{:S(2)}) collective-permute-start(bf16[16,4096]{1,0:T(8,128)(2,1)S(1)} %collective-permute-done.15.x2), channel_id=1, source_target_pairs={{0,1},{1,0},{2,3},{3,2},{4,5},{5,4},{6,7},{7,6},{8,9},{9,8},{10,11... | collective-permute-start | bytes 393224 | tf_op jit(solution)/shard_map/ppermute | solution.py:32
  89.0 16.1 %collective-permute-start.18 = (bf16[64,4096]{1,0:T(8,128)(2,1)S(1)}, bf16[64,4096]{1,0:T(8,128)(2,1)S(1)}, u32[]{:S(2)}, u32[]{:S(2)}) collective-permute-start(bf16[64,4096]{1,0:T(8,128)(2,1)S(1)} %assemble.1.x_ref), channel_id=1, source_target_pairs={{0,4},{1,33},{2,6},{3,35},{4,8},{5,37},{6,10},{7,39},{8,12},{9,41}... | collective-permute-start | bytes 1572872 | tf_op jit(solution)/shard_map/ppermute | solution.py:32
  89.1 16.8 %collective-permute-start.19 = (bf16[64,4096]{1,0:T(8,128)(2,1)S(1)}, bf16[64,4096]{1,0:T(8,128)(2,1)S(1)}, u32[]{:S(2)}, u32[]{:S(2)}) collective-permute-start(bf16[64,4096]{1,0:T(8,128)(2,1)S(1)} %assemble.1.x_ref), channel_id=1, source_target_pairs={{0,12},{1,97},{2,14},{3,99},{4,0},{5,101},{6,2},{7,103},{8,4},{9,1... | collective-permute-start | bytes 1572872 | tf_op jit(solution)/shard_map/ppermute | solution.py:32
  92.3 14.5 %collective-permute-start.20 = (bf16[64,4096]{1,0:T(8,128)(2,1)S(1)}, bf16[64,4096]{1,0:T(8,128)(2,1)S(1)}, u32[]{:S(2)}, u32[]{:S(2)}) collective-permute-start(bf16[64,4096]{1,0:T(8,128)(2,1)S(1)} %assemble.1.x_ref), channel_id=1, source_target_pairs={{0,8},{1,65},{2,10},{3,67},{4,12},{5,69},{6,14},{7,71},{8,0},{9,73... | collective-permute-start | bytes 1572872 | tf_op jit(solution)/shard_map/ppermute | solution.py:32
  108.2 1.6 %collective-permute-start.21 = (f32[128,512]{1,0:T(8,128)S(1)}, f32[128,512]{1,0:T(8,128)S(1)}, u32[]{:S(2)}, u32[]{:S(2)}) collective-permute-start(f32[128,512]{1,0:T(8,128)S(1)} %slice.38), channel_id=1, source_target_pairs={{0,1},{1,0},{2,3},{3,2},{4,5},{5,4},{6,7},{7,6},{8,9},{9,8},{10,11... | collective-permute-start | bytes 786440 | tf_op jit(solution)/shard_map/ppermute | solution.py:32
  109.9 4.3 %collective-permute-start.22 = (bf16[64,512]{1,0:T(8,128)(2,1)S(1)}, bf16[64,512]{1,0:T(8,128)(2,1)S(1)}, u32[]{:S(2)}, u32[]{:S(2)}) collective-permute-start(bf16[64,512]{1,0:T(8,128)(2,1)S(1)} %slice.46), channel_id=1, source_target_pairs={{0,2},{1,3},{2,0},{3,1},{4,6},{5,7},{6,4},{7,5},{8,10},{9,11},{10,... | collective-permute-start | bytes 196616 | tf_op jit(solution)/shard_map/ppermute | solution.py:32

commit v3 on v2

--- a/solution.py
+++ b/solution.py
@@ -61,38 +61,37 @@
     return jnp.concatenate([m, high, l - high, jnp.zeros((13, 128), jnp.float32)], axis=0).astype(jnp.bfloat16)
 
 
-def prepare_kernel(me_ref, len_ref, start_ref, k_ref, *refs, planes):
+def prepare_kernel(info, k_ref, v_ref, vx, *masked):
     nkv, span = k_ref.shape[:2]
-    me = tuple(me_ref[i] for i in range(5))
+    me = tuple(info[i] for i in range(5))
+    length, start = info[5], info[6]
     shard = (me[0] * 2 + me[1]) * 4 + me[2]
     lane = lax.broadcasted_iota(jnp.int32, (1, 128), 1)
     slot = lax.broadcasted_iota(jnp.int32, (span, 128), 0)
-    for db, kx in zip(planes, refs[-len(planes) :]):
+    for db, kx in enumerate(masked):
         z, yh, x = source(me, lane >> 4, db, (lane >> 3) & 1)
-        seen = start_ref[0] + z * 64 + yh * 32 + x * 8 + (lane & 7) + 1 - shard * span
-        seen = jnp.minimum(seen, len_ref[0])
+        seen = start + z * 64 + yh * 32 + x * 8 + (lane & 7) + 1 - shard * span
+        seen = jnp.minimum(seen, length)
         mask = jnp.where((slot >= seen) & (lane < 64), NEG, 0.0).astype(jnp.bfloat16)
         for kv in range(nkv):
             kx[kv, :, :128] = k_ref[kv]
             kx[kv, :, 128:] = mask
-    if len(refs) > len(planes):
-        v_ref, vx = refs[:2]
-        for kv in range(nkv):
-            vx[kv, :, :128] = v_ref[kv]
-            vx[kv, :, 128:] = jnp.ones((span, 128), jnp.bfloat16)
-
-
-def prepare(me, lengths, start, k, planes, *v):
-    smem, vmem = pl.BlockSpec(memory_space=pltpu.SMEM), pl.BlockSpec(memory_space=pltpu.VMEM)
-    count = len(planes) + len(v)
-    return pl.pallas_call(
-        functools.partial(prepare_kernel, planes=planes),
-        in_specs=[smem, smem, smem, vmem] + [vmem] * len(v),
+    for kv in range(nkv):
+        vx[kv, :, :128] = v_ref[kv]
+        vx[kv, :, 128:] = jnp.ones((span, 128), jnp.bfloat16)
+
+
+def prepare(info, k, v):
+    vmem = pl.BlockSpec(memory_space=pltpu.VMEM)
+    count = 1 + RING
+    return pl.pallas_call(
+        prepare_kernel,
+        in_specs=[pl.BlockSpec(memory_space=pltpu.SMEM), vmem, vmem],
         out_specs=[vmem] * count,
         out_shape=[jax.ShapeDtypeStruct((*k.shape[:2], 256), jnp.bfloat16)] * count,
         compiler_params=pltpu.CompilerParams(vmem_limit_bytes=4 * MIB),
         name="prepare",
-    )(me, lengths, start, k, *v)
+    )(info, k, v)
 
 
 def attend_kernel(q_ref, kx, vx, o_ref, *, kvs, first, nb, tile, scale):
@@ -102,10 +101,11 @@
     eye = diagonal()
     row = lax.broadcasted_iota(jnp.int32, (rows, 128), 0)
     lane = lax.broadcasted_iota(jnp.int32, (rows, 128), 1)
-    hot = jnp.where(lane == (first + step * nb + (row >> 7)) * 8 + (row & 7), 1.0, 0.0).astype(jnp.bfloat16)
+    hot = jnp.where(lane == (first + step * nb + (row >> 7)) * 8 + ((row >> 4) & 7), 1.0, 0.0).astype(jnp.bfloat16)
 
     def scores(i, t):
-        q = jnp.concatenate([q_ref[:, kvs[i]].reshape(rows, 128), hot], axis=1)
+        heads = q_ref[:, :, kvs[i] * 16 : (kvs[i] + 1) * 16, :].reshape(rows, 128)
+        q = jnp.concatenate([heads, hot], axis=1)
         return lax.dot_general(
             q, kx[kvs[i], pl.ds(t, tile), :], (((1,), (1,)), ((), ())), preferred_element_type=jnp.float32
         )
@@ -206,16 +206,16 @@
     )(*own, *others)
 
 
-def finish_kernel(mine, theirs, o_ref):
+def finish_kernel(mine, theirs, o_ref, rows):
     eye = diagonal()
     for kv in range(mine.shape[1]):
-        attn = []
         for dy in range(2):
             out, _, total = merged([mine[dy, kv], theirs[1 - dy, kv]], eye)
-            attn.append((out * spread(1.0 / total, eye)).astype(jnp.bfloat16))
-        for h in range(16):
-            c = (kv * 16 + h) * 128
-            o_ref[:, c : c + 128] = jnp.concatenate([a[h * 8 : (h + 1) * 8, :] for a in attn], axis=0)
+            rows[kv, dy] = out * spread(1.0 / total, eye)
+    for kv, h in itertools.product(range(mine.shape[1]), range(16)):
+        c = (kv * 16 + h) * 128
+        both = [rows[kv, dy, pl.ds(h, 8, stride=16), :] for dy in range(2)]
+        o_ref[:, c : c + 128] = jnp.concatenate(both, axis=0).astype(jnp.bfloat16)
 
 
 def finish(mine, theirs):
@@ -224,6 +224,7 @@
         finish_kernel,
         in_specs=[vmem, vmem],
         out_specs=vmem,
+        scratch_shapes=[pltpu.VMEM((mine.shape[1], 2, 128, 128), jnp.float32)],
         compiler_params=pltpu.CompilerParams(vmem_limit_bytes=4 * MIB),
         out_shape=jax.ShapeDtypeStruct((16, mine.shape[1] * 2048), jnp.bfloat16),
         name="finish",
@@ -267,10 +268,11 @@
     )(x, w)
 
 
-def place_kernel(me_ref, y0, y1, y3, x_ref, w_ref, o_ref):
-    me = tuple(me_ref[i] for i in range(5))
+def place_kernel(info, y0, y1, y3, xa_ref, xb_ref, w_ref, o_ref):
+    me = tuple(info[i] for i in range(5))
     yl, core = me[3], me[4]
-    y2 = jnp.dot(x_ref[...], w_ref[...], preferred_element_type=jnp.float32)
+    x = jnp.concatenate([xa_ref[...], xb_ref[...]], axis=0)
+    y2 = jnp.dot(x, w_ref[...], preferred_element_type=jnp.float32)
     for db, y in ((0, y0), (1, y1), (2, y2), (3, y3)):
         for da, dy in itertools.product(range(RING), range(2)):
             z, yh, xx = source(me, da, db, dy)
@@ -279,39 +281,44 @@
             o_ref[pl.ds(pl.multiple_of(row, 8), 8), :] = y[at : at + 8, :]
 
 
-def place(me, y0, y1, y3, x, w):
+def place(info, y0, y1, y3, xa, xb, w):
     vmem = pl.BlockSpec(memory_space=pltpu.VMEM)
     return pl.pallas_call(
         place_kernel,
-        in_specs=[pl.BlockSpec(memory_space=pltpu.SMEM)] + [vmem] * 5,
-        out_specs=vmem,
-        out_shape=jax.ShapeDtypeStruct((RING * x.shape[0], w.shape[1]), jnp.float32),
+        in_specs=[pl.BlockSpec(memory_space=pltpu.SMEM)] + [vmem] * 6,
+        out_specs=vmem,
+        out_shape=jax.ShapeDtypeStruct((RING * y0.shape[0], w.shape[1]), jnp.float32),
         compiler_params=pltpu.CompilerParams(vmem_limit_bytes=8 * MIB),
         name="place",
-    )(me, y0, y1, y3, x, w)
+    )(info, y0, y1, y3, xa, xb, w)
 
 
 def on_device(queries, keys, values, lengths, start, out_weight):
     nkv = keys.shape[1]
-    me = jnp.stack(coords(lax.axis_index("cp"), lax.axis_index("tp"))).astype(jnp.int32)
+    me = coords(lax.axis_index("cp"), lax.axis_index("tp"))
+    info = jnp.concatenate([jnp.stack(me).astype(jnp.int32), lengths, start])
     k = keys.transpose(1, 0, 2)
     v = values.transpose(1, 0, 2)
-    q = queries.reshape(8, nkv, 16, 128).transpose(1, 2, 0, 3).reshape(1, nkv, 128, 128)
+    q = queries[None]
     q = jnp.concatenate([q, moved(q, yh=1)], axis=0)
-    vx, kx0 = prepare(me, lengths, start, k, (0,), v)
-    q, vx, kx0 = together(q, vx, kx0)
-    kx1, kx2, kx3 = prepare(me, lengths, start, k, (1, 2, 3))
+    q, k, v, info = together(q, k, v, info)
+    vx, kx0, kx1, kx2, kx3 = prepare(info, k, v)
     q = jnp.concatenate([q] + [moved(q, a=d) for d in (1, 2, 3)], axis=0)
-    q, kx1, kx2, kx3 = together(q, kx1, kx2, kx3)
-    q1, q2, q3 = (moved(q, b=d) for d in (1, 2, 3))
-
+    q, vx, kx0, kx1, kx2, kx3 = together(q, vx, kx0, kx1, kx2, kx3)
+
+    def neighbours(x):
+        x1, x3 = moved(x, b=1), moved(x, b=3)
+        half = x.shape[0] // 2
+        return x1, x3, moved(x1[:half], b=1), moved(x3[half:], b=3)
+
+    q1, q3, q2a, q2b = neighbours(q)
     kvs = tuple(range(nkv))
     own0 = attend(q, kx0, vx, kvs, 0, 4)
     q1, own0 = together(q1, own0)
     p1 = attend(q1, kx1, vx, kvs)
     r1 = moved(p1, b=-1)
-    q2, q3, p1 = together(q2, q3, p1)
-    p2 = attend(q2, kx2, vx, kvs)
+    q2a, q2b, p1 = together(q2a, q2b, p1)
+    p2 = attend(jnp.concatenate([q2a, q2b], axis=0), kx2, vx, kvs)
     r2 = moved(p2, b=-2)
     q3, p2, r1 = together(q3, p2, r1)
     p3 = attend(q3, kx3, vx, kvs)
@@ -323,8 +330,8 @@
     attn = finish(c, moved(c, yh=1))
     pieces = [moved(attn, a=d) for d in (1, 2, 3)]
     attn = assemble(attn, *pieces, moved(pieces[1], core=1))
-    x1, x3, x2 = (moved(attn, b=d) for d in (1, 3, 2))
-    y = place(me, project(attn, out_weight), project(x1, out_weight), project(x3, out_weight), x2, out_weight)
+    x1, x3, x2a, x2b = neighbours(attn)
+    y = place(info, project(attn, out_weight), project(x1, out_weight), project(x3, out_weight), x2a, x2b, out_weight)
     y = y[:128] + moved(y[128:], core=1)
     y = y[:64] + moved(y[64:].astype(jnp.bfloat16), yl=1).astype(jnp.float32)
     return y.astype(jnp.bfloat16)

time: 115 us -> 117 us (1.017)
  starting transfers between devices: 33.9 us -> 37.3 us
    ppermute x23 -> x25, starting transfers between devices: 33.9 us -> 37.3 us  [moved(): return lax.ppermute(x, ('cp', 'tp'), pairs)]
    pallas_call x3 -> x2, Pallas kernels: 3.01 us -> 2.48 us  [the longest x1 2.16 us: prepare(): pl.pallas_call(prepare_kernel, in_specs=[pl.BlockSpec(memory_space=pltpu....]
    ppermute x23 -> x25, waiting for transfers between devices: 44.9 us -> 44.8 us  [moved(): return lax.ppermute(x, ('cp', 'tp'), pairs)]
  transfers between devices with their start and end apart: 23 -> 25, of which waited for: 14 -> 15; matrix products, arithmetic and copies ran while one was open for 2% -> 2% of each run, Pallas kernels for 24% -> 23%
where the time goes in v3:
time: 117 us
  waiting for transfers between devices  44.8 us (38%)
  starting transfers between devices  37.3 us (32%)
  Pallas kernels  30.2 us (26%)
  local copies, waits for them, and re-layouts  2.05 us (2%)
  between operations  1.6 us (1%)
    ppermute x25, waiting for transfers between devices, moved(): return lax.ppermute(x, ('cp', 'tp'), pairs)  44.8 us
    ppermute x25, starting transfers between devices, moved(): return lax.ppermute(x, ('cp', 'tp'), pairs)  37.3 us
    pallas_call x5, Pallas kernels, attend(): pl.pallas_call(functools.partial(attend_kernel, kvs=kvs, first=first, nb=...  22.2 us
    pallas_call x3, Pallas kernels, project(): pl.pallas_call(project_kernel, in_specs=[vmem, vmem], out_specs=vmem, out...  2.5 us
  transfers between devices with their start and end apart: 25, of which 15 were waited for; matrix products, arithmetic and copies ran while one was open for 2% of the time, Pallas kernels for 23%

profile of v3, /device:TPU:0, one launch (start us, length us, event | category | flops | bytes accessed | tf_op | source)
XLA Modules:
  0.0 116.7 jit_solution(15833060785234178151)
XLA Ops:
  0.0 3.3 %collective-permute-start = (bf16[1,8,32,128]{3,2,1,0:T(8,128)(2,1)}, bf16[1,8,32,128]{3,2,1,0:T(8,128)(2,1)S(1)}, u32[]{:S(2)}, u32[]{:S(2)}) collective-permute-start(bf16[1,8,32,128]{3,2,1,0:T(8,128)(2,1)} %bitcast.10), channel_id=1, source_target_pairs={{0,16},{1,17},{2,18},{3,19},{4,20},{5,21},{6,22},{7,23},{8,24},{9,... | collective-permute-start | bytes 196616 | tf_op jit(solution)/shard_map/ppermute | solution.py:32
  3.3 1.8 %copy_bitcast_fusion = (bf16[2,2048,128]{2,1,0:T(8,128)(2,1)S(1)}, bf16[2,2048,128]{2,1,0:T(8,128)(2,1)S(1)}) fusion(bf16[2048,2,128]{2,1,0:T(2,128)(2,1)} %param.8, bf16[2048,2,128]{2,1,0:T(2,128)(2,1)} %param.7), kind=kLoop, calls=%fused_computation | loop fusion | bytes 4194304 | tf_op jit(solution)/shard_map/transpose | solution.py:301
  6.6 2.0 %collective-permute-start.1 = (bf16[2,8,32,128]{3,2,1,0:T(8,128)(2,1)S(1)}, bf16[2,8,32,128]{3,2,1,0:T(8,128)(2,1)S(1)}, u32[]{:S(2)}, u32[]{:S(2)}) collective-permute-start(bf16[2,8,32,128]{3,2,1,0:T(8,128)(2,1)S(1)} %pad_maximum_fusion.2), channel_id=1, source_target_pairs={{0,32},{1,5},{2,34},{3,7},{4,36},{5,9},{6,38},{7,11},{8,40},{9,13}... | collective-permute-start | bytes 393224 | tf_op jit(solution)/shard_map/ppermute | solution.py:32
  8.5 3.6 %collective-permute-start.2 = (bf16[2,8,32,128]{3,2,1,0:T(8,128)(2,1)S(1)}, bf16[2,8,32,128]{3,2,1,0:T(8,128)(2,1)S(1)}, u32[]{:S(2)}, u32[]{:S(2)}) collective-permute-start(bf16[2,8,32,128]{3,2,1,0:T(8,128)(2,1)S(1)} %pad_maximum_fusion.2), channel_id=1, source_target_pairs={{0,64},{1,9},{2,66},{3,11},{4,68},{5,13},{6,70},{7,15},{8,72},{9,1... | collective-permute-start | bytes 393224 | tf_op jit(solution)/shard_map/ppermute | solution.py:32
  13.1 2.2 %prepare.1 = (bf16[2,2048,256]{2,1,0:T(8,128)(2,1)S(1)}, bf16[2,2048,256]{2,1,0:T(8,128)(2,1)S(1)}, bf16[2,2048,256]{2,1,0:T(8,128)(2,1)S(1)}, bf16[2,2048,256]{...) custom-call(s32[7]{0:T(128)S(1)} %concatenate.13.info, bf16[2,2048,128]{2,1,0:T(8,128)(2,1)S(1)} %get-tuple-element.30.k_ref, ...), custom_call_target="tpu_custom_call" | custom-call | tf_op jit(solution)/shard_map/prepare/pallas_call | solution.py:87
  17.2 1.6 %collective-permute-start.4 = (bf16[8,8,32,128]{3,2,1,0:T(8,128)(2,1)S(1)}, bf16[8,8,32,128]{3,2,1,0:T(8,128)(2,1)S(1)}, u32[]{:S(2)}, u32[]{:S(2)}) collective-permute-start(bf16[8,8,32,128]{3,2,1,0:T(8,128)(2,1)S(1)} %pad_maximum_fusion.q_ref), channel_id=1, source_target_pairs={{0,4},{1,33},{2,6},{3,35},{4,8},{5,37},{6,10},{7,39},{8,12},{9,41}... | collective-permute-start | bytes 1572872 | tf_op jit(solution)/shard_map/ppermute | solution.py:32
  18.7 1.7 %collective-permute-start.5 = (bf16[8,8,32,128]{3,2,1,0:T(8,128)(2,1)S(1)}, bf16[8,8,32,128]{3,2,1,0:T(8,128)(2,1)S(1)}, u32[]{:S(2)}, u32[]{:S(2)}) collective-permute-start(bf16[8,8,32,128]{3,2,1,0:T(8,128)(2,1)S(1)} %pad_maximum_fusion.q_ref), channel_id=1, source_target_pairs={{0,12},{1,97},{2,14},{3,99},{4,0},{5,101},{6,2},{7,103},{8,4},{9,1... | collective-permute-start | bytes 1572872 | tf_op jit(solution)/shard_map/ppermute | solution.py:32
  20.5 2.8 %attend_plane.5.refs_0_ = bf16[4,2,144,128]{3,2,1,0:T(8,128)(2,1)S(1)} custom-call(bf16[8,8,32,128]{3,2,1,0:T(8,128)(2,1)S(1)} %pad_maximum_fusion.q_ref, bf16[2,2048,256]{2,1,0:T(8,128)(2,1)S(1)} %get-tuple-element.38.kx, bf16[2,2048,256]{2,1,0:T(8,128)(2,1)S(1)} %get-tuple-element.39.vx), custom_call_target="tpu_custom_call" | custom-call | flops 2147483648 | bytes 4194304 | tf_op jit(solution)/shard_map/attend_plane/pallas_call | solution.py:157
  23.2 4.4 %collective-permute-done.4.q_ref = bf16[8,8,32,128]{3,2,1,0:T(8,128)(2,1)S(1)} collective-permute-done((bf16[8,8,32,128]{3,2,1,0:T(8,128)(2,1)S(1)}, bf16[8,8,32,128]{3,2,1,0:T(8,128)(2,1)S(1)}, u32[]{:S(2)}, u32[]{:S(2)}) %collective-permute-start.4) | collective-permute-done | bytes 524320 | tf_op jit(solution)/shard_map/ppermute | solution.py:32
  28.0 3.2 %collective-permute-start.7 = (bf16[4,8,32,128]{3,2,1,0:T(8,128)(2,1)S(1)}, bf16[4,8,32,128]{3,2,1,0:T(8,128)(2,1)S(1)}, u32[]{:S(2)}, u32[]{:S(2)}) collective-permute-start(bf16[4,8,32,128]{3,2,1,0:T(8,128)(2,1)S(1)} %slice.50), channel_id=1, source_target_pairs={{0,12},{1,97},{2,14},{3,99},{4,0},{5,101},{6,2},{7,103},{8,4},{9,1... | collective-permute-start | bytes 786440 | tf_op jit(solution)/shard_map/ppermute | solution.py:32
  31.2 5.5 %attend_plane.6 = bf16[8,2,144,128]{3,2,1,0:T(8,128)(2,1)S(1)} custom-call(bf16[8,8,32,128]{3,2,1,0:T(8,128)(2,1)S(1)} %collective-permute-done.4.q_ref, bf16[2,2048,256]{2,1,0:T(8,128)(2,1)S(1)} %get-tuple-element.42.kx, bf16[2,2048,256]{2,1,0:T(8,128)(2,1)S(1)} %get-tuple-element.39.vx), custom_call_target="tpu_custom_call" | custom-call | flops 4294967296 | bytes 4194304 | tf_op jit(solution)/shard_map/attend_plane/pallas_call | solution.py:157
  37.3 5.6 %attend_plane.7 = bf16[8,2,144,128]{3,2,1,0:T(8,128)(2,1)S(1)} custom-call(bf16[8,8,32,128]{3,2,1,0:T(8,128)(2,1)S(1)} %pad_maximum_fusion.1.q_ref, bf16[2,2048,256]{2,1,0:T(8,128)(2,1)S(1)} %get-tuple-element.45.kx, bf16[2,2048,256]{2,1,0:T(8,128)(2,1)S(1)} %get-tuple-element.39.vx), custom_call_target="tpu_custom_call" | custom-call | flops 4294967296 | bytes 4194304 | tf_op jit(solution)/shard_map/attend_plane/pallas_call | solution.py:157
  43.9 2.8 %collective-permute-done.8.refs_2_ = bf16[8,2,144,128]{3,2,1,0:T(8,128)(2,1)S(1)} collective-permute-done((bf16[8,2,144,128]{3,2,1,0:T(8,128)(2,1)S(1)}, bf16[8,2,144,128]{3,2,1,0:T(8,128)(2,1)S(1)}, u32[]{:S(2)}, u32[]{:S(2)}) %collective-permute-start.8) | collective-permute-done | bytes 589856 | tf_op jit(solution)/shard_map/ppermute | solution.py:32
  46.7 5.5 %attend_plane.8 = bf16[8,2,144,128]{3,2,1,0:T(8,128)(2,1)S(1)} custom-call(bf16[8,8,32,128]{3,2,1,0:T(8,128)(2,1)S(1)} %collective-permute-done.5.q_ref, bf16[2,2048,256]{2,1,0:T(8,128)(2,1)S(1)} %get-tuple-element.47.kx, bf16[2,2048,256]{2,1,0:T(8,128)(2,1)S(1)} %get-tuple-element.39.vx), custom_call_target="tpu_custom_call" | custom-call | flops 4294967296 | bytes 4194304 | tf_op jit(solution)/shard_map/attend_plane/pallas_call | solution.py:157
  52.4 2.1 %collective-permute-done.9.refs_3_ = bf16[8,2,144,128]{3,2,1,0:T(8,128)(2,1)S(1)} collective-permute-done((bf16[8,2,144,128]{3,2,1,0:T(8,128)(2,1)S(1)}, bf16[8,2,144,128]{3,2,1,0:T(8,128)(2,1)S(1)}, u32[]{:S(2)}, u32[]{:S(2)}) %collective-permute-start.9) | collective-permute-done | bytes 589856 | tf_op jit(solution)/shard_map/ppermute | solution.py:32
  54.5 2.8 %attend_plane.9.refs_1_ = bf16[4,2,144,128]{3,2,1,0:T(8,128)(2,1)S(1)} custom-call(bf16[8,8,32,128]{3,2,1,0:T(8,128)(2,1)S(1)} %pad_maximum_fusion.q_ref, bf16[2,2048,256]{2,1,0:T(8,128)(2,1)S(1)} %get-tuple-element.38.kx, bf16[2,2048,256]{2,1,0:T(8,128)(2,1)S(1)} %get-tuple-element.39.vx), custom_call_target="tpu_custom_call" | custom-call | flops 2147483648 | bytes 4194304 | tf_op jit(solution)/shard_map/attend_plane/pallas_call | solution.py:157
  57.3 6.2 %collective-permute-done.10.refs_4_ = bf16[8,2,144,128]{3,2,1,0:T(8,128)(2,1)S(1)} collective-permute-done((bf16[8,2,144,128]{3,2,1,0:T(8,128)(2,1)S(1)}, bf16[8,2,144,128]{3,2,1,0:T(8,128)(2,1)S(1)}, u32[]{:S(2)}, u32[]{:S(2)}) %collective-permute-start.10) | collective-permute-done | bytes 589856 | tf_op jit(solution)/shard_map/ppermute | solution.py:32
  64.8 2.3 %collective-permute-start.11 = (bf16[2,2,144,128]{3,2,1,0:T(8,128)(2,1)S(1)}, bf16[2,2,144,128]{3,2,1,0:T(8,128)(2,1)S(1)}, u32[]{:S(2)}, u32[]{:S(2)}) collective-permute-start(bf16[2,2,144,128]{3,2,1,0:T(8,128)(2,1)S(1)} %get-tuple-element.53), channel_id=1, source_target_pairs={{0,96},{1,13},{2,98},{3,15},{4,100},{5,1},{6,102},{7,3},{8,104},{9... | collective-permute-start | bytes 442376 | tf_op jit(solution)/shard_map/ppermute | solution.py:32
  67.1 1.9 %collective-permute-start.13 = (bf16[2,2,144,128]{3,2,1,0:T(8,128)(2,1)S(1)}, bf16[2,2,144,128]{3,2,1,0:T(8,128)(2,1)S(1)}, u32[]{:S(2)}, u32[]{:S(2)}) collective-permute-start(bf16[2,2,144,128]{3,2,1,0:T(8,128)(2,1)S(1)} %get-tuple-element.51), channel_id=1, source_target_pairs={{0,64},{1,9},{2,66},{3,11},{4,68},{5,13},{6,70},{7,15},{8,72},{9,1... | collective-permute-start | bytes 442376 | tf_op jit(solution)/shard_map/ppermute | solution.py:32
  70.0 5.0 %collective-permute-done.12.refs_2_ = bf16[2,2,144,128]{3,2,1,0:T(8,128)(2,1)S(1)} collective-permute-done((bf16[2,2,144,128]{3,2,1,0:T(8,128)(2,1)S(1)}, bf16[2,2,144,128]{3,2,1,0:T(8,128)(2,1)S(1)}, u32[]{:S(2)}, u32[]{:S(2)}) %collective-permute-start.12) | collective-permute-done | bytes 147488 | tf_op jit(solution)/shard_map/ppermute | solution.py:32
  75.4 2.9 %collective-permute-start.14 = (bf16[2,2,144,128]{3,2,1,0:T(8,128)(2,1)S(1)}, bf16[2,2,144,128]{3,2,1,0:T(8,128)(2,1)S(1)}, u32[]{:S(2)}, u32[]{:S(2)}) collective-permute-start(bf16[2,2,144,128]{3,2,1,0:T(8,128)(2,1)S(1)} %combine.3.mine), channel_id=1, source_target_pairs={{0,16},{1,17},{2,18},{3,19},{4,20},{5,21},{6,22},{7,23},{8,24},{9,... | collective-permute-start | bytes 442376 | tf_op jit(solution)/shard_map/ppermute | solution.py:32
  78.3 3.8 %collective-permute-done.14.theirs = bf16[2,2,144,128]{3,2,1,0:T(8,128)(2,1)S(1)} collective-permute-done((bf16[2,2,144,128]{3,2,1,0:T(8,128)(2,1)S(1)}, bf16[2,2,144,128]{3,2,1,0:T(8,128)(2,1)S(1)}, u32[]{:S(2)}, u32[]{:S(2)}) %collective-permute-start.14) | collective-permute-done | bytes 147488 | tf_op jit(solution)/shard_map/ppermute | solution.py:32
  83.2 2.2 %collective-permute-start.15 = (bf16[16,4096]{1,0:T(8,128)(2,1)S(1)}, bf16[16,4096]{1,0:T(8,128)(2,1)S(1)}, u32[]{:S(2)}, u32[]{:S(2)}) collective-permute-start(bf16[16,4096]{1,0:T(8,128)(2,1)S(1)} %finish.1.x0), channel_id=1, source_target_pairs={{0,32},{1,5},{2,34},{3,7},{4,36},{5,9},{6,38},{7,11},{8,40},{9,13}... | collective-permute-start | bytes 393224 | tf_op jit(solution)/shard_map/ppermute | solution.py:32
  86.4 2.7 %collective-permute-done.16.x2 = bf16[16,4096]{1,0:T(8,128)(2,1)S(1)} collective-permute-done((bf16[16,4096]{1,0:T(8,128)(2,1)S(1)}, bf16[16,4096]{1,0:T(8,128)(2,1)S(1)}, u32[]{:S(2)}, u32[]{:S(2)}) %collective-permute-start.16) | collective-permute-done | bytes 131104 | tf_op jit(solution)/shard_map/ppermute | solution.py:32
  89.1 1.3 %collective-permute-done.15.x1 = bf16[16,4096]{1,0:T(8,128)(2,1)S(1)} collective-permute-done((bf16[16,4096]{1,0:T(8,128)(2,1)S(1)}, bf16[16,4096]{1,0:T(8,128)(2,1)S(1)}, u32[]{:S(2)}, u32[]{:S(2)}) %collective-permute-start.15) | collective-permute-done | bytes 131104 | tf_op jit(solution)/shard_map/ppermute | solution.py:32
  90.6 3.2 %collective-permute-start.20 = (bf16[64,4096]{1,0:T(8,128)(2,1)S(1)}, bf16[64,4096]{1,0:T(8,128)(2,1)S(1)}, u32[]{:S(2)}, u32[]{:S(2)}) collective-permute-start(bf16[64,4096]{1,0:T(8,128)(2,1)S(1)} %assemble.1.x_ref), channel_id=1, source_target_pairs={{0,12},{1,97},{2,14},{3,99},{4,0},{5,101},{6,2},{7,103},{8,4},{9,1... | collective-permute-start | bytes 1572872 | tf_op jit(solution)/shard_map/ppermute | solution.py:32
  93.8 7.2 %collective-permute-done.19.x_ref = bf16[64,4096]{1,0:T(8,128)(2,1)S(1)} collective-permute-done((bf16[64,4096]{1,0:T(8,128)(2,1)S(1)}, bf16[64,4096]{1,0:T(8,128)(2,1)S(1)}, u32[]{:S(2)}, u32[]{:S(2)}) %collective-permute-start.19) | collective-permute-done | bytes 524320 | tf_op jit(solution)/shard_map/ppermute | solution.py:32
  101.1 3.3 %collective-permute-start.22 = (bf16[32,4096]{1,0:T(8,128)(2,1)S(1)}, bf16[32,4096]{1,0:T(8,128)(2,1)S(1)}, u32[]{:S(2)}, u32[]{:S(2)}) collective-permute-start(bf16[32,4096]{1,0:T(8,128)(2,1)S(1)} %slice.56), channel_id=1, source_target_pairs={{0,12},{1,97},{2,14},{3,99},{4,0},{5,101},{6,2},{7,103},{8,4},{9,1... | collective-permute-start | bytes 786440 | tf_op jit(solution)/shard_map/ppermute | solution.py:32
  106.9 1.7 %collective-permute-done.21.xa_ref = bf16[32,4096]{1,0:T(8,128)(2,1)S(1)} collective-permute-done((bf16[32,4096]{1,0:T(8,128)(2,1)S(1)}, bf16[32,4096]{1,0:T(8,128)(2,1)S(1)}, u32[]{:S(2)}, u32[]{:S(2)}) %collective-permute-start.21) | collective-permute-done | bytes 262176 | tf_op jit(solution)/shard_map/ppermute | solution.py:32
  108.6 1.4 %place.1 = f32[256,512]{1,0:T(8,128)S(1)} custom-call(s32[7]{0:T(128)S(1)} %concatenate.13.info, f32[64,512]{1,0:T(8,128)S(1)} %project.3.y0, f32[64,512]{1,0:T(8,128)S(1)} %project.4.y1, f32[64,512]{1,0:T(8,128)S(1)} %project.5.y3, bf16[32,4096]{1,0:T(8,128)(2,1)S(1)} %collective-permute-done.21.xa_ref, ...), custom_call_target="tpu_custom_call" | custom-call | tf_op jit(solution)/shard_map/place/pallas_call | solution.py:286
  110.1 1.5 %collective-permute-done.23 = f32[128,512]{1,0:T(8,128)S(1)} collective-permute-done((f32[128,512]{1,0:T(8,128)S(1)}, f32[128,512]{1,0:T(8,128)S(1)}, u32[]{:S(2)}, u32[]{:S(2)}) %collective-permute-start.23) | collective-permute-done | bytes 262176 | tf_op jit(solution)/shard_map/ppermute | solution.py:32
  112.9 3.2 %collective-permute-done.24 = bf16[64,512]{1,0:T(8,128)(2,1)S(1)} collective-permute-done((bf16[64,512]{1,0:T(8,128)(2,1)S(1)}, bf16[64,512]{1,0:T(8,128)(2,1)S(1)}, u32[]{:S(2)}, u32[]{:S(2)}) %collective-permute-start.24) | collective-permute-done | bytes 65568 | tf_op jit(solution)/shard_map/ppermute | solution.py:32
  (50 shorter events, 14.5 us)
Async XLA Ops:
  0.0 6.5 %copy-start.1 = (bf16[8,32,128]{2,1,0:T(8,128)(2,1)S(1)}, bf16[8,32,128]{2,1,0:T(8,128)(2,1)}, u32[]{:S(2)}) copy-start(bf16[8,32,128]{2,1,0:T(8,128)(2,1)} %param.6) | copy-start | bytes 196612
  0.0 6.5 %collective-permute-start = (bf16[1,8,32,128]{3,2,1,0:T(8,128)(2,1)}, bf16[1,8,32,128]{3,2,1,0:T(8,128)(2,1)S(1)}, u32[]{:S(2)}, u32[]{:S(2)}) collective-permute-start(bf16[1,8,32,128]{3,2,1,0:T(8,128)(2,1)} %bitcast.10), channel_id=1, source_target_pairs={{0,16},{1,17},{2,18},{3,19},{4,20},{5,21},{6,22},{7,23},{8,24},{9,... | collective-permute-start | bytes 196616 | tf_op jit(solution)/shard_map/ppermute | solution.py:32
  6.6 8.7 %collective-permute-start.1 = (bf16[2,8,32,128]{3,2,1,0:T(8,128)(2,1)S(1)}, bf16[2,8,32,128]{3,2,1,0:T(8,128)(2,1)S(1)}, u32[]{:S(2)}, u32[]{:S(2)}) collective-permute-start(bf16[2,8,32,128]{3,2,1,0:T(8,128)(2,1)S(1)} %pad_maximum_fusion.2), channel_id=1, source_target_pairs={{0,32},{1,5},{2,34},{3,7},{4,36},{5,9},{6,38},{7,11},{8,40},{9,13}... | collective-permute-start | bytes 393224 | tf_op jit(solution)/shard_map/ppermute | solution.py:32
  8.5 7.9 %collective-permute-start.2 = (bf16[2,8,32,128]{3,2,1,0:T(8,128)(2,1)S(1)}, bf16[2,8,32,128]{3,2,1,0:T(8,128)(2,1)S(1)}, u32[]{:S(2)}, u32[]{:S(2)}) collective-permute-start(bf16[2,8,32,128]{3,2,1,0:T(8,128)(2,1)S(1)} %pad_maximum_fusion.2), channel_id=1, source_target_pairs={{0,64},{1,9},{2,66},{3,11},{4,68},{5,13},{6,70},{7,15},{8,72},{9,1... | collective-permute-start | bytes 393224 | tf_op jit(solution)/shard_map/ppermute | solution.py:32
  12.1 5.0 %collective-permute-start.3 = (bf16[2,8,32,128]{3,2,1,0:T(8,128)(2,1)S(1)}, bf16[2,8,32,128]{3,2,1,0:T(8,128)(2,1)S(1)}, u32[]{:S(2)}, u32[]{:S(2)}) collective-permute-start(bf16[2,8,32,128]{3,2,1,0:T(8,128)(2,1)S(1)} %pad_maximum_fusion.2), channel_id=1, source_target_pairs={{0,96},{1,13},{2,98},{3,15},{4,100},{5,1},{6,102},{7,3},{8,104},{9... | collective-permute-start | bytes 393224 | tf_op jit(solution)/shard_map/ppermute | solution.py:32
  17.2 10.5 %collective-permute-start.4 = (bf16[8,8,32,128]{3,2,1,0:T(8,128)(2,1)S(1)}, bf16[8,8,32,128]{3,2,1,0:T(8,128)(2,1)S(1)}, u32[]{:S(2)}, u32[]{:S(2)}) collective-permute-start(bf16[8,8,32,128]{3,2,1,0:T(8,128)(2,1)S(1)} %pad_maximum_fusion.q_ref), channel_id=1, source_target_pairs={{0,4},{1,33},{2,6},{3,35},{4,8},{5,37},{6,10},{7,39},{8,12},{9,41}... | collective-permute-start | bytes 1572872 | tf_op jit(solution)/shard_map/ppermute | solution.py:32
  18.7 9.3 %collective-permute-start.5 = (bf16[8,8,32,128]{3,2,1,0:T(8,128)(2,1)S(1)}, bf16[8,8,32,128]{3,2,1,0:T(8,128)(2,1)S(1)}, u32[]{:S(2)}, u32[]{:S(2)}) collective-permute-start(bf16[8,8,32,128]{3,2,1,0:T(8,128)(2,1)S(1)} %pad_maximum_fusion.q_ref), channel_id=1, source_target_pairs={{0,12},{1,97},{2,14},{3,99},{4,0},{5,101},{6,2},{7,103},{8,4},{9,1... | collective-permute-start | bytes 1572872 | tf_op jit(solution)/shard_map/ppermute | solution.py:32
  27.7 9.5 %collective-permute-start.6 = (bf16[4,8,32,128]{3,2,1,0:T(8,128)(2,1)S(1)}, bf16[4,8,32,128]{3,2,1,0:T(8,128)(2,1)S(1)}, u32[]{:S(2)}, u32[]{:S(2)}) collective-permute-start(bf16[4,8,32,128]{3,2,1,0:T(8,128)(2,1)S(1)} %slice.49), channel_id=1, source_target_pairs={{0,4},{1,33},{2,6},{3,35},{4,8},{5,37},{6,10},{7,39},{8,12},{9,41}... | collective-permute-start | bytes 786440 | tf_op jit(solution)/shard_map/ppermute | solution.py:32
  28.0 9.2 %collective-permute-start.7 = (bf16[4,8,32,128]{3,2,1,0:T(8,128)(2,1)S(1)}, bf16[4,8,32,128]{3,2,1,0:T(8,128)(2,1)S(1)}, u32[]{:S(2)}, u32[]{:S(2)}) collective-permute-start(bf16[4,8,32,128]{3,2,1,0:T(8,128)(2,1)S(1)} %slice.50), channel_id=1, source_target_pairs={{0,12},{1,97},{2,14},{3,99},{4,0},{5,101},{6,2},{7,103},{8,4},{9,1... | collective-permute-start | bytes 786440 | tf_op jit(solution)/shard_map/ppermute | solution.py:32
  36.8 10.0 %collective-permute-start.8 = (bf16[8,2,144,128]{3,2,1,0:T(8,128)(2,1)S(1)}, bf16[8,2,144,128]{3,2,1,0:T(8,128)(2,1)S(1)}, u32[]{:S(2)}, u32[]{:S(2)}) collective-permute-start(bf16[8,2,144,128]{3,2,1,0:T(8,128)(2,1)S(1)} %attend_plane.6), channel_id=1, source_target_pairs={{0,12},{1,97},{2,14},{3,99},{4,0},{5,101},{6,2},{7,103},{8,4},{9,1... | collective-permute-start | bytes 1769480 | tf_op jit(solution)/shard_map/ppermute | solution.py:32
  42.8 11.7 %collective-permute-start.9 = (bf16[8,2,144,128]{3,2,1,0:T(8,128)(2,1)S(1)}, bf16[8,2,144,128]{3,2,1,0:T(8,128)(2,1)S(1)}, u32[]{:S(2)}, u32[]{:S(2)}) collective-permute-start(bf16[8,2,144,128]{3,2,1,0:T(8,128)(2,1)S(1)} %attend_plane.7), channel_id=1, source_target_pairs={{0,8},{1,65},{2,10},{3,67},{4,12},{5,69},{6,14},{7,71},{8,0},{9,73... | collective-permute-start | bytes 1769480 | tf_op jit(solution)/shard_map/ppermute | solution.py:32
  52.3 11.2 %collective-permute-start.10 = (bf16[8,2,144,128]{3,2,1,0:T(8,128)(2,1)S(1)}, bf16[8,2,144,128]{3,2,1,0:T(8,128)(2,1)S(1)}, u32[]{:S(2)}, u32[]{:S(2)}) collective-permute-start(bf16[8,2,144,128]{3,2,1,0:T(8,128)(2,1)S(1)} %attend_plane.8), channel_id=1, source_target_pairs={{0,4},{1,33},{2,6},{3,35},{4,8},{5,37},{6,10},{7,39},{8,12},{9,41}... | collective-permute-start | bytes 1769480 | tf_op jit(solution)/shard_map/ppermute | solution.py:32
  64.7 39.7 %copy-start = (bf16[4096,512]{1,0:T(8,128)(2,1)S(1)}, bf16[4096,512]{1,0:T(8,128)(2,1)}, u32[]{:S(2)}) copy-start(bf16[4096,512]{1,0:T(8,128)(2,1)} %w_ref.7) | copy-start | bytes 12582916
  64.8 5.2 %collective-permute-start.11 = (bf16[2,2,144,128]{3,2,1,0:T(8,128)(2,1)S(1)}, bf16[2,2,144,128]{3,2,1,0:T(8,128)(2,1)S(1)}, u32[]{:S(2)}, u32[]{:S(2)}) collective-permute-start(bf16[2,2,144,128]{3,2,1,0:T(8,128)(2,1)S(1)} %get-tuple-element.53), channel_id=1, source_target_pairs={{0,96},{1,13},{2,98},{3,15},{4,100},{5,1},{6,102},{7,3},{8,104},{9... | collective-permute-start | bytes 442376 | tf_op jit(solution)/shard_map/ppermute | solution.py:32
  67.1 7.9 %collective-permute-start.12 = (bf16[2,2,144,128]{3,2,1,0:T(8,128)(2,1)S(1)}, bf16[2,2,144,128]{3,2,1,0:T(8,128)(2,1)S(1)}, u32[]{:S(2)}, u32[]{:S(2)}) collective-permute-start(bf16[2,2,144,128]{3,2,1,0:T(8,128)(2,1)S(1)} %get-tuple-element.52), channel_id=1, source_target_pairs={{0,32},{1,5},{2,34},{3,7},{4,36},{5,9},{6,38},{7,11},{8,40},{9,13}... | collective-permute-start | bytes 442376 | tf_op jit(solution)/shard_map/ppermute | solution.py:32
  67.1 7.9 %collective-permute-start.13 = (bf16[2,2,144,128]{3,2,1,0:T(8,128)(2,1)S(1)}, bf16[2,2,144,128]{3,2,1,0:T(8,128)(2,1)S(1)}, u32[]{:S(2)}, u32[]{:S(2)}) collective-permute-start(bf16[2,2,144,128]{3,2,1,0:T(8,128)(2,1)S(1)} %get-tuple-element.51), channel_id=1, source_target_pairs={{0,64},{1,9},{2,66},{3,11},{4,68},{5,13},{6,70},{7,15},{8,72},{9,1... | collective-permute-start | bytes 442376 | tf_op jit(solution)/shard_map/ppermute | solution.py:32
  75.4 6.7 %collective-permute-start.14 = (bf16[2,2,144,128]{3,2,1,0:T(8,128)(2,1)S(1)}, bf16[2,2,144,128]{3,2,1,0:T(8,128)(2,1)S(1)}, u32[]{:S(2)}, u32[]{:S(2)}) collective-permute-start(bf16[2,2,144,128]{3,2,1,0:T(8,128)(2,1)S(1)} %combine.3.mine), channel_id=1, source_target_pairs={{0,16},{1,17},{2,18},{3,19},{4,20},{5,21},{6,22},{7,23},{8,24},{9,... | collective-permute-start | bytes 442376 | tf_op jit(solution)/shard_map/ppermute | solution.py:32
  82.5 6.7 %collective-permute-start.16 = (bf16[16,4096]{1,0:T(8,128)(2,1)S(1)}, bf16[16,4096]{1,0:T(8,128)(2,1)S(1)}, u32[]{:S(2)}, u32[]{:S(2)}) collective-permute-start(bf16[16,4096]{1,0:T(8,128)(2,1)S(1)} %finish.1.x0), channel_id=1, source_target_pairs={{0,64},{1,9},{2,66},{3,11},{4,68},{5,13},{6,70},{7,15},{8,72},{9,1... | collective-permute-start | bytes 393224 | tf_op jit(solution)/shard_map/ppermute | solution.py:32
  83.2 7.2 %collective-permute-start.15 = (bf16[16,4096]{1,0:T(8,128)(2,1)S(1)}, bf16[16,4096]{1,0:T(8,128)(2,1)S(1)}, u32[]{:S(2)}, u32[]{:S(2)}) collective-permute-start(bf16[16,4096]{1,0:T(8,128)(2,1)S(1)} %finish.1.x0), channel_id=1, source_target_pairs={{0,32},{1,5},{2,34},{3,7},{4,36},{5,9},{6,38},{7,11},{8,40},{9,13}... | collective-permute-start | bytes 393224 | tf_op jit(solution)/shard_map/ppermute | solution.py:32
  85.3 5.1 %collective-permute-start.17 = (bf16[16,4096]{1,0:T(8,128)(2,1)S(1)}, bf16[16,4096]{1,0:T(8,128)(2,1)S(1)}, u32[]{:S(2)}, u32[]{:S(2)}) collective-permute-start(bf16[16,4096]{1,0:T(8,128)(2,1)S(1)} %finish.1.x0), channel_id=1, source_target_pairs={{0,96},{1,13},{2,98},{3,15},{4,100},{5,1},{6,102},{7,3},{8,104},{9... | collective-permute-start | bytes 393224 | tf_op jit(solution)/shard_map/ppermute | solution.py:32
  89.1 1.3 %collective-permute-start.18 = (bf16[16,4096]{1,0:T(8,128)(2,1)S(1)}, bf16[16,4096]{1,0:T(8,128)(2,1)S(1)}, u32[]{:S(2)}, u32[]{:S(2)}) collective-permute-start(bf16[16,4096]{1,0:T(8,128)(2,1)S(1)} %collective-permute-done.16.x2), channel_id=1, source_target_pairs={{0,1},{1,0},{2,3},{3,2},{4,5},{5,4},{6,7},{7,6},{8,9},{9,8},{10,11... | collective-permute-start | bytes 393224 | tf_op jit(solution)/shard_map/ppermute | solution.py:32
  90.5 10.5 %collective-permute-start.19 = (bf16[64,4096]{1,0:T(8,128)(2,1)S(1)}, bf16[64,4096]{1,0:T(8,128)(2,1)S(1)}, u32[]{:S(2)}, u32[]{:S(2)}) collective-permute-start(bf16[64,4096]{1,0:T(8,128)(2,1)S(1)} %assemble.1.x_ref), channel_id=1, source_target_pairs={{0,4},{1,33},{2,6},{3,35},{4,8},{5,37},{6,10},{7,39},{8,12},{9,41}... | collective-permute-start | bytes 1572872 | tf_op jit(solution)/shard_map/ppermute | solution.py:32
  90.6 10.5 %collective-permute-start.20 = (bf16[64,4096]{1,0:T(8,128)(2,1)S(1)}, bf16[64,4096]{1,0:T(8,128)(2,1)S(1)}, u32[]{:S(2)}, u32[]{:S(2)}) collective-permute-start(bf16[64,4096]{1,0:T(8,128)(2,1)S(1)} %assemble.1.x_ref), channel_id=1, source_target_pairs={{0,12},{1,97},{2,14},{3,99},{4,0},{5,101},{6,2},{7,103},{8,4},{9,1... | collective-permute-start | bytes 1572872 | tf_op jit(solution)/shard_map/ppermute | solution.py:32
  101.0 7.7 %collective-permute-start.21 = (bf16[32,4096]{1,0:T(8,128)(2,1)S(1)}, bf16[32,4096]{1,0:T(8,128)(2,1)S(1)}, u32[]{:S(2)}, u32[]{:S(2)}) collective-permute-start(bf16[32,4096]{1,0:T(8,128)(2,1)S(1)} %slice.55), channel_id=1, source_target_pairs={{0,4},{1,33},{2,6},{3,35},{4,8},{5,37},{6,10},{7,39},{8,12},{9,41}... | collective-permute-start | bytes 786440 | tf_op jit(solution)/shard_map/ppermute | solution.py:32
  101.1 7.5 %collective-permute-start.22 = (bf16[32,4096]{1,0:T(8,128)(2,1)S(1)}, bf16[32,4096]{1,0:T(8,128)(2,1)S(1)}, u32[]{:S(2)}, u32[]{:S(2)}) collective-permute-start(bf16[32,4096]{1,0:T(8,128)(2,1)S(1)} %slice.56), channel_id=1, source_target_pairs={{0,12},{1,97},{2,14},{3,99},{4,0},{5,101},{6,2},{7,103},{8,4},{9,1... | collective-permute-start | bytes 786440 | tf_op jit(solution)/shard_map/ppermute | solution.py:32
  110.0 1.6 %collective-permute-start.23 = (f32[128,512]{1,0:T(8,128)S(1)}, f32[128,512]{1,0:T(8,128)S(1)}, u32[]{:S(2)}, u32[]{:S(2)}) collective-permute-start(f32[128,512]{1,0:T(8,128)S(1)} %slice.58), channel_id=1, source_target_pairs={{0,1},{1,0},{2,3},{3,2},{4,5},{5,4},{6,7},{7,6},{8,9},{9,8},{10,11... | collective-permute-start | bytes 786440 | tf_op jit(solution)/shard_map/ppermute | solution.py:32
  111.7 4.3 %collective-permute-start.24 = (bf16[64,512]{1,0:T(8,128)(2,1)S(1)}, bf16[64,512]{1,0:T(8,128)(2,1)S(1)}, u32[]{:S(2)}, u32[]{:S(2)}) collective-permute-start(bf16[64,512]{1,0:T(8,128)(2,1)S(1)} %slice.66), channel_id=1, source_target_pairs={{0,2},{1,3},{2,0},{3,1},{4,6},{5,7},{6,4},{7,5},{8,10},{9,11},{10,... | collective-permute-start | bytes 196616 | tf_op jit(solution)/shard_map/ppermute | solution.py:32

commit v4 on v3

--- a/solution.py
+++ b/solution.py
@@ -206,32 +206,30 @@
     )(*own, *others)
 
 
-def finish_kernel(mine, theirs, o_ref, rows):
+def finish_kernel(mine, theirs, o_ref, rows, *, kv):
     eye = diagonal()
-    for kv in range(mine.shape[1]):
-        for dy in range(2):
-            out, _, total = merged([mine[dy, kv], theirs[1 - dy, kv]], eye)
-            rows[kv, dy] = out * spread(1.0 / total, eye)
-    for kv, h in itertools.product(range(mine.shape[1]), range(16)):
-        c = (kv * 16 + h) * 128
-        both = [rows[kv, dy, pl.ds(h, 8, stride=16), :] for dy in range(2)]
-        o_ref[:, c : c + 128] = jnp.concatenate(both, axis=0).astype(jnp.bfloat16)
-
-
-def finish(mine, theirs):
-    vmem = pl.BlockSpec(memory_space=pltpu.VMEM)
-    return pl.pallas_call(
-        finish_kernel,
+    for dy in range(2):
+        out, _, total = merged([mine[dy, kv], theirs[1 - dy]], eye)
+        rows[dy] = out * spread(1.0 / total, eye)
+    for h in range(16):
+        both = [rows[dy, pl.ds(h, 8, stride=16), :] for dy in range(2)]
+        o_ref[:, h * 128 : (h + 1) * 128] = jnp.concatenate(both, axis=0).astype(jnp.bfloat16)
+
+
+def finish(mine, theirs, kv):
+    vmem = pl.BlockSpec(memory_space=pltpu.VMEM)
+    return pl.pallas_call(
+        functools.partial(finish_kernel, kv=kv),
         in_specs=[vmem, vmem],
         out_specs=vmem,
-        scratch_shapes=[pltpu.VMEM((mine.shape[1], 2, 128, 128), jnp.float32)],
+        scratch_shapes=[pltpu.VMEM((2, 128, 128), jnp.float32)],
         compiler_params=pltpu.CompilerParams(vmem_limit_bytes=4 * MIB),
-        out_shape=jax.ShapeDtypeStruct((16, mine.shape[1] * 2048), jnp.bfloat16),
+        out_shape=jax.ShapeDtypeStruct((16, 2048), jnp.bfloat16),
         name="finish",
     )(mine, theirs)
 
 
-def assemble_kernel(x0, x1, x2, x3, _, o_ref):
+def assemble_kernel(x0, x1, x2, x3, o_ref):
     for i, x in enumerate((x0, x1, x2, x3)):
         o_ref[i * x.shape[0] : (i + 1) * x.shape[0], :] = x[...]
 
@@ -241,7 +239,7 @@
     rows, width = pieces[0].shape
     return pl.pallas_call(
         assemble_kernel,
-        in_specs=[vmem] * 4 + [pl.BlockSpec(memory_space=pl.ANY)],
+        in_specs=[vmem] * RING,
         out_specs=vmem,
         out_shape=jax.ShapeDtypeStruct((RING * rows, width), pieces[0].dtype),
         compiler_params=pltpu.CompilerParams(vmem_limit_bytes=4 * MIB),
@@ -249,48 +247,60 @@
     )(*pieces)
 
 
-def project_kernel(x_ref, w_ref, o_ref):
-    o_ref[...] = jnp.dot(x_ref[...], w_ref[...], preferred_element_type=jnp.float32)
-
-
-def project(x, w):
-    vmem = pl.BlockSpec(memory_space=pltpu.VMEM)
-    return pl.pallas_call(
-        project_kernel,
-        in_specs=[vmem, vmem],
-        out_specs=vmem,
-        out_shape=jax.ShapeDtypeStruct((x.shape[0], w.shape[1]), jnp.float32),
+def times_weight(xs, w_ref, kv):
+    depth = xs[0].shape[1]
+    x = jnp.concatenate([x[...] for x in xs], axis=0)
+    return jnp.dot(x, w_ref[kv * depth : (kv + 1) * depth, :], preferred_element_type=jnp.float32)
+
+
+def project_kernel(*refs, kv):
+    w_ref, o_ref = refs[-2:]
+    o_ref[...] = times_weight(refs[:-2], w_ref, kv)
+
+
+def project(xs, w, kv):
+    vmem = pl.BlockSpec(memory_space=pltpu.VMEM)
+    rows, depth = len(xs) * xs[0].shape[0], xs[0].shape[1]
+    return pl.pallas_call(
+        functools.partial(project_kernel, kv=kv),
+        in_specs=[vmem] * (len(xs) + 1),
+        out_specs=vmem,
+        out_shape=jax.ShapeDtypeStruct((rows, w.shape[1]), jnp.float32),
         compiler_params=pltpu.CompilerParams(vmem_limit_bytes=8 * MIB),
-        cost_estimate=pl.CostEstimate(
-            flops=8 * x.shape[0] * w.shape[0] * w.shape[1], bytes_accessed=4 * MIB, transcendentals=0
-        ),
+        cost_estimate=pl.CostEstimate(flops=4 * rows * depth * w.shape[1], bytes_accessed=4 * MIB, transcendentals=0),
         name="project",
-    )(x, w)
-
-
-def place_kernel(info, y0, y1, y3, xa_ref, xb_ref, w_ref, o_ref):
+    )(*xs, w)
+
+
+def place_kernel(info, y0, y1, x_ref, w_ref, o_ref):
     me = tuple(info[i] for i in range(5))
     yl, core = me[3], me[4]
-    x = jnp.concatenate([xa_ref[...], xb_ref[...]], axis=0)
-    y2 = jnp.dot(x, w_ref[...], preferred_element_type=jnp.float32)
-    for db, y in ((0, y0), (1, y1), (2, y2), (3, y3)):
-        for da, dy in itertools.product(range(RING), range(2)):
-            z, yh, xx = source(me, da, db, dy)
-            row = (((z & 1) ^ core) * 2 + ((z >> 1) ^ yl)) * 64 + yh * 32 + xx * 8
-            at = da * 16 + dy * 8
-            o_ref[pl.ds(pl.multiple_of(row, 8), 8), :] = y[at : at + 8, :]
-
-
-def place(info, y0, y1, y3, xa, xb, w):
+    last = times_weight([x_ref], w_ref, 1)
+    for kv, d2, d1, dy in itertools.product(range(2), range(RING), range(RING), range(2)):
+        da, db = (d1, d2) if kv == 0 else (d2, d1)
+        z, yh, x = source(me, da, db, dy)
+        row = (((z & 1) ^ core) * 2 + ((z >> 1) ^ yl)) * 64 + yh * 32 + x * 8
+        at = pl.ds(pl.multiple_of(row, 8), 8)
+        within = d1 * 16 + dy * 8
+        if kv == 0:
+            o_ref[at, :] = y0[d2 * 64 + within : d2 * 64 + within + 8, :]
+        elif d2 == 2:
+            o_ref[at, :] += last[within : within + 8, :]
+        else:
+            i = min(d2, 2) * 64 + within
+            o_ref[at, :] += y1[i : i + 8, :]
+
+
+def place(info, y0, y1, x, w):
     vmem = pl.BlockSpec(memory_space=pltpu.VMEM)
     return pl.pallas_call(
         place_kernel,
-        in_specs=[pl.BlockSpec(memory_space=pltpu.SMEM)] + [vmem] * 6,
-        out_specs=vmem,
-        out_shape=jax.ShapeDtypeStruct((RING * y0.shape[0], w.shape[1]), jnp.float32),
+        in_specs=[pl.BlockSpec(memory_space=pltpu.SMEM)] + [vmem] * 4,
+        out_specs=vmem,
+        out_shape=jax.ShapeDtypeStruct(y0.shape, jnp.float32),
         compiler_params=pltpu.CompilerParams(vmem_limit_bytes=8 * MIB),
         name="place",
-    )(info, y0, y1, y3, xa, xb, w)
+    )(info, y0, y1, x, w)
 
 
 def on_device(queries, keys, values, lengths, start, out_weight):
@@ -306,19 +316,15 @@
     q = jnp.concatenate([q] + [moved(q, a=d) for d in (1, 2, 3)], axis=0)
     q, vx, kx0, kx1, kx2, kx3 = together(q, vx, kx0, kx1, kx2, kx3)
 
-    def neighbours(x):
-        x1, x3 = moved(x, b=1), moved(x, b=3)
-        half = x.shape[0] // 2
-        return x1, x3, moved(x1[:half], b=1), moved(x3[half:], b=3)
-
-    q1, q3, q2a, q2b = neighbours(q)
+    q1, q2, q3 = (moved(q, b=d) for d in (1, 2, 3))
+
     kvs = tuple(range(nkv))
     own0 = attend(q, kx0, vx, kvs, 0, 4)
     q1, own0 = together(q1, own0)
     p1 = attend(q1, kx1, vx, kvs)
     r1 = moved(p1, b=-1)
-    q2a, q2b, p1 = together(q2a, q2b, p1)
-    p2 = attend(jnp.concatenate([q2a, q2b], axis=0), kx2, vx, kvs)
+    q2, q3, p1 = together(q2, q3, p1)
+    p2 = attend(q2, kx2, vx, kvs)
     r2 = moved(p2, b=-2)
     q3, p2, r1 = together(q3, p2, r1)
     p3 = attend(q3, kx3, vx, kvs)
@@ -327,11 +333,20 @@
     own1 = attend(q, kx0, vx, kvs, 4, 4)
     c = combine([own0, own1], [r1, r2, r3])
     c = combine([c[:2]], [moved(c[2 * d : 2 * d + 2], a=-d) for d in (1, 3, 2)])
-    attn = finish(c, moved(c, yh=1))
+    theirs = [moved(c[:, kv], yh=1) for kv in kvs]
+    attn = finish(c, theirs[0], 0)
     pieces = [moved(attn, a=d) for d in (1, 2, 3)]
-    attn = assemble(attn, *pieces, moved(pieces[1], core=1))
-    x1, x3, x2a, x2b = neighbours(attn)
-    y = place(info, project(attn, out_weight), project(x1, out_weight), project(x3, out_weight), x2a, x2b, out_weight)
+    later = finish(c, theirs[1], 1)
+    others = [moved(later, b=d) for d in (1, 2, 3)]
+    attn = assemble(attn, *pieces)
+    attn, *others = together(attn, *others)
+    x = [attn] + [moved(attn, b=d) for d in (1, 2, 3)]
+    later = assemble(later, *others)
+    later = [later] + [moved(later, a=d) for d in (1, 2, 3)]
+    y0 = project(x, out_weight, 0)
+    y0, *later = together(y0, *later[:2], later[3]) + (later[2],)
+    y1 = project(later[:3], out_weight, 1)
+    y = place(info, y0, y1, later[3], out_weight)
     y = y[:128] + moved(y[128:], core=1)
     y = y[:64] + moved(y[64:].astype(jnp.bfloat16), yl=1).astype(jnp.float32)
     return y.astype(jnp.bfloat16)

time: 117 us -> 120 us (1.026)
  starting transfers between devices: 37.3 us -> 42.9 us
  waiting for transfers between devices: 44.8 us -> 43.2 us
    ppermute x25 -> x29, starting transfers between devices: 37.3 us -> 42.9 us  [moved(): return lax.ppermute(x, ('cp', 'tp'), pairs)]
    ppermute x25 -> x29, waiting for transfers between devices: 44.8 us -> 43.2 us  [moved(): return lax.ppermute(x, ('cp', 'tp'), pairs)]
    pallas_call x5 -> x6, Pallas kernels: 2.85 us -> 1.77 us  [the longest x2 1.32 us: project(): pl.pallas_call(functools.partial(project_kernel, kv=kv), in_specs=[vmem]...]
  transfers between devices with their start and end apart: 25 -> 29, of which waited for: 15 -> 16; matrix products, arithmetic and copies ran while one was open for 2% -> 2% of each run, Pallas kernels for 23% -> 22%
where the time goes in v4:
time: 120 us; the launch traced here: 119 us
  waiting for transfers between devices  43.2 us (36%)
  starting transfers between devices  42.9 us (36%)
  Pallas kernels  29 us (24%)
  local copies, waits for them, and re-layouts  1.99 us (2%)
  between operations  1.6 us (1%)
    ppermute x29, waiting for transfers between devices, moved(): return lax.ppermute(x, ('cp', 'tp'), pairs)  43.2 us
    ppermute x29, starting transfers between devices, moved(): return lax.ppermute(x, ('cp', 'tp'), pairs)  42.9 us
    pallas_call x5, Pallas kernels, attend(): pl.pallas_call(functools.partial(attend_kernel, kvs=kvs, first=first, nb=...  22.3 us
  transfers between devices with their start and end apart: 29, of which 16 were waited for; matrix products, arithmetic and copies ran while one was open for 2% of the time, Pallas kernels for 22%

profile of v4, /device:TPU:0, one launch (start us, length us, event | category | flops | bytes accessed | tf_op | source)
XLA Modules:
  0.0 119.4 jit_solution(11133377037275565219)
XLA Ops:
  0.0 3.3 %collective-permute-start = (bf16[1,8,32,128]{3,2,1,0:T(8,128)(2,1)}, bf16[1,8,32,128]{3,2,1,0:T(8,128)(2,1)S(1)}, u32[]{:S(2)}, u32[]{:S(2)}) collective-permute-start(bf16[1,8,32,128]{3,2,1,0:T(8,128)(2,1)} %bitcast.18), channel_id=1, source_target_pairs={{0,16},{1,17},{2,18},{3,19},{4,20},{5,21},{6,22},{7,23},{8,24},{9,... | collective-permute-start | bytes 196616 | tf_op jit(solution)/shard_map/ppermute | solution.py:32
  3.3 1.8 %copy_bitcast_fusion = (bf16[2,2048,128]{2,1,0:T(8,128)(2,1)S(1)}, bf16[2,2048,128]{2,1,0:T(8,128)(2,1)S(1)}) fusion(bf16[2048,2,128]{2,1,0:T(2,128)(2,1)} %param.8, bf16[2048,2,128]{2,1,0:T(2,128)(2,1)} %param.7), kind=kLoop, calls=%fused_computation | loop fusion | bytes 4194304 | tf_op jit(solution)/shard_map/transpose | solution.py:311
  6.6 2.0 %collective-permute-start.1 = (bf16[2,8,32,128]{3,2,1,0:T(8,128)(2,1)S(1)}, bf16[2,8,32,128]{3,2,1,0:T(8,128)(2,1)S(1)}, u32[]{:S(2)}, u32[]{:S(2)}) collective-permute-start(bf16[2,8,32,128]{3,2,1,0:T(8,128)(2,1)S(1)} %pad_maximum_fusion.1), channel_id=1, source_target_pairs={{0,32},{1,5},{2,34},{3,7},{4,36},{5,9},{6,38},{7,11},{8,40},{9,13}... | collective-permute-start | bytes 393224 | tf_op jit(solution)/shard_map/ppermute | solution.py:32
  8.5 3.6 %collective-permute-start.2 = (bf16[2,8,32,128]{3,2,1,0:T(8,128)(2,1)S(1)}, bf16[2,8,32,128]{3,2,1,0:T(8,128)(2,1)S(1)}, u32[]{:S(2)}, u32[]{:S(2)}) collective-permute-start(bf16[2,8,32,128]{3,2,1,0:T(8,128)(2,1)S(1)} %pad_maximum_fusion.1), channel_id=1, source_target_pairs={{0,64},{1,9},{2,66},{3,11},{4,68},{5,13},{6,70},{7,15},{8,72},{9,1... | collective-permute-start | bytes 393224 | tf_op jit(solution)/shard_map/ppermute | solution.py:32
  13.1 2.2 %prepare.1 = (bf16[2,2048,256]{2,1,0:T(8,128)(2,1)S(1)}, bf16[2,2048,256]{2,1,0:T(8,128)(2,1)S(1)}, bf16[2,2048,256]{2,1,0:T(8,128)(2,1)S(1)}, bf16[2,2048,256]{...) custom-call(s32[7]{0:T(128)S(1)} %concatenate.10.info, bf16[2,2048,128]{2,1,0:T(8,128)(2,1)S(1)} %get-tuple-element.38.k_ref, ...), custom_call_target="tpu_custom_call" | custom-call | tf_op jit(solution)/shard_map/prepare/pallas_call | solution.py:87
  17.2 1.6 %collective-permute-start.4 = (bf16[8,8,32,128]{3,2,1,0:T(8,128)(2,1)S(1)}, bf16[8,8,32,128]{3,2,1,0:T(8,128)(2,1)S(1)}, u32[]{:S(2)}, u32[]{:S(2)}) collective-permute-start(bf16[8,8,32,128]{3,2,1,0:T(8,128)(2,1)S(1)} %pad_maximum_fusion.q_ref), channel_id=1, source_target_pairs={{0,4},{1,33},{2,6},{3,35},{4,8},{5,37},{6,10},{7,39},{8,12},{9,41}... | collective-permute-start | bytes 1572872 | tf_op jit(solution)/shard_map/ppermute | solution.py:32
  18.7 2.7 %collective-permute-start.5 = (bf16[8,8,32,128]{3,2,1,0:T(8,128)(2,1)S(1)}, bf16[8,8,32,128]{3,2,1,0:T(8,128)(2,1)S(1)}, u32[]{:S(2)}, u32[]{:S(2)}) collective-permute-start(bf16[8,8,32,128]{3,2,1,0:T(8,128)(2,1)S(1)} %pad_maximum_fusion.q_ref), channel_id=1, source_target_pairs={{0,8},{1,65},{2,10},{3,67},{4,12},{5,69},{6,14},{7,71},{8,0},{9,73... | collective-permute-start | bytes 1572872 | tf_op jit(solution)/shard_map/ppermute | solution.py:32
  21.5 1.4 %collective-permute-start.6 = (bf16[8,8,32,128]{3,2,1,0:T(8,128)(2,1)S(1)}, bf16[8,8,32,128]{3,2,1,0:T(8,128)(2,1)S(1)}, u32[]{:S(2)}, u32[]{:S(2)}) collective-permute-start(bf16[8,8,32,128]{3,2,1,0:T(8,128)(2,1)S(1)} %pad_maximum_fusion.q_ref), channel_id=1, source_target_pairs={{0,12},{1,97},{2,14},{3,99},{4,0},{5,101},{6,2},{7,103},{8,4},{9,1... | collective-permute-start | bytes 1572872 | tf_op jit(solution)/shard_map/ppermute | solution.py:32
  22.9 2.9 %attend_plane.5.refs_0_ = bf16[4,2,144,128]{3,2,1,0:T(8,128)(2,1)S(1)} custom-call(bf16[8,8,32,128]{3,2,1,0:T(8,128)(2,1)S(1)} %pad_maximum_fusion.q_ref, bf16[2,2048,256]{2,1,0:T(8,128)(2,1)S(1)} %get-tuple-element.46.kx, bf16[2,2048,256]{2,1,0:T(8,128)(2,1)S(1)} %get-tuple-element.47.vx), custom_call_target="tpu_custom_call" | custom-call | flops 2147483648 | bytes 4194304 | tf_op jit(solution)/shard_map/attend_plane/pallas_call | solution.py:157
  25.8 1.8 %collective-permute-done.4.q_ref = bf16[8,8,32,128]{3,2,1,0:T(8,128)(2,1)S(1)} collective-permute-done((bf16[8,8,32,128]{3,2,1,0:T(8,128)(2,1)S(1)}, bf16[8,8,32,128]{3,2,1,0:T(8,128)(2,1)S(1)}, u32[]{:S(2)}, u32[]{:S(2)}) %collective-permute-start.4) | collective-permute-done | bytes 524320 | tf_op jit(solution)/shard_map/ppermute | solution.py:32
  27.6 5.5 %attend_plane.6 = bf16[8,2,144,128]{3,2,1,0:T(8,128)(2,1)S(1)} custom-call(bf16[8,8,32,128]{3,2,1,0:T(8,128)(2,1)S(1)} %collective-permute-done.4.q_ref, bf16[2,2048,256]{2,1,0:T(8,128)(2,1)S(1)} %get-tuple-element.50.kx, bf16[2,2048,256]{2,1,0:T(8,128)(2,1)S(1)} %get-tuple-element.47.vx), custom_call_target="tpu_custom_call" | custom-call | flops 4294967296 | bytes 4194304 | tf_op jit(solution)/shard_map/attend_plane/pallas_call | solution.py:157
  33.2 1.6 %collective-permute-start.7 = (bf16[8,2,144,128]{3,2,1,0:T(8,128)(2,1)S(1)}, bf16[8,2,144,128]{3,2,1,0:T(8,128)(2,1)S(1)}, u32[]{:S(2)}, u32[]{:S(2)}) collective-permute-start(bf16[8,2,144,128]{3,2,1,0:T(8,128)(2,1)S(1)} %attend_plane.6), channel_id=1, source_target_pairs={{0,12},{1,97},{2,14},{3,99},{4,0},{5,101},{6,2},{7,103},{8,4},{9,1... | collective-permute-start | bytes 1769480 | tf_op jit(solution)/shard_map/ppermute | solution.py:32
  34.8 5.5 %attend_plane.7 = bf16[8,2,144,128]{3,2,1,0:T(8,128)(2,1)S(1)} custom-call(bf16[8,8,32,128]{3,2,1,0:T(8,128)(2,1)S(1)} %collective-permute-done.5.q_ref, bf16[2,2048,256]{2,1,0:T(8,128)(2,1)S(1)} %get-tuple-element.53.kx, bf16[2,2048,256]{2,1,0:T(8,128)(2,1)S(1)} %get-tuple-element.47.vx), custom_call_target="tpu_custom_call" | custom-call | flops 4294967296 | bytes 4194304 | tf_op jit(solution)/shard_map/attend_plane/pallas_call | solution.py:157
  40.4 2.7 %collective-permute-start.8 = (bf16[8,2,144,128]{3,2,1,0:T(8,128)(2,1)S(1)}, bf16[8,2,144,128]{3,2,1,0:T(8,128)(2,1)S(1)}, u32[]{:S(2)}, u32[]{:S(2)}) collective-permute-start(bf16[8,2,144,128]{3,2,1,0:T(8,128)(2,1)S(1)} %attend_plane.7), channel_id=1, source_target_pairs={{0,8},{1,65},{2,10},{3,67},{4,12},{5,69},{6,14},{7,71},{8,0},{9,73... | collective-permute-start | bytes 1769480 | tf_op jit(solution)/shard_map/ppermute | solution.py:32
  43.1 5.5 %attend_plane.8 = bf16[8,2,144,128]{3,2,1,0:T(8,128)(2,1)S(1)} custom-call(bf16[8,8,32,128]{3,2,1,0:T(8,128)(2,1)S(1)} %collective-permute-done.6.q_ref, bf16[2,2048,256]{2,1,0:T(8,128)(2,1)S(1)} %get-tuple-element.55.kx, bf16[2,2048,256]{2,1,0:T(8,128)(2,1)S(1)} %get-tuple-element.47.vx), custom_call_target="tpu_custom_call" | custom-call | flops 4294967296 | bytes 4194304 | tf_op jit(solution)/shard_map/attend_plane/pallas_call | solution.py:157
  49.1 2.9 %collective-permute-done.8.refs_3_ = bf16[8,2,144,128]{3,2,1,0:T(8,128)(2,1)S(1)} collective-permute-done((bf16[8,2,144,128]{3,2,1,0:T(8,128)(2,1)S(1)}, bf16[8,2,144,128]{3,2,1,0:T(8,128)(2,1)S(1)}, u32[]{:S(2)}, u32[]{:S(2)}) %collective-permute-start.8) | collective-permute-done | bytes 589856 | tf_op jit(solution)/shard_map/ppermute | solution.py:32
  52.1 2.8 %attend_plane.9.refs_1_ = bf16[4,2,144,128]{3,2,1,0:T(8,128)(2,1)S(1)} custom-call(bf16[8,8,32,128]{3,2,1,0:T(8,128)(2,1)S(1)} %pad_maximum_fusion.q_ref, bf16[2,2048,256]{2,1,0:T(8,128)(2,1)S(1)} %get-tuple-element.46.kx, bf16[2,2048,256]{2,1,0:T(8,128)(2,1)S(1)} %get-tuple-element.47.vx), custom_call_target="tpu_custom_call" | custom-call | flops 2147483648 | bytes 4194304 | tf_op jit(solution)/shard_map/attend_plane/pallas_call | solution.py:157
  54.8 5.0 %collective-permute-done.9.refs_4_ = bf16[8,2,144,128]{3,2,1,0:T(8,128)(2,1)S(1)} collective-permute-done((bf16[8,2,144,128]{3,2,1,0:T(8,128)(2,1)S(1)}, bf16[8,2,144,128]{3,2,1,0:T(8,128)(2,1)S(1)}, u32[]{:S(2)}, u32[]{:S(2)}) %collective-permute-start.9) | collective-permute-done | bytes 589856 | tf_op jit(solution)/shard_map/ppermute | solution.py:32
  61.2 2.3 %collective-permute-start.10 = (bf16[2,2,144,128]{3,2,1,0:T(8,128)(2,1)S(1)}, bf16[2,2,144,128]{3,2,1,0:T(8,128)(2,1)S(1)}, u32[]{:S(2)}, u32[]{:S(2)}) collective-permute-start(bf16[2,2,144,128]{3,2,1,0:T(8,128)(2,1)S(1)} %get-tuple-element.69), channel_id=1, source_target_pairs={{0,96},{1,13},{2,98},{3,15},{4,100},{5,1},{6,102},{7,3},{8,104},{9... | collective-permute-start | bytes 442376 | tf_op jit(solution)/shard_map/ppermute | solution.py:32
  63.5 1.7 %collective-permute-start.12 = (bf16[2,2,144,128]{3,2,1,0:T(8,128)(2,1)S(1)}, bf16[2,2,144,128]{3,2,1,0:T(8,128)(2,1)S(1)}, u32[]{:S(2)}, u32[]{:S(2)}) collective-permute-start(bf16[2,2,144,128]{3,2,1,0:T(8,128)(2,1)S(1)} %get-tuple-element.67), channel_id=1, source_target_pairs={{0,64},{1,9},{2,66},{3,11},{4,68},{5,13},{6,70},{7,15},{8,72},{9,1... | collective-permute-start | bytes 442376 | tf_op jit(solution)/shard_map/ppermute | solution.py:32
  66.4 5.0 %collective-permute-done.11.refs_2_ = bf16[2,2,144,128]{3,2,1,0:T(8,128)(2,1)S(1)} collective-permute-done((bf16[2,2,144,128]{3,2,1,0:T(8,128)(2,1)S(1)}, bf16[2,2,144,128]{3,2,1,0:T(8,128)(2,1)S(1)}, u32[]{:S(2)}, u32[]{:S(2)}) %collective-permute-start.11) | collective-permute-done | bytes 147488 | tf_op jit(solution)/shard_map/ppermute | solution.py:32
  71.8 2.8 %collective-permute-start.13 = (bf16[2,144,128]{2,1,0:T(8,128)(2,1)S(1)}, bf16[2,144,128]{2,1,0:T(8,128)(2,1)S(1)}, u32[]{:S(2)}, u32[]{:S(2)}) collective-permute-start(bf16[2,144,128]{2,1,0:T(8,128)(2,1)S(1)} %get-tuple-element.72), channel_id=1, source_target_pairs={{0,16},{1,17},{2,18},{3,19},{4,20},{5,21},{6,22},{7,23},{8,24},{9,... | collective-permute-start | bytes 221192 | tf_op jit(solution)/shard_map/ppermute | solution.py:32
  75.4 2.3 %collective-permute-done.13.theirs = bf16[2,144,128]{2,1,0:T(8,128)(2,1)S(1)} collective-permute-done((bf16[2,144,128]{2,1,0:T(8,128)(2,1)S(1)}, bf16[2,144,128]{2,1,0:T(8,128)(2,1)S(1)}, u32[]{:S(2)}, u32[]{:S(2)}) %collective-permute-start.13) | collective-permute-done | bytes 73760 | tf_op jit(solution)/shard_map/ppermute | solution.py:32
  78.0 3.4 %collective-permute-start.15 = (bf16[16,2048]{1,0:T(8,128)(2,1)S(1)}, bf16[16,2048]{1,0:T(8,128)(2,1)S(1)}, u32[]{:S(2)}, u32[]{:S(2)}) collective-permute-start(bf16[16,2048]{1,0:T(8,128)(2,1)S(1)} %finish.2.x0), channel_id=1, source_target_pairs={{0,64},{1,9},{2,66},{3,11},{4,68},{5,13},{6,70},{7,15},{8,72},{9,1... | collective-permute-start | bytes 196616 | tf_op jit(solution)/shard_map/ppermute | solution.py:32
  81.9 3.0 %collective-permute-start.19 = (bf16[16,2048]{1,0:T(8,128)(2,1)S(1)}, bf16[16,2048]{1,0:T(8,128)(2,1)S(1)}, u32[]{:S(2)}, u32[]{:S(2)}) collective-permute-start(bf16[16,2048]{1,0:T(8,128)(2,1)S(1)} %finish.3.x0), channel_id=1, source_target_pairs={{0,8},{1,65},{2,10},{3,67},{4,12},{5,69},{6,14},{7,71},{8,0},{9,73... | collective-permute-start | bytes 196616 | tf_op jit(solution)/shard_map/ppermute | solution.py:32
  85.7 2.4 %collective-permute-done.18.x1 = bf16[16,2048]{1,0:T(8,128)(2,1)S(1)} collective-permute-done((bf16[16,2048]{1,0:T(8,128)(2,1)S(1)}, bf16[16,2048]{1,0:T(8,128)(2,1)S(1)}, u32[]{:S(2)}, u32[]{:S(2)}) %collective-permute-start.18) | collective-permute-done | bytes 65568 | tf_op jit(solution)/shard_map/ppermute | solution.py:32
  90.3 2.8 %collective-permute-start.22 = (bf16[64,2048]{1,0:T(8,128)(2,1)S(1)}, bf16[64,2048]{1,0:T(8,128)(2,1)S(1)}, u32[]{:S(2)}, u32[]{:S(2)}) collective-permute-start(bf16[64,2048]{1,0:T(8,128)(2,1)S(1)} %assemble.2.refs_0_), channel_id=1, source_target_pairs={{0,8},{1,65},{2,10},{3,67},{4,12},{5,69},{6,14},{7,71},{8,0},{9,73... | collective-permute-start | bytes 786440 | tf_op jit(solution)/shard_map/ppermute | solution.py:32
  93.4 1.9 %collective-permute-start.24 = (bf16[64,2048]{1,0:T(8,128)(2,1)S(1)}, bf16[64,2048]{1,0:T(8,128)(2,1)S(1)}, u32[]{:S(2)}, u32[]{:S(2)}) collective-permute-start(bf16[64,2048]{1,0:T(8,128)(2,1)S(1)} %assemble.3.refs_0_), channel_id=1, source_target_pairs={{0,32},{1,5},{2,34},{3,7},{4,36},{5,9},{6,38},{7,11},{8,40},{9,13}... | collective-permute-start | bytes 786440 | tf_op jit(solution)/shard_map/ppermute | solution.py:32
  96.7 7.1 %collective-permute-done.21.refs_1_ = bf16[64,2048]{1,0:T(8,128)(2,1)S(1)} collective-permute-done((bf16[64,2048]{1,0:T(8,128)(2,1)S(1)}, bf16[64,2048]{1,0:T(8,128)(2,1)S(1)}, u32[]{:S(2)}, u32[]{:S(2)}) %collective-permute-start.21) | collective-permute-done | bytes 262176 | tf_op jit(solution)/shard_map/ppermute | solution.py:32
  105.2 6.5 %collective-permute-done.26.x_ref = bf16[64,2048]{1,0:T(8,128)(2,1)S(1)} collective-permute-done((bf16[64,2048]{1,0:T(8,128)(2,1)S(1)}, bf16[64,2048]{1,0:T(8,128)(2,1)S(1)}, u32[]{:S(2)}, u32[]{:S(2)}) %collective-permute-start.26) | collective-permute-done | bytes 262176 | tf_op jit(solution)/shard_map/ppermute | solution.py:32
  112.9 1.5 %collective-permute-done.27 = f32[128,512]{1,0:T(8,128)S(1)} collective-permute-done((f32[128,512]{1,0:T(8,128)S(1)}, f32[128,512]{1,0:T(8,128)S(1)}, u32[]{:S(2)}, u32[]{:S(2)}) %collective-permute-start.27) | collective-permute-done | bytes 262176 | tf_op jit(solution)/shard_map/ppermute | solution.py:32
  114.5 4.3 %collective-permute-done.28 = bf16[64,512]{1,0:T(8,128)(2,1)S(1)} collective-permute-done((bf16[64,512]{1,0:T(8,128)(2,1)S(1)}, bf16[64,512]{1,0:T(8,128)(2,1)S(1)}, u32[]{:S(2)}, u32[]{:S(2)}) %collective-permute-start.28) | collective-permute-done | bytes 65568 | tf_op jit(solution)/shard_map/ppermute | solution.py:32
  (55 shorter events, 15.9 us)
Async XLA Ops:
  0.0 6.5 %copy-start.1 = (bf16[8,32,128]{2,1,0:T(8,128)(2,1)S(1)}, bf16[8,32,128]{2,1,0:T(8,128)(2,1)}, u32[]{:S(2)}) copy-start(bf16[8,32,128]{2,1,0:T(8,128)(2,1)} %param.6) | copy-start | bytes 196612
  0.0 6.5 %collective-permute-start = (bf16[1,8,32,128]{3,2,1,0:T(8,128)(2,1)}, bf16[1,8,32,128]{3,2,1,0:T(8,128)(2,1)S(1)}, u32[]{:S(2)}, u32[]{:S(2)}) collective-permute-start(bf16[1,8,32,128]{3,2,1,0:T(8,128)(2,1)} %bitcast.18), channel_id=1, source_target_pairs={{0,16},{1,17},{2,18},{3,19},{4,20},{5,21},{6,22},{7,23},{8,24},{9,... | collective-permute-start | bytes 196616 | tf_op jit(solution)/shard_map/ppermute | solution.py:32
  6.6 8.7 %collective-permute-start.1 = (bf16[2,8,32,128]{3,2,1,0:T(8,128)(2,1)S(1)}, bf16[2,8,32,128]{3,2,1,0:T(8,128)(2,1)S(1)}, u32[]{:S(2)}, u32[]{:S(2)}) collective-permute-start(bf16[2,8,32,128]{3,2,1,0:T(8,128)(2,1)S(1)} %pad_maximum_fusion.1), channel_id=1, source_target_pairs={{0,32},{1,5},{2,34},{3,7},{4,36},{5,9},{6,38},{7,11},{8,40},{9,13}... | collective-permute-start | bytes 393224 | tf_op jit(solution)/shard_map/ppermute | solution.py:32
  8.5 7.9 %collective-permute-start.2 = (bf16[2,8,32,128]{3,2,1,0:T(8,128)(2,1)S(1)}, bf16[2,8,32,128]{3,2,1,0:T(8,128)(2,1)S(1)}, u32[]{:S(2)}, u32[]{:S(2)}) collective-permute-start(bf16[2,8,32,128]{3,2,1,0:T(8,128)(2,1)S(1)} %pad_maximum_fusion.1), channel_id=1, source_target_pairs={{0,64},{1,9},{2,66},{3,11},{4,68},{5,13},{6,70},{7,15},{8,72},{9,1... | collective-permute-start | bytes 393224 | tf_op jit(solution)/shard_map/ppermute | solution.py:32
  12.1 5.0 %collective-permute-start.3 = (bf16[2,8,32,128]{3,2,1,0:T(8,128)(2,1)S(1)}, bf16[2,8,32,128]{3,2,1,0:T(8,128)(2,1)S(1)}, u32[]{:S(2)}, u32[]{:S(2)}) collective-permute-start(bf16[2,8,32,128]{3,2,1,0:T(8,128)(2,1)S(1)} %pad_maximum_fusion.1), channel_id=1, source_target_pairs={{0,96},{1,13},{2,98},{3,15},{4,100},{5,1},{6,102},{7,3},{8,104},{9... | collective-permute-start | bytes 393224 | tf_op jit(solution)/shard_map/ppermute | solution.py:32
  17.2 10.5 %collective-permute-start.4 = (bf16[8,8,32,128]{3,2,1,0:T(8,128)(2,1)S(1)}, bf16[8,8,32,128]{3,2,1,0:T(8,128)(2,1)S(1)}, u32[]{:S(2)}, u32[]{:S(2)}) collective-permute-start(bf16[8,8,32,128]{3,2,1,0:T(8,128)(2,1)S(1)} %pad_maximum_fusion.q_ref), channel_id=1, source_target_pairs={{0,4},{1,33},{2,6},{3,35},{4,8},{5,37},{6,10},{7,39},{8,12},{9,41}... | collective-permute-start | bytes 1572872 | tf_op jit(solution)/shard_map/ppermute | solution.py:32
  18.7 16.1 %collective-permute-start.5 = (bf16[8,8,32,128]{3,2,1,0:T(8,128)(2,1)S(1)}, bf16[8,8,32,128]{3,2,1,0:T(8,128)(2,1)S(1)}, u32[]{:S(2)}, u32[]{:S(2)}) collective-permute-start(bf16[8,8,32,128]{3,2,1,0:T(8,128)(2,1)S(1)} %pad_maximum_fusion.q_ref), channel_id=1, source_target_pairs={{0,8},{1,65},{2,10},{3,67},{4,12},{5,69},{6,14},{7,71},{8,0},{9,73... | collective-permute-start | bytes 1572872 | tf_op jit(solution)/shard_map/ppermute | solution.py:32
  21.5 13.3 %collective-permute-start.6 = (bf16[8,8,32,128]{3,2,1,0:T(8,128)(2,1)S(1)}, bf16[8,8,32,128]{3,2,1,0:T(8,128)(2,1)S(1)}, u32[]{:S(2)}, u32[]{:S(2)}) collective-permute-start(bf16[8,8,32,128]{3,2,1,0:T(8,128)(2,1)S(1)} %pad_maximum_fusion.q_ref), channel_id=1, source_target_pairs={{0,12},{1,97},{2,14},{3,99},{4,0},{5,101},{6,2},{7,103},{8,4},{9,1... | collective-permute-start | bytes 1572872 | tf_op jit(solution)/shard_map/ppermute | solution.py:32
  33.2 10.0 %collective-permute-start.7 = (bf16[8,2,144,128]{3,2,1,0:T(8,128)(2,1)S(1)}, bf16[8,2,144,128]{3,2,1,0:T(8,128)(2,1)S(1)}, u32[]{:S(2)}, u32[]{:S(2)}) collective-permute-start(bf16[8,2,144,128]{3,2,1,0:T(8,128)(2,1)S(1)} %attend_plane.6), channel_id=1, source_target_pairs={{0,12},{1,97},{2,14},{3,99},{4,0},{5,101},{6,2},{7,103},{8,4},{9,1... | collective-permute-start | bytes 1769480 | tf_op jit(solution)/shard_map/ppermute | solution.py:32
  40.4 11.7 %collective-permute-start.8 = (bf16[8,2,144,128]{3,2,1,0:T(8,128)(2,1)S(1)}, bf16[8,2,144,128]{3,2,1,0:T(8,128)(2,1)S(1)}, u32[]{:S(2)}, u32[]{:S(2)}) collective-permute-start(bf16[8,2,144,128]{3,2,1,0:T(8,128)(2,1)S(1)} %attend_plane.7), channel_id=1, source_target_pairs={{0,8},{1,65},{2,10},{3,67},{4,12},{5,69},{6,14},{7,71},{8,0},{9,73... | collective-permute-start | bytes 1769480 | tf_op jit(solution)/shard_map/ppermute | solution.py:32
  48.7 11.2 %collective-permute-start.9 = (bf16[8,2,144,128]{3,2,1,0:T(8,128)(2,1)S(1)}, bf16[8,2,144,128]{3,2,1,0:T(8,128)(2,1)S(1)}, u32[]{:S(2)}, u32[]{:S(2)}) collective-permute-start(bf16[8,2,144,128]{3,2,1,0:T(8,128)(2,1)S(1)} %attend_plane.8), channel_id=1, source_target_pairs={{0,4},{1,33},{2,6},{3,35},{4,8},{5,37},{6,10},{7,39},{8,12},{9,41}... | collective-permute-start | bytes 1769480 | tf_op jit(solution)/shard_map/ppermute | solution.py:32
  59.9 44.0 %copy-start = (bf16[4096,512]{1,0:T(8,128)(2,1)S(1)}, bf16[4096,512]{1,0:T(8,128)(2,1)}, u32[]{:S(2)}) copy-start(bf16[4096,512]{1,0:T(8,128)(2,1)} %w_ref.1) | copy-start | bytes 12582916
  61.2 5.2 %collective-permute-start.10 = (bf16[2,2,144,128]{3,2,1,0:T(8,128)(2,1)S(1)}, bf16[2,2,144,128]{3,2,1,0:T(8,128)(2,1)S(1)}, u32[]{:S(2)}, u32[]{:S(2)}) collective-permute-start(bf16[2,2,144,128]{3,2,1,0:T(8,128)(2,1)S(1)} %get-tuple-element.69), channel_id=1, source_target_pairs={{0,96},{1,13},{2,98},{3,15},{4,100},{5,1},{6,102},{7,3},{8,104},{9... | collective-permute-start | bytes 442376 | tf_op jit(solution)/shard_map/ppermute | solution.py:32
  63.5 7.9 %collective-permute-start.11 = (bf16[2,2,144,128]{3,2,1,0:T(8,128)(2,1)S(1)}, bf16[2,2,144,128]{3,2,1,0:T(8,128)(2,1)S(1)}, u32[]{:S(2)}, u32[]{:S(2)}) collective-permute-start(bf16[2,2,144,128]{3,2,1,0:T(8,128)(2,1)S(1)} %get-tuple-element.68), channel_id=1, source_target_pairs={{0,32},{1,5},{2,34},{3,7},{4,36},{5,9},{6,38},{7,11},{8,40},{9,13}... | collective-permute-start | bytes 442376 | tf_op jit(solution)/shard_map/ppermute | solution.py:32
  63.5 7.9 %collective-permute-start.12 = (bf16[2,2,144,128]{3,2,1,0:T(8,128)(2,1)S(1)}, bf16[2,2,144,128]{3,2,1,0:T(8,128)(2,1)S(1)}, u32[]{:S(2)}, u32[]{:S(2)}) collective-permute-start(bf16[2,2,144,128]{3,2,1,0:T(8,128)(2,1)S(1)} %get-tuple-element.67), channel_id=1, source_target_pairs={{0,64},{1,9},{2,66},{3,11},{4,68},{5,13},{6,70},{7,15},{8,72},{9,1... | collective-permute-start | bytes 442376 | tf_op jit(solution)/shard_map/ppermute | solution.py:32
  71.8 5.9 %collective-permute-start.13 = (bf16[2,144,128]{2,1,0:T(8,128)(2,1)S(1)}, bf16[2,144,128]{2,1,0:T(8,128)(2,1)S(1)}, u32[]{:S(2)}, u32[]{:S(2)}) collective-permute-start(bf16[2,144,128]{2,1,0:T(8,128)(2,1)S(1)} %get-tuple-element.72), channel_id=1, source_target_pairs={{0,16},{1,17},{2,18},{3,19},{4,20},{5,21},{6,22},{7,23},{8,24},{9,... | collective-permute-start | bytes 221192 | tf_op jit(solution)/shard_map/ppermute | solution.py:32
  74.6 7.0 %collective-permute-start.17 = (bf16[2,144,128]{2,1,0:T(8,128)(2,1)S(1)}, bf16[2,144,128]{2,1,0:T(8,128)(2,1)S(1)}, u32[]{:S(2)}, u32[]{:S(2)}) collective-permute-start(bf16[2,144,128]{2,1,0:T(8,128)(2,1)S(1)} %get-tuple-element.71), channel_id=1, source_target_pairs={{0,16},{1,17},{2,18},{3,19},{4,20},{5,21},{6,22},{7,23},{8,24},{9,... | collective-permute-start | bytes 221192 | tf_op jit(solution)/shard_map/ppermute | solution.py:32
  78.0 7.0 %collective-permute-start.14 = (bf16[16,2048]{1,0:T(8,128)(2,1)S(1)}, bf16[16,2048]{1,0:T(8,128)(2,1)S(1)}, u32[]{:S(2)}, u32[]{:S(2)}) collective-permute-start(bf16[16,2048]{1,0:T(8,128)(2,1)S(1)} %finish.2.x0), channel_id=1, source_target_pairs={{0,32},{1,5},{2,34},{3,7},{4,36},{5,9},{6,38},{7,11},{8,40},{9,13}... | collective-permute-start | bytes 196616 | tf_op jit(solution)/shard_map/ppermute | solution.py:32
  78.0 7.5 %collective-permute-start.15 = (bf16[16,2048]{1,0:T(8,128)(2,1)S(1)}, bf16[16,2048]{1,0:T(8,128)(2,1)S(1)}, u32[]{:S(2)}, u32[]{:S(2)}) collective-permute-start(bf16[16,2048]{1,0:T(8,128)(2,1)S(1)} %finish.2.x0), channel_id=1, source_target_pairs={{0,64},{1,9},{2,66},{3,11},{4,68},{5,13},{6,70},{7,15},{8,72},{9,1... | collective-permute-start | bytes 196616 | tf_op jit(solution)/shard_map/ppermute | solution.py:32
  81.4 4.3 %collective-permute-start.16 = (bf16[16,2048]{1,0:T(8,128)(2,1)S(1)}, bf16[16,2048]{1,0:T(8,128)(2,1)S(1)}, u32[]{:S(2)}, u32[]{:S(2)}) collective-permute-start(bf16[16,2048]{1,0:T(8,128)(2,1)S(1)} %finish.2.x0), channel_id=1, source_target_pairs={{0,96},{1,13},{2,98},{3,15},{4,100},{5,1},{6,102},{7,3},{8,104},{9... | collective-permute-start | bytes 196616 | tf_op jit(solution)/shard_map/ppermute | solution.py:32
  81.9 6.2 %collective-permute-start.18 = (bf16[16,2048]{1,0:T(8,128)(2,1)S(1)}, bf16[16,2048]{1,0:T(8,128)(2,1)S(1)}, u32[]{:S(2)}, u32[]{:S(2)}) collective-permute-start(bf16[16,2048]{1,0:T(8,128)(2,1)S(1)} %finish.3.x0), channel_id=1, source_target_pairs={{0,4},{1,33},{2,6},{3,35},{4,8},{5,37},{6,10},{7,39},{8,12},{9,41}... | collective-permute-start | bytes 196616 | tf_op jit(solution)/shard_map/ppermute | solution.py:32
  81.9 6.2 %collective-permute-start.19 = (bf16[16,2048]{1,0:T(8,128)(2,1)S(1)}, bf16[16,2048]{1,0:T(8,128)(2,1)S(1)}, u32[]{:S(2)}, u32[]{:S(2)}) collective-permute-start(bf16[16,2048]{1,0:T(8,128)(2,1)S(1)} %finish.3.x0), channel_id=1, source_target_pairs={{0,8},{1,65},{2,10},{3,67},{4,12},{5,69},{6,14},{7,71},{8,0},{9,73... | collective-permute-start | bytes 196616 | tf_op jit(solution)/shard_map/ppermute | solution.py:32
  84.9 4.3 %collective-permute-start.20 = (bf16[16,2048]{1,0:T(8,128)(2,1)S(1)}, bf16[16,2048]{1,0:T(8,128)(2,1)S(1)}, u32[]{:S(2)}, u32[]{:S(2)}) collective-permute-start(bf16[16,2048]{1,0:T(8,128)(2,1)S(1)} %finish.3.x0), channel_id=1, source_target_pairs={{0,12},{1,97},{2,14},{3,99},{4,0},{5,101},{6,2},{7,103},{8,4},{9,1... | collective-permute-start | bytes 196616 | tf_op jit(solution)/shard_map/ppermute | solution.py:32
  89.2 14.6 %collective-permute-start.21 = (bf16[64,2048]{1,0:T(8,128)(2,1)S(1)}, bf16[64,2048]{1,0:T(8,128)(2,1)S(1)}, u32[]{:S(2)}, u32[]{:S(2)}) collective-permute-start(bf16[64,2048]{1,0:T(8,128)(2,1)S(1)} %assemble.2.refs_0_), channel_id=1, source_target_pairs={{0,4},{1,33},{2,6},{3,35},{4,8},{5,37},{6,10},{7,39},{8,12},{9,41}... | collective-permute-start | bytes 786440 | tf_op jit(solution)/shard_map/ppermute | solution.py:32
  90.3 13.5 %collective-permute-start.22 = (bf16[64,2048]{1,0:T(8,128)(2,1)S(1)}, bf16[64,2048]{1,0:T(8,128)(2,1)S(1)}, u32[]{:S(2)}, u32[]{:S(2)}) collective-permute-start(bf16[64,2048]{1,0:T(8,128)(2,1)S(1)} %assemble.2.refs_0_), channel_id=1, source_target_pairs={{0,8},{1,65},{2,10},{3,67},{4,12},{5,69},{6,14},{7,71},{8,0},{9,73... | collective-permute-start | bytes 786440 | tf_op jit(solution)/shard_map/ppermute | solution.py:32
  93.1 10.7 %collective-permute-start.23 = (bf16[64,2048]{1,0:T(8,128)(2,1)S(1)}, bf16[64,2048]{1,0:T(8,128)(2,1)S(1)}, u32[]{:S(2)}, u32[]{:S(2)}) collective-permute-start(bf16[64,2048]{1,0:T(8,128)(2,1)S(1)} %assemble.2.refs_0_), channel_id=1, source_target_pairs={{0,12},{1,97},{2,14},{3,99},{4,0},{5,101},{6,2},{7,103},{8,4},{9,1... | collective-permute-start | bytes 786440 | tf_op jit(solution)/shard_map/ppermute | solution.py:32
  93.4 11.2 %collective-permute-start.24 = (bf16[64,2048]{1,0:T(8,128)(2,1)S(1)}, bf16[64,2048]{1,0:T(8,128)(2,1)S(1)}, u32[]{:S(2)}, u32[]{:S(2)}) collective-permute-start(bf16[64,2048]{1,0:T(8,128)(2,1)S(1)} %assemble.3.refs_0_), channel_id=1, source_target_pairs={{0,32},{1,5},{2,34},{3,7},{4,36},{5,9},{6,38},{7,11},{8,40},{9,13}... | collective-permute-start | bytes 786440 | tf_op jit(solution)/shard_map/ppermute | solution.py:32
  95.3 9.3 %collective-permute-start.25 = (bf16[64,2048]{1,0:T(8,128)(2,1)S(1)}, bf16[64,2048]{1,0:T(8,128)(2,1)S(1)}, u32[]{:S(2)}, u32[]{:S(2)}) collective-permute-start(bf16[64,2048]{1,0:T(8,128)(2,1)S(1)} %assemble.3.refs_0_), channel_id=1, source_target_pairs={{0,96},{1,13},{2,98},{3,15},{4,100},{5,1},{6,102},{7,3},{8,104},{9... | collective-permute-start | bytes 786440 | tf_op jit(solution)/shard_map/ppermute | solution.py:32
  103.8 7.9 %collective-permute-start.26 = (bf16[64,2048]{1,0:T(8,128)(2,1)S(1)}, bf16[64,2048]{1,0:T(8,128)(2,1)S(1)}, u32[]{:S(2)}, u32[]{:S(2)}) collective-permute-start(bf16[64,2048]{1,0:T(8,128)(2,1)S(1)} %assemble.3.refs_0_), channel_id=1, source_target_pairs={{0,64},{1,9},{2,66},{3,11},{4,68},{5,13},{6,70},{7,15},{8,72},{9,1... | collective-permute-start | bytes 786440 | tf_op jit(solution)/shard_map/ppermute | solution.py:32
  112.8 1.6 %collective-permute-start.27 = (f32[128,512]{1,0:T(8,128)S(1)}, f32[128,512]{1,0:T(8,128)S(1)}, u32[]{:S(2)}, u32[]{:S(2)}) collective-permute-start(f32[128,512]{1,0:T(8,128)S(1)} %slice.48), channel_id=1, source_target_pairs={{0,1},{1,0},{2,3},{3,2},{4,5},{5,4},{6,7},{7,6},{8,9},{9,8},{10,11... | collective-permute-start | bytes 786440 | tf_op jit(solution)/shard_map/ppermute | solution.py:32
  114.5 4.3 %collective-permute-start.28 = (bf16[64,512]{1,0:T(8,128)(2,1)S(1)}, bf16[64,512]{1,0:T(8,128)(2,1)S(1)}, u32[]{:S(2)}, u32[]{:S(2)}) collective-permute-start(bf16[64,512]{1,0:T(8,128)(2,1)S(1)} %slice.58), channel_id=1, source_target_pairs={{0,2},{1,3},{2,0},{3,1},{4,6},{5,7},{6,4},{7,5},{8,10},{9,11},{10,... | collective-permute-start | bytes 196616 | tf_op jit(solution)/shard_map/ppermute | solution.py:32
